TPU v7x, 32 devices: a whole 2x2x4 slice. The times are simulated.
32 devices in a mesh: fsdp: 2 (over y), ctx: 16 (over z, x, core).
Axes of the slice: x: 2, y: 2, z: 4, core: 2. Of those that a mesh axis runs over, the one named last changes fastest.
Arguments:
- block_input: bfloat16 [4096, 1088], P(('fsdp', 'ctx')), may hold values from -6 to 6
- cotangent: bfloat16 [4096, 1088], P(('fsdp', 'ctx')), may hold values from -6 to 6
- first_gain: bfloat16 [1088], P('fsdp'), may hold values from 0.5 to 1.5
- first_shift: bfloat16 [1088], P('fsdp'), may hold values from -3 to 3
- qkv_weight: bfloat16 [1088, 3264], P('fsdp'), may hold values from -0.1875 to 0.1875
- query_bias: bfloat16 [1088], P('fsdp'), may hold values from -3 to 3
- value_bias: bfloat16 [1088], P('fsdp'), may hold values from -3 to 3
- out_weight: bfloat16 [1088, 1088], P('fsdp'), may hold values from -1 to 1
- out_bias: bfloat16 [1088], P('fsdp'), may hold values from -3 to 3
- second_gain: bfloat16 [1088], P('fsdp'), may hold values from 0.5 to 1.5
- second_shift: bfloat16 [1088], P('fsdp'), may hold values from -3 to 3
- up_weight: bfloat16 [1088, 4352], P('fsdp'), may hold values from -0.1875 to 0.1875
- up_bias: bfloat16 [4352], P('fsdp'), may hold values from -3 to 3
- down_weight: bfloat16 [4352, 1088], P('fsdp'), may hold values from -0.09375 to 0.09375
- down_bias: bfloat16 [1088], P('fsdp'), may hold values from -3 to 3
Outputs:
- block_output: float32 [4096, 1088], P(('fsdp', 'ctx'))
- input_grad: float32 [4096, 1088], P(('fsdp', 'ctx'))
- grad_first_gain: float32 [1088], P('fsdp')
- grad_first_shift: float32 [1088], P('fsdp')
- grad_qkv: float32 [1088, 3264], P('fsdp')
- grad_query_bias: float32 [1088], P('fsdp')
- grad_value_bias: float32 [1088], P('fsdp')
- grad_out: float32 [1088, 1088], P('fsdp')
- grad_out_bias: float32 [1088], P('fsdp')
- grad_second_gain: float32 [1088], P('fsdp')
- grad_second_shift: float32 [1088], P('fsdp')
- grad_up: float32 [1088, 4352], P('fsdp')
- grad_up_bias: float32 [4352], P('fsdp')
- grad_down: float32 [4352, 1088], P('fsdp')
- grad_down_bias: float32 [1088], P('fsdp')
All inputs are finite; a program needn't handle non-finite values.
Results may differ from a plain program's by a relative error of at most 0.025.
Values may be sent and summed in bfloat16 or wider, within the bound.
A program may use at most 192 MiB of HBM per device.

v0:
```python
import jax
import jax.numpy as jnp
from jax import lax
from jax.sharding import PartitionSpec as P

HEADS = 17
HEAD_DIM = 64


EPS = 1e-05
NEG = -1e30


def shifted(block, axis, distance):
    devices = range(lax.axis_size(axis))
    route = [(i - distance, i) for i in devices if i - distance in devices]
    return lax.ppermute(block, axis, route)


def from_behind(value, axis, steps):
    count = lax.axis_size(axis)
    pairs = [(source, (source + steps) % count) for source in range(count)]
    return lax.ppermute(value, axis, pairs)


def normalize(rows, gain, shift):
    mean = jnp.mean(rows, axis=-1, keepdims=True)
    centered = rows - mean
    rstd = lax.rsqrt(jnp.mean(centered * centered, axis=-1, keepdims=True) + EPS)
    hat = centered * rstd
    return (hat * gain.astype(jnp.float32) + shift.astype(jnp.float32), hat, rstd)


def normalize_back(grad, hat, rstd, gain):
    scaled = grad * gain.astype(jnp.float32)
    return rstd * (
        scaled
        - jnp.mean(scaled, axis=-1, keepdims=True)
        - hat * jnp.mean(scaled * hat, axis=-1, keepdims=True)
    )


def gelu_tanh(value):
    return jax.nn.gelu(value, approximate=True)


def gelu_back(pre, grad):
    _, pull = jax.vjp(gelu_tanh, pre)
    return pull(grad)[0]


def contract(left, right, left_dim, right_dim):
    return lax.dot_general(
        left, right, (((left_dim,), (right_dim,)), ((), ())), preferred_element_type=jnp.float32
    )


def block_scores(query, key_block, query_pos, key_pos, scale):
    scores = (
        jnp.einsum("the,khe->htk", query, key_block, preferred_element_type=jnp.float32) * scale
    )
    allowed = key_pos[None, None, :] <= query_pos[None, :, None]
    return jnp.where(allowed, scores, NEG)


def on_device(
    block_input,
    cotangent,
    first_gain,
    first_shift,
    qkv_weight,
    query_bias,
    value_bias,
    out_weight,
    out_bias,
    second_gain,
    second_shift,
    up_weight,
    up_bias,
    down_weight,
    down_bias,
):
    (
        whole_gain_one,
        whole_shift_one,
        whole_qkv,
        whole_query_bias,
        whole_value_bias,
        whole_out,
        whole_out_bias,
        whole_gain_two,
        whole_shift_two,
        whole_up,
        whole_up_bias,
        whole_down,
        whole_down_bias,
    ) = (
        lax.all_gather(first_gain, "fsdp", axis=0, tiled=True),
        lax.all_gather(first_shift, "fsdp", axis=0, tiled=True),
        lax.all_gather(qkv_weight, "fsdp", axis=0, tiled=True),
        lax.all_gather(query_bias, "fsdp", axis=0, tiled=True),
        lax.all_gather(value_bias, "fsdp", axis=0, tiled=True),
        lax.all_gather(out_weight, "fsdp", axis=0, tiled=True),
        lax.all_gather(out_bias, "fsdp", axis=0, tiled=True),
        lax.all_gather(second_gain, "fsdp", axis=0, tiled=True),
        lax.all_gather(second_shift, "fsdp", axis=0, tiled=True),
        lax.all_gather(up_weight, "fsdp", axis=0, tiled=True),
        lax.all_gather(up_bias, "fsdp", axis=0, tiled=True),
        lax.all_gather(down_weight, "fsdp", axis=0, tiled=True),
        lax.all_gather(down_bias, "fsdp", axis=0, tiled=True),
    )
    position = lax.axis_index("ctx")
    blocks = lax.axis_size("ctx")
    count_rows = block_input.shape[0]
    width = HEADS * HEAD_DIM
    scale = HEAD_DIM ** (-0.5)
    offsets = jnp.arange(count_rows, dtype=jnp.int32)
    query_pos = position * count_rows + offsets
    shape_heads = (count_rows, HEADS, HEAD_DIM)
    rows = block_input.astype(jnp.float32)
    first_norm, first_hat, first_rstd = normalize(rows, whole_gain_one, whole_shift_one)
    first_act = first_norm.astype(jnp.bfloat16)
    qkv = jnp.dot(first_act, whole_qkv, preferred_element_type=jnp.float32)
    query = (
        (qkv[:, :width] + whole_query_bias.astype(jnp.float32))
        .astype(jnp.bfloat16)
        .reshape(shape_heads)
    )
    keys = qkv[:, width : 2 * width].astype(jnp.bfloat16).reshape(shape_heads)
    values = (
        (qkv[:, 2 * width :] + whole_value_bias.astype(jnp.float32))
        .astype(jnp.bfloat16)
        .reshape(shape_heads)
    )

    def forward_block(carry, key_block, value_block, source):
        run_max, run_sum, accum = carry
        scores = block_scores(query, key_block, query_pos, source * count_rows + offsets, scale)
        new_max = jnp.maximum(run_max, jnp.max(scores, axis=-1))
        factor = jnp.exp(run_max - new_max)
        weights = jnp.exp(scores - new_max[:, :, None])
        run_sum = run_sum * factor + jnp.sum(weights, axis=-1)
        accum = accum * factor[:, :, None] + jnp.einsum(
            "htk,khe->hte",
            weights.astype(jnp.bfloat16),
            value_block,
            preferred_element_type=jnp.float32,
        )
        return (new_max, run_sum, accum)

    def forward_visit(step, state):
        carry, key_block, value_block, stored = state
        source = (position - step) % blocks
        carry = lax.cond(
            source <= position,
            lambda inner: forward_block(inner, key_block, value_block, source),
            lambda inner: inner,
            carry,
        )
        return (carry, key_block, value_block, stored)

    def forward_step(step, state):
        carry, key_block, value_block, stored = forward_visit(step, state)
        key_block, value_block = shifted((key_block, value_block), "ctx", 1)
        return (carry, key_block, value_block, stored)

    stored_start = ()
    start = (
        jnp.full((HEADS, count_rows), NEG, jnp.float32),
        jnp.zeros((HEADS, count_rows), jnp.float32),
        jnp.zeros((HEADS, count_rows, HEAD_DIM), jnp.float32),
    )
    state = lax.fori_loop(0, blocks - 1, forward_step, (start, keys, values, stored_start))
    (run_max, run_sum, accum), _, _, stored_blocks = forward_visit(blocks - 1, state)
    attended = (accum / run_sum[:, :, None]).transpose(1, 0, 2).astype(jnp.bfloat16)
    lse = run_max + jnp.log(run_sum)
    joined = attended.reshape(count_rows, width)
    mid = (
        rows
        + jnp.dot(joined, whole_out, preferred_element_type=jnp.float32)
        + whole_out_bias.astype(jnp.float32)
    )
    second_norm, second_hat, second_rstd = normalize(mid, whole_gain_two, whole_shift_two)
    second_act = second_norm.astype(jnp.bfloat16)
    pre = jnp.dot(second_act, whole_up, preferred_element_type=jnp.float32) + whole_up_bias.astype(
        jnp.float32
    )
    act = gelu_tanh(pre).astype(jnp.bfloat16)
    block_output = (
        mid
        + jnp.dot(act, whole_down, preferred_element_type=jnp.float32)
        + whole_down_bias.astype(jnp.float32)
    )
    back_gain_one, back_qkv, back_out, back_gain_two, back_up, back_down = (
        whole_gain_one,
        whole_qkv,
        whole_out,
        whole_gain_two,
        whole_up,
        whole_down,
    )
    cot_float = cotangent.astype(jnp.float32)
    grad_down_bias = jnp.sum(cot_float, axis=0)
    grad_pre = gelu_back(pre, contract(cotangent, back_down, 1, 1))
    grad_pre_b = grad_pre.astype(jnp.bfloat16)
    grad_up_bias = jnp.sum(grad_pre, axis=0)
    grad_second = contract(grad_pre_b, back_up, 1, 1)
    grad_second_gain = jnp.sum(grad_second * second_hat, axis=0)
    grad_second_shift = jnp.sum(grad_second, axis=0)
    grad_mid = cot_float + normalize_back(grad_second, second_hat, second_rstd, back_gain_two)
    grad_mid_b = grad_mid.astype(jnp.bfloat16)
    grad_out_bias = jnp.sum(grad_mid, axis=0)
    grad_attended = contract(grad_mid_b, back_out, 1, 1).astype(jnp.bfloat16).reshape(shape_heads)
    delta_rows = jnp.sum(
        grad_attended.astype(jnp.float32) * attended.astype(jnp.float32), axis=-1
    ).T

    def backward_block(source, key_block, value_block, grads):
        grad_query, grad_keys, grad_values = grads
        scores = block_scores(query, key_block, query_pos, source * count_rows + offsets, scale)
        prob = jnp.exp(scores - lse[:, :, None])
        grad_values = grad_values + jnp.einsum(
            "htk,the->khe",
            prob.astype(jnp.bfloat16),
            grad_attended,
            preferred_element_type=jnp.float32,
        )
        grad_prob = jnp.einsum(
            "the,khe->htk", grad_attended, value_block, preferred_element_type=jnp.float32
        )
        grad_score = (prob * (grad_prob - delta_rows[:, :, None]) * scale).astype(jnp.bfloat16)
        grad_query = grad_query + jnp.einsum(
            "htk,khe->the", grad_score, key_block, preferred_element_type=jnp.float32
        )
        grad_keys = grad_keys + jnp.einsum(
            "htk,the->khe", grad_score, query, preferred_element_type=jnp.float32
        )
        return (grad_query, grad_keys, grad_values)

    zero_block = jnp.zeros(shape_heads, jnp.float32)

    def backward_step(step, state):
        grad_query, key_block, value_block, grad_keys, grad_values = state
        source = (position - step) % blocks
        grad_query, grad_keys, grad_values = lax.cond(
            source <= position,
            lambda inner: backward_block(source, key_block, value_block, inner),
            lambda inner: inner,
            (grad_query, grad_keys, grad_values),
        )
        key_block, value_block = shifted((key_block, value_block), "ctx", 1)
        grad_keys, grad_values = from_behind((grad_keys, grad_values), "ctx", 1)
        return (grad_query, key_block, value_block, grad_keys, grad_values)

    grad_query, _, _, grad_keys, grad_values = lax.fori_loop(
        0, blocks, backward_step, (zero_block, keys, values, zero_block, zero_block)
    )
    grad_query = grad_query.reshape(count_rows, width)
    grad_keys = grad_keys.reshape(count_rows, width)
    grad_values = grad_values.reshape(count_rows, width)
    grad_query_bias = jnp.sum(grad_query, axis=0)
    grad_value_bias = jnp.sum(grad_values, axis=0)
    grad_qkv_b = jnp.concatenate([grad_query, grad_keys, grad_values], axis=1).astype(jnp.bfloat16)
    grad_first = contract(grad_qkv_b, back_qkv, 1, 1)
    grad_first_gain = jnp.sum(grad_first * first_hat, axis=0)
    grad_first_shift = jnp.sum(grad_first, axis=0)
    input_grad = grad_mid + normalize_back(grad_first, first_hat, first_rstd, back_gain_one)
    left_first, left_joined, left_second, left_act = (
        lax.all_to_all(first_act, "fsdp", split_axis=1, concat_axis=0, tiled=True),
        lax.all_to_all(joined, "fsdp", split_axis=1, concat_axis=0, tiled=True),
        lax.all_to_all(second_act, "fsdp", split_axis=1, concat_axis=0, tiled=True),
        lax.all_to_all(act, "fsdp", split_axis=1, concat_axis=0, tiled=True),
    )
    right_qkv, right_mid, right_pre, right_cot = (
        lax.all_gather(grad_qkv_b, "fsdp", axis=0, tiled=True),
        lax.all_gather(grad_mid_b, "fsdp", axis=0, tiled=True),
        lax.all_gather(grad_pre_b, "fsdp", axis=0, tiled=True),
        lax.all_gather(cotangent, "fsdp", axis=0, tiled=True),
    )
    grad_qkv = contract(left_first, right_qkv, 0, 0)
    grad_out = contract(left_joined, right_mid, 0, 0)
    grad_up = contract(left_second, right_pre, 0, 0)
    grad_down = contract(left_act, right_cot, 0, 0)
    vectors = (
        lax.psum_scatter(grad_first_gain, "fsdp", scatter_dimension=0, tiled=True),
        lax.psum_scatter(grad_first_shift, "fsdp", scatter_dimension=0, tiled=True),
        lax.psum_scatter(grad_query_bias, "fsdp", scatter_dimension=0, tiled=True),
        lax.psum_scatter(grad_value_bias, "fsdp", scatter_dimension=0, tiled=True),
        lax.psum_scatter(grad_out_bias, "fsdp", scatter_dimension=0, tiled=True),
        lax.psum_scatter(grad_second_gain, "fsdp", scatter_dimension=0, tiled=True),
        lax.psum_scatter(grad_second_shift, "fsdp", scatter_dimension=0, tiled=True),
        lax.psum_scatter(grad_up_bias, "fsdp", scatter_dimension=0, tiled=True),
        lax.psum_scatter(grad_down_bias, "fsdp", scatter_dimension=0, tiled=True),
    )
    totals = lax.psum(
        (
            vectors[0],
            vectors[1],
            grad_qkv,
            vectors[2],
            vectors[3],
            grad_out,
            vectors[4],
            vectors[5],
            vectors[6],
            grad_up,
            vectors[7],
            grad_down,
            vectors[8],
        ),
        "ctx",
    )
    return (
        block_output,
        input_grad,
        totals[0],
        totals[1],
        totals[2],
        totals[3],
        totals[4],
        totals[5],
        totals[6],
        totals[7],
        totals[8],
        totals[9],
        totals[10],
        totals[11],
        totals[12],
    )


def solution(mesh):
    placed = (
        P(("fsdp", "ctx"), None),
        P(("fsdp", "ctx"), None),
        P("fsdp"),
        P("fsdp"),
        P("fsdp", None),
        P("fsdp"),
        P("fsdp"),
        P("fsdp", None),
        P("fsdp"),
        P("fsdp"),
        P("fsdp"),
        P("fsdp", None),
        P("fsdp"),
        P("fsdp", None),
        P("fsdp"),
    )
    return jax.shard_map(
        on_device,
        mesh=mesh,
        in_specs=placed,
        out_specs=(
            P(("fsdp", "ctx"), None),
            P(("fsdp", "ctx"), None),
            P("fsdp"),
            P("fsdp"),
            P("fsdp", None),
            P("fsdp"),
            P("fsdp"),
            P("fsdp", None),
            P("fsdp"),
            P("fsdp"),
            P("fsdp"),
            P("fsdp", None),
            P("fsdp"),
            P("fsdp", None),
            P("fsdp"),
        ),
        check_vma=False,
    )
```

profile of v0, /device:TPU:0, one launch (start us, length us, event | category | flops | bytes accessed | tf_op | source)
XLA Modules:
  0.0 1428.3 jit_solution(10872870336351741819)
XLA Ops:
  13.4 10.0 all-reduce.20
  29.5 73.9 %all-gather.8.cloned.1.call-done = bf16[1088,3264]{1,0:T(8,128)(2,1)} async-done(((bf16[544,3264]{1,0:T(8,128)(2,1)}), bf16[1088,3264]{1,0:T(8,128)(2,1)}) %all-gather.8.cloned.1.call-update) | async-done | bytes 7102480 | tf_op jit(solution)/shard_map/all_gather | solution.py:100
  103.5 6.2 fusion.71
  113.5 182.5 %while.48 = (s32[]{:T(128)}, f32[17,128]{1,0:T(8,128)S(1)}, f32[17,128]{1,0:T(8,128)S(1)}, f32[17,128,64]{1,2,0:T(8,128)S(1)}, bf16[128,17,64]{0,2,1:T(8,128)(2,...) while((s32[]{:T(128)}, f32[17,128]{1,0:T(8,128)S(1)}, ...), condition=%wide.region_7.8_spmd.clone, body=%wide.region_2.7_spmd.clone.sunk | while | flops 73552400 | bytes 8810480 | solution.py:173
  157.7 5.3 collective-permute-start
  170.1 5.6 collective-permute-start
  182.8 5.6 collective-permute-start
  195.4 5.6 collective-permute-start
  208.1 5.6 collective-permute-start
  220.7 5.6 collective-permute-start
  233.4 5.6 collective-permute-start
  246.0 5.6 collective-permute-start
  258.7 5.6 collective-permute-start
  271.4 5.6 collective-permute-start
  284.0 5.6 collective-permute-start
  300.4 6.8 fusion.72
  307.1 75.4 %all-gather.12.cloned.1.call-done = bf16[1088,4352]{1,0:T(8,128)(2,1)} async-done(((bf16[544,4352]{1,0:T(8,128)(2,1)}), bf16[1088,4352]{1,0:T(8,128)(2,1)}) %all-gather.12.cloned.1.call-update) | async-done | bytes 9469968 | tf_op jit(solution)/shard_map/all_gather | solution.py:107
  382.6 8.6 fusion.62
  391.1 6.8 multiply_reduce_fusion
  401.0 385.3 %while.49 = (s32[]{:T(128)}, f32[128,17,64]{0,2,1:T(8,128)S(1)}, bf16[128,17,64]{0,2,1:T(8,128)(2,1)}, bf16[128,17,64]{0,2,1:T(8,128)(2,1)}, f32[128,17,64]{0,2,...) while((s32[]{:T(128)}, f32[128,17,64]{0,2,1:T(8,128)S(1)}, ...), condition=%wide.region_20.21_spmd.clone, body=%wide.region_17.20_spmd.clone.sunk | while | flops 180920592 | bytes 20386928 | solution.py:255
  418.4 4.8 collective-permute-done.5
  444.8 7.9 collective-permute-start.4
  452.8 4.9 collective-permute-start.5
  460.4 5.2 collective-permute-start.3
  468.7 9.3 collective-permute-start.4
  480.6 5.8 collective-permute-start.2
  486.4 5.4 collective-permute-start.3
  494.9 6.1 collective-permute-start.4
  503.5 6.7 collective-permute-start.2
  510.2 7.7 collective-permute-start.3
  526.4 9.9 collective-permute-start.2
  536.4 5.4 collective-permute-start.3
  550.7 9.5 collective-permute-start.2
  560.2 5.4 collective-permute-start.3
  574.5 9.5 collective-permute-start.2
  584.0 5.4 collective-permute-start.3
  598.4 9.5 collective-permute-start.2
  607.8 5.4 collective-permute-start.3
  622.2 9.5 collective-permute-start.2
  631.7 5.4 collective-permute-start.3
  646.0 9.5 collective-permute-start.2
  655.5 5.4 collective-permute-start.3
  669.8 9.5 collective-permute-start.2
  679.3 5.4 collective-permute-start.3
  693.6 9.5 collective-permute-start.2
  703.1 5.4 collective-permute-start.3
  717.4 9.5 collective-permute-start.2
  726.9 5.4 collective-permute-start.3
  741.3 9.5 collective-permute-start.2
  750.7 5.4 collective-permute-start.3
  765.1 9.5 collective-permute-start.2
  774.6 5.4 collective-permute-start.3
  801.5 18.0 %all_gather.67 = bf16[256,1088]{0,1:T(8,128)(2,1)S(1)} all-gather(bf16[128,1088]{0,1:T(8,128)(2,1)S(1)} %copy-done.10), channel_id=1, replica_groups=mesh['fsdp'=2,'ctx'=16] {'fsdp'}, dimensions={0}, use_global_device_ids=true | all-gather | bytes 835584 | tf_op jit(solution)/shard_map/all_gather | solution.py:278
  819.5 13.8 all_gather.65
  839.8 5.2 fusion.73
  852.7 5.6 fusion.58
  858.3 35.2 %all-gather.18.cloned.1.call-done = bf16[256,4352]{1,0:T(8,128)(2,1)} async-done(((bf16[128,4352]{1,0:T(8,128)(2,1)}), bf16[256,4352]{1,0:T(8,128)(2,1)}) %all-gather.18.cloned.1.call-update) | async-done | bytes 2228240 | tf_op jit(solution)/shard_map/all_gather | solution.py:277
  893.5 6.8 fusion.52
  901.9 5.3 fusion.48
  907.2 8.2 all-reduce.19
  916.1 67.7 %all-reduce.17 = (f32[544]{0:T(1024)}, f32[544]{0:T(1024)}, f32[544]{0:T(1024)}, f32[544]{0:T(1024)}, f32[544]{0:T(1024)}, /*index=5*/f32[544]{0:T(1024)}, f32[544]{0:T(1024)}, f32[2176]{0:T(1024)}, f32[544]{0:T(1024)}) all-reduce(f32[544]{0:T(1024)S(1)} %dynamic-slice.9, ...), channel_id=1, replica_groups=mesh['fsdp'=2,'ctx'=16] {'ctx'}, use_global_device_ids=true, to_apply=%region_25.26 | all-reduce | flops 6528 | bytes 52224 | tf_op jit(solution)/shard_map/psum | solution.py:295
  984.8 7.2 fusion.29
  992.0 409.5 %all-reduce.23.cloned.1.call-done = (f32[544,3264]{1,0:T(8,128)}, f32[544,1088]{1,0:T(8,128)}, f32[544,4352]{1,0:T(8,128)}, f32[2176,1088]{0,1:T(8,128)}) async-done(((f32[544,3264]{1,0:T(8,128)}, f32[544,1088]{1,0:T(8,128)}, f32[544,4352]{1,0:T(8,128)}, f32[2176,1088]{0,1:T(8,128)}), (f32[544,3264]{1,0:T(8,128)}, f32[544,1088]{1,0:T(8,128)}, f32[544,4352]{1,0:T(8,128)}, ...) | async-done | bytes 28409872 | tf_op jit(solution)/shard_map/psum | solution.py:295
  1401.5 7.4 copy.130
  (490 shorter events, 347.6 us)
Async XLA Ops:
  7.2 96.3 %all-gather.8.cloned.1.call-start = ((), (), s32[]{:S(2)}) async-start(), calls=%async_computation.4 | async-start | bytes 10862592 | tf_op jit(solution)/shard_map/all_gather | solution.py:100
  7.9 288.8 %all-gather.10.cloned.1.call-start = ((), (), s32[]{:S(2)}) async-start(), calls=%async_computation.5 | async-start | bytes 3760128 | tf_op jit(solution)/shard_map/all_gather | solution.py:103
  8.7 291.7 %all-gather.14.cloned.1.call-start = ((), (), s32[]{:S(2)}) async-start(), calls=%async_computation.7 | async-start | bytes 14204928 | tf_op jit(solution)/shard_map/all_gather | solution.py:109
  9.5 373.0 %all-gather.12.cloned.1.call-start = ((), (), s32[]{:S(2)}) async-start(), calls=%async_computation.6 | async-start | bytes 14204928 | tf_op jit(solution)/shard_map/all_gather | solution.py:107
  10.1 842.6 %all-gather.16.cloned.1.call-start = ((), (), s32[]{:S(2)}) async-start(), calls=%async_computation.8 | async-start | bytes 2506752 | tf_op jit(solution)/shard_map/all_gather | solution.py:275
  170.1 10.6 collective-permute-start
  182.8 10.6 collective-permute-start
  195.4 10.6 collective-permute-start
  220.7 10.6 collective-permute-start
  246.0 10.6 collective-permute-start
  258.7 10.6 collective-permute-start
  271.4 10.6 collective-permute-start
  405.5 11.8 collective-permute-start.4
  405.6 17.6 %collective-permute-start.5 = (f32[128,17,64]{0,2,1:T(8,128)S(1)}, f32[128,17,64]{0,2,1:T(8,128)S(1)}, u32[]{:S(2)}, u32[]{:S(2)}) collective-permute-start(f32[128,17,64]{0,2,1:T(8,128)S(1)} %get-tuple-element.1077), channel_id=1, source_target_pairs={{0,1},{1,2},{2,3},{3,4},{4,5},{5,6},{6,7},{7,8},{8,9},{9,10},{10,1... | collective-permute-start | bytes 1671176 | tf_op jit(solution)/shard_map/while/body/eval_jaxpr/ppermute | solution.py:23
  407.1 16.1 %collective-permute-start.2 = (bf16[128,17,64]{0,2,1:T(8,128)(2,1)S(1)}, bf16[128,17,64]{0,2,1:T(8,128)(2,1)}, u32[]{:S(2)}, u32[]{:S(2)}) collective-permute-start(bf16[128,17,64]{0,2,1:T(8,128)(2,1)S(1)} %copy.116), channel_id=1, source_target_pairs={{0,1},{1,2},{2,3},{3,4},{4,5},{5,6},{6,7},{7,8},{8,9},{9,10},{10,1... | collective-permute-start | bytes 835592 | tf_op jit(solution)/shard_map/while/body/eval_jaxpr/ppermute | solution.py:17
  409.8 13.4 collective-permute-start.3
  425.2 14.2 collective-permute-start.4
  429.8 13.0 collective-permute-start.5
  444.8 20.8 %collective-permute-start.4 = (f32[128,17,64]{0,2,1:T(8,128)S(1)}, f32[128,17,64]{0,2,1:T(8,128)}, u32[]{:S(2)}, u32[]{:S(2)}) collective-permute-start(f32[128,17,64]{0,2,1:T(8,128)S(1)} %get-tuple-element.1076), channel_id=1, source_target_pairs={{0,1},{1,2},{2,3},{3,4},{4,5},{5,6},{6,7},{7,8},{8,9},{9,10},{10,1... | collective-permute-start | bytes 1671176 | tf_op jit(solution)/shard_map/while/body/eval_jaxpr/ppermute | solution.py:23
  452.8 13.9 collective-permute-start.5
  468.7 23.1 %collective-permute-start.4 = (f32[128,17,64]{0,2,1:T(8,128)S(1)}, f32[128,17,64]{0,2,1:T(8,128)}, u32[]{:S(2)}, u32[]{:S(2)}) collective-permute-start(f32[128,17,64]{0,2,1:T(8,128)S(1)} %get-tuple-element.1076), channel_id=1, source_target_pairs={{0,1},{1,2},{2,3},{3,4},{4,5},{5,6},{6,7},{7,8},{8,9},{9,10},{10,1... | collective-permute-start | bytes 1671176 | tf_op jit(solution)/shard_map/while/body/eval_jaxpr/ppermute | solution.py:23
  478.0 14.8 %collective-permute-start.5 = (f32[128,17,64]{0,2,1:T(8,128)S(1)}, f32[128,17,64]{0,2,1:T(8,128)S(1)}, u32[]{:S(2)}, u32[]{:S(2)}) collective-permute-start(f32[128,17,64]{0,2,1:T(8,128)S(1)} %get-tuple-element.1077), channel_id=1, source_target_pairs={{0,1},{1,2},{2,3},{3,4},{4,5},{5,6},{6,7},{7,8},{8,9},{9,10},{10,1... | collective-permute-start | bytes 1671176 | tf_op jit(solution)/shard_map/while/body/eval_jaxpr/ppermute | solution.py:23
  480.6 12.3 collective-permute-start.2
  494.9 23.1 %collective-permute-start.4 = (f32[128,17,64]{0,2,1:T(8,128)S(1)}, f32[128,17,64]{0,2,1:T(8,128)}, u32[]{:S(2)}, u32[]{:S(2)}) collective-permute-start(f32[128,17,64]{0,2,1:T(8,128)S(1)} %get-tuple-element.1076), channel_id=1, source_target_pairs={{0,1},{1,2},{2,3},{3,4},{4,5},{5,6},{6,7},{7,8},{8,9},{9,10},{10,1... | collective-permute-start | bytes 1671176 | tf_op jit(solution)/shard_map/while/body/eval_jaxpr/ppermute | solution.py:23
  500.9 18.1 %collective-permute-start.5 = (f32[128,17,64]{0,2,1:T(8,128)S(1)}, f32[128,17,64]{0,2,1:T(8,128)S(1)}, u32[]{:S(2)}, u32[]{:S(2)}) collective-permute-start(f32[128,17,64]{0,2,1:T(8,128)S(1)} %get-tuple-element.1077), channel_id=1, source_target_pairs={{0,1},{1,2},{2,3},{3,4},{4,5},{5,6},{6,7},{7,8},{8,9},{9,10},{10,1... | collective-permute-start | bytes 1671176 | tf_op jit(solution)/shard_map/while/body/eval_jaxpr/ppermute | solution.py:23
  503.5 15.5 %collective-permute-start.2 = (bf16[128,17,64]{0,2,1:T(8,128)(2,1)S(1)}, bf16[128,17,64]{0,2,1:T(8,128)(2,1)}, u32[]{:S(2)}, u32[]{:S(2)}) collective-permute-start(bf16[128,17,64]{0,2,1:T(8,128)(2,1)S(1)} %copy.116), channel_id=1, source_target_pairs={{0,1},{1,2},{2,3},{3,4},{4,5},{5,6},{6,7},{7,8},{8,9},{9,10},{10,1... | collective-permute-start | bytes 835592 | tf_op jit(solution)/shard_map/while/body/eval_jaxpr/ppermute | solution.py:17
  521.0 20.7 %collective-permute-start.4 = (f32[128,17,64]{0,2,1:T(8,128)S(1)}, f32[128,17,64]{0,2,1:T(8,128)}, u32[]{:S(2)}, u32[]{:S(2)}) collective-permute-start(f32[128,17,64]{0,2,1:T(8,128)S(1)} %get-tuple-element.1076), channel_id=1, source_target_pairs={{0,1},{1,2},{2,3},{3,4},{4,5},{5,6},{6,7},{7,8},{8,9},{9,10},{10,1... | collective-permute-start | bytes 1671176 | tf_op jit(solution)/shard_map/while/body/eval_jaxpr/ppermute | solution.py:23
  523.9 19.0 %collective-permute-start.5 = (f32[128,17,64]{0,2,1:T(8,128)S(1)}, f32[128,17,64]{0,2,1:T(8,128)S(1)}, u32[]{:S(2)}, u32[]{:S(2)}) collective-permute-start(f32[128,17,64]{0,2,1:T(8,128)S(1)} %get-tuple-element.1077), channel_id=1, source_target_pairs={{0,1},{1,2},{2,3},{3,4},{4,5},{5,6},{6,7},{7,8},{8,9},{9,10},{10,1... | collective-permute-start | bytes 1671176 | tf_op jit(solution)/shard_map/while/body/eval_jaxpr/ppermute | solution.py:23
  526.4 16.4 %collective-permute-start.2 = (bf16[128,17,64]{0,2,1:T(8,128)(2,1)S(1)}, bf16[128,17,64]{0,2,1:T(8,128)(2,1)}, u32[]{:S(2)}, u32[]{:S(2)}) collective-permute-start(bf16[128,17,64]{0,2,1:T(8,128)(2,1)S(1)} %copy.116), channel_id=1, source_target_pairs={{0,1},{1,2},{2,3},{3,4},{4,5},{5,6},{6,7},{7,8},{8,9},{9,10},{10,1... | collective-permute-start | bytes 835592 | tf_op jit(solution)/shard_map/while/body/eval_jaxpr/ppermute | solution.py:17
  544.9 20.7 %collective-permute-start.4 = (f32[128,17,64]{0,2,1:T(8,128)S(1)}, f32[128,17,64]{0,2,1:T(8,128)}, u32[]{:S(2)}, u32[]{:S(2)}) collective-permute-start(f32[128,17,64]{0,2,1:T(8,128)S(1)} %get-tuple-element.1076), channel_id=1, source_target_pairs={{0,1},{1,2},{2,3},{3,4},{4,5},{5,6},{6,7},{7,8},{8,9},{9,10},{10,1... | collective-permute-start | bytes 1671176 | tf_op jit(solution)/shard_map/while/body/eval_jaxpr/ppermute | solution.py:23
  548.1 18.5 %collective-permute-start.5 = (f32[128,17,64]{0,2,1:T(8,128)S(1)}, f32[128,17,64]{0,2,1:T(8,128)S(1)}, u32[]{:S(2)}, u32[]{:S(2)}) collective-permute-start(f32[128,17,64]{0,2,1:T(8,128)S(1)} %get-tuple-element.1077), channel_id=1, source_target_pairs={{0,1},{1,2},{2,3},{3,4},{4,5},{5,6},{6,7},{7,8},{8,9},{9,10},{10,1... | collective-permute-start | bytes 1671176 | tf_op jit(solution)/shard_map/while/body/eval_jaxpr/ppermute | solution.py:23
  550.7 16.0 %collective-permute-start.2 = (bf16[128,17,64]{0,2,1:T(8,128)(2,1)S(1)}, bf16[128,17,64]{0,2,1:T(8,128)(2,1)}, u32[]{:S(2)}, u32[]{:S(2)}) collective-permute-start(bf16[128,17,64]{0,2,1:T(8,128)(2,1)S(1)} %copy.116), channel_id=1, source_target_pairs={{0,1},{1,2},{2,3},{3,4},{4,5},{5,6},{6,7},{7,8},{8,9},{9,10},{10,1... | collective-permute-start | bytes 835592 | tf_op jit(solution)/shard_map/while/body/eval_jaxpr/ppermute | solution.py:17
  568.7 20.7 %collective-permute-start.4 = (f32[128,17,64]{0,2,1:T(8,128)S(1)}, f32[128,17,64]{0,2,1:T(8,128)}, u32[]{:S(2)}, u32[]{:S(2)}) collective-permute-start(f32[128,17,64]{0,2,1:T(8,128)S(1)} %get-tuple-element.1076), channel_id=1, source_target_pairs={{0,1},{1,2},{2,3},{3,4},{4,5},{5,6},{6,7},{7,8},{8,9},{9,10},{10,1... | collective-permute-start | bytes 1671176 | tf_op jit(solution)/shard_map/while/body/eval_jaxpr/ppermute | solution.py:23
  571.9 18.5 %collective-permute-start.5 = (f32[128,17,64]{0,2,1:T(8,128)S(1)}, f32[128,17,64]{0,2,1:T(8,128)S(1)}, u32[]{:S(2)}, u32[]{:S(2)}) collective-permute-start(f32[128,17,64]{0,2,1:T(8,128)S(1)} %get-tuple-element.1077), channel_id=1, source_target_pairs={{0,1},{1,2},{2,3},{3,4},{4,5},{5,6},{6,7},{7,8},{8,9},{9,10},{10,1... | collective-permute-start | bytes 1671176 | tf_op jit(solution)/shard_map/while/body/eval_jaxpr/ppermute | solution.py:23
  574.5 16.0 %collective-permute-start.2 = (bf16[128,17,64]{0,2,1:T(8,128)(2,1)S(1)}, bf16[128,17,64]{0,2,1:T(8,128)(2,1)}, u32[]{:S(2)}, u32[]{:S(2)}) collective-permute-start(bf16[128,17,64]{0,2,1:T(8,128)(2,1)S(1)} %copy.116), channel_id=1, source_target_pairs={{0,1},{1,2},{2,3},{3,4},{4,5},{5,6},{6,7},{7,8},{8,9},{9,10},{10,1... | collective-permute-start | bytes 835592 | tf_op jit(solution)/shard_map/while/body/eval_jaxpr/ppermute | solution.py:17
  592.5 20.7 %collective-permute-start.4 = (f32[128,17,64]{0,2,1:T(8,128)S(1)}, f32[128,17,64]{0,2,1:T(8,128)}, u32[]{:S(2)}, u32[]{:S(2)}) collective-permute-start(f32[128,17,64]{0,2,1:T(8,128)S(1)} %get-tuple-element.1076), channel_id=1, source_target_pairs={{0,1},{1,2},{2,3},{3,4},{4,5},{5,6},{6,7},{7,8},{8,9},{9,10},{10,1... | collective-permute-start | bytes 1671176 | tf_op jit(solution)/shard_map/while/body/eval_jaxpr/ppermute | solution.py:23
  595.8 18.5 %collective-permute-start.5 = (f32[128,17,64]{0,2,1:T(8,128)S(1)}, f32[128,17,64]{0,2,1:T(8,128)S(1)}, u32[]{:S(2)}, u32[]{:S(2)}) collective-permute-start(f32[128,17,64]{0,2,1:T(8,128)S(1)} %get-tuple-element.1077), channel_id=1, source_target_pairs={{0,1},{1,2},{2,3},{3,4},{4,5},{5,6},{6,7},{7,8},{8,9},{9,10},{10,1... | collective-permute-start | bytes 1671176 | tf_op jit(solution)/shard_map/while/body/eval_jaxpr/ppermute | solution.py:23
  598.4 16.0 %collective-permute-start.2 = (bf16[128,17,64]{0,2,1:T(8,128)(2,1)S(1)}, bf16[128,17,64]{0,2,1:T(8,128)(2,1)}, u32[]{:S(2)}, u32[]{:S(2)}) collective-permute-start(bf16[128,17,64]{0,2,1:T(8,128)(2,1)S(1)} %copy.116), channel_id=1, source_target_pairs={{0,1},{1,2},{2,3},{3,4},{4,5},{5,6},{6,7},{7,8},{8,9},{9,10},{10,1... | collective-permute-start | bytes 835592 | tf_op jit(solution)/shard_map/while/body/eval_jaxpr/ppermute | solution.py:17
  616.3 20.7 %collective-permute-start.4 = (f32[128,17,64]{0,2,1:T(8,128)S(1)}, f32[128,17,64]{0,2,1:T(8,128)}, u32[]{:S(2)}, u32[]{:S(2)}) collective-permute-start(f32[128,17,64]{0,2,1:T(8,128)S(1)} %get-tuple-element.1076), channel_id=1, source_target_pairs={{0,1},{1,2},{2,3},{3,4},{4,5},{5,6},{6,7},{7,8},{8,9},{9,10},{10,1... | collective-permute-start | bytes 1671176 | tf_op jit(solution)/shard_map/while/body/eval_jaxpr/ppermute | solution.py:23
  619.6 18.5 %collective-permute-start.5 = (f32[128,17,64]{0,2,1:T(8,128)S(1)}, f32[128,17,64]{0,2,1:T(8,128)S(1)}, u32[]{:S(2)}, u32[]{:S(2)}) collective-permute-start(f32[128,17,64]{0,2,1:T(8,128)S(1)} %get-tuple-element.1077), channel_id=1, source_target_pairs={{0,1},{1,2},{2,3},{3,4},{4,5},{5,6},{6,7},{7,8},{8,9},{9,10},{10,1... | collective-permute-start | bytes 1671176 | tf_op jit(solution)/shard_map/while/body/eval_jaxpr/ppermute | solution.py:23
  622.2 16.0 %collective-permute-start.2 = (bf16[128,17,64]{0,2,1:T(8,128)(2,1)S(1)}, bf16[128,17,64]{0,2,1:T(8,128)(2,1)}, u32[]{:S(2)}, u32[]{:S(2)}) collective-permute-start(bf16[128,17,64]{0,2,1:T(8,128)(2,1)S(1)} %copy.116), channel_id=1, source_target_pairs={{0,1},{1,2},{2,3},{3,4},{4,5},{5,6},{6,7},{7,8},{8,9},{9,10},{10,1... | collective-permute-start | bytes 835592 | tf_op jit(solution)/shard_map/while/body/eval_jaxpr/ppermute | solution.py:17
  640.1 20.7 %collective-permute-start.4 = (f32[128,17,64]{0,2,1:T(8,128)S(1)}, f32[128,17,64]{0,2,1:T(8,128)}, u32[]{:S(2)}, u32[]{:S(2)}) collective-permute-start(f32[128,17,64]{0,2,1:T(8,128)S(1)} %get-tuple-element.1076), channel_id=1, source_target_pairs={{0,1},{1,2},{2,3},{3,4},{4,5},{5,6},{6,7},{7,8},{8,9},{9,10},{10,1... | collective-permute-start | bytes 1671176 | tf_op jit(solution)/shard_map/while/body/eval_jaxpr/ppermute | solution.py:23
  643.4 18.5 %collective-permute-start.5 = (f32[128,17,64]{0,2,1:T(8,128)S(1)}, f32[128,17,64]{0,2,1:T(8,128)S(1)}, u32[]{:S(2)}, u32[]{:S(2)}) collective-permute-start(f32[128,17,64]{0,2,1:T(8,128)S(1)} %get-tuple-element.1077), channel_id=1, source_target_pairs={{0,1},{1,2},{2,3},{3,4},{4,5},{5,6},{6,7},{7,8},{8,9},{9,10},{10,1... | collective-permute-start | bytes 1671176 | tf_op jit(solution)/shard_map/while/body/eval_jaxpr/ppermute | solution.py:23
  646.0 16.0 %collective-permute-start.2 = (bf16[128,17,64]{0,2,1:T(8,128)(2,1)S(1)}, bf16[128,17,64]{0,2,1:T(8,128)(2,1)}, u32[]{:S(2)}, u32[]{:S(2)}) collective-permute-start(bf16[128,17,64]{0,2,1:T(8,128)(2,1)S(1)} %copy.116), channel_id=1, source_target_pairs={{0,1},{1,2},{2,3},{3,4},{4,5},{5,6},{6,7},{7,8},{8,9},{9,10},{10,1... | collective-permute-start | bytes 835592 | tf_op jit(solution)/shard_map/while/body/eval_jaxpr/ppermute | solution.py:17
  663.9 20.7 %collective-permute-start.4 = (f32[128,17,64]{0,2,1:T(8,128)S(1)}, f32[128,17,64]{0,2,1:T(8,128)}, u32[]{:S(2)}, u32[]{:S(2)}) collective-permute-start(f32[128,17,64]{0,2,1:T(8,128)S(1)} %get-tuple-element.1076), channel_id=1, source_target_pairs={{0,1},{1,2},{2,3},{3,4},{4,5},{5,6},{6,7},{7,8},{8,9},{9,10},{10,1... | collective-permute-start | bytes 1671176 | tf_op jit(solution)/shard_map/while/body/eval_jaxpr/ppermute | solution.py:23
  667.2 18.5 %collective-permute-start.5 = (f32[128,17,64]{0,2,1:T(8,128)S(1)}, f32[128,17,64]{0,2,1:T(8,128)S(1)}, u32[]{:S(2)}, u32[]{:S(2)}) collective-permute-start(f32[128,17,64]{0,2,1:T(8,128)S(1)} %get-tuple-element.1077), channel_id=1, source_target_pairs={{0,1},{1,2},{2,3},{3,4},{4,5},{5,6},{6,7},{7,8},{8,9},{9,10},{10,1... | collective-permute-start | bytes 1671176 | tf_op jit(solution)/shard_map/while/body/eval_jaxpr/ppermute | solution.py:23
  669.8 16.0 %collective-permute-start.2 = (bf16[128,17,64]{0,2,1:T(8,128)(2,1)S(1)}, bf16[128,17,64]{0,2,1:T(8,128)(2,1)}, u32[]{:S(2)}, u32[]{:S(2)}) collective-permute-start(bf16[128,17,64]{0,2,1:T(8,128)(2,1)S(1)} %copy.116), channel_id=1, source_target_pairs={{0,1},{1,2},{2,3},{3,4},{4,5},{5,6},{6,7},{7,8},{8,9},{9,10},{10,1... | collective-permute-start | bytes 835592 | tf_op jit(solution)/shard_map/while/body/eval_jaxpr/ppermute | solution.py:17
  687.8 20.7 %collective-permute-start.4 = (f32[128,17,64]{0,2,1:T(8,128)S(1)}, f32[128,17,64]{0,2,1:T(8,128)}, u32[]{:S(2)}, u32[]{:S(2)}) collective-permute-start(f32[128,17,64]{0,2,1:T(8,128)S(1)} %get-tuple-element.1076), channel_id=1, source_target_pairs={{0,1},{1,2},{2,3},{3,4},{4,5},{5,6},{6,7},{7,8},{8,9},{9,10},{10,1... | collective-permute-start | bytes 1671176 | tf_op jit(solution)/shard_map/while/body/eval_jaxpr/ppermute | solution.py:23
  691.0 19.5 %collective-permute-start.5 = (f32[128,17,64]{0,2,1:T(8,128)S(1)}, f32[128,17,64]{0,2,1:T(8,128)S(1)}, u32[]{:S(2)}, u32[]{:S(2)}) collective-permute-start(f32[128,17,64]{0,2,1:T(8,128)S(1)} %get-tuple-element.1077), channel_id=1, source_target_pairs={{0,1},{1,2},{2,3},{3,4},{4,5},{5,6},{6,7},{7,8},{8,9},{9,10},{10,1... | collective-permute-start | bytes 1671176 | tf_op jit(solution)/shard_map/while/body/eval_jaxpr/ppermute | solution.py:23
  693.6 16.9 %collective-permute-start.2 = (bf16[128,17,64]{0,2,1:T(8,128)(2,1)S(1)}, bf16[128,17,64]{0,2,1:T(8,128)(2,1)}, u32[]{:S(2)}, u32[]{:S(2)}) collective-permute-start(bf16[128,17,64]{0,2,1:T(8,128)(2,1)S(1)} %copy.116), channel_id=1, source_target_pairs={{0,1},{1,2},{2,3},{3,4},{4,5},{5,6},{6,7},{7,8},{8,9},{9,10},{10,1... | collective-permute-start | bytes 835592 | tf_op jit(solution)/shard_map/while/body/eval_jaxpr/ppermute | solution.py:17
  712.5 19.8 %collective-permute-start.4 = (f32[128,17,64]{0,2,1:T(8,128)S(1)}, f32[128,17,64]{0,2,1:T(8,128)}, u32[]{:S(2)}, u32[]{:S(2)}) collective-permute-start(f32[128,17,64]{0,2,1:T(8,128)S(1)} %get-tuple-element.1076), channel_id=1, source_target_pairs={{0,1},{1,2},{2,3},{3,4},{4,5},{5,6},{6,7},{7,8},{8,9},{9,10},{10,1... | collective-permute-start | bytes 1671176 | tf_op jit(solution)/shard_map/while/body/eval_jaxpr/ppermute | solution.py:23
  714.9 20.9 %collective-permute-start.5 = (f32[128,17,64]{0,2,1:T(8,128)S(1)}, f32[128,17,64]{0,2,1:T(8,128)S(1)}, u32[]{:S(2)}, u32[]{:S(2)}) collective-permute-start(f32[128,17,64]{0,2,1:T(8,128)S(1)} %get-tuple-element.1077), channel_id=1, source_target_pairs={{0,1},{1,2},{2,3},{3,4},{4,5},{5,6},{6,7},{7,8},{8,9},{9,10},{10,1... | collective-permute-start | bytes 1671176 | tf_op jit(solution)/shard_map/while/body/eval_jaxpr/ppermute | solution.py:23
  717.4 18.4 %collective-permute-start.2 = (bf16[128,17,64]{0,2,1:T(8,128)(2,1)S(1)}, bf16[128,17,64]{0,2,1:T(8,128)(2,1)}, u32[]{:S(2)}, u32[]{:S(2)}) collective-permute-start(bf16[128,17,64]{0,2,1:T(8,128)(2,1)S(1)} %copy.116), channel_id=1, source_target_pairs={{0,1},{1,2},{2,3},{3,4},{4,5},{5,6},{6,7},{7,8},{8,9},{9,10},{10,1... | collective-permute-start | bytes 835592 | tf_op jit(solution)/shard_map/while/body/eval_jaxpr/ppermute | solution.py:17
  737.8 18.4 %collective-permute-start.4 = (f32[128,17,64]{0,2,1:T(8,128)S(1)}, f32[128,17,64]{0,2,1:T(8,128)}, u32[]{:S(2)}, u32[]{:S(2)}) collective-permute-start(f32[128,17,64]{0,2,1:T(8,128)S(1)} %get-tuple-element.1076), channel_id=1, source_target_pairs={{0,1},{1,2},{2,3},{3,4},{4,5},{5,6},{6,7},{7,8},{8,9},{9,10},{10,1... | collective-permute-start | bytes 1671176 | tf_op jit(solution)/shard_map/while/body/eval_jaxpr/ppermute | solution.py:23
  738.7 22.4 %collective-permute-start.5 = (f32[128,17,64]{0,2,1:T(8,128)S(1)}, f32[128,17,64]{0,2,1:T(8,128)S(1)}, u32[]{:S(2)}, u32[]{:S(2)}) collective-permute-start(f32[128,17,64]{0,2,1:T(8,128)S(1)} %get-tuple-element.1077), channel_id=1, source_target_pairs={{0,1},{1,2},{2,3},{3,4},{4,5},{5,6},{6,7},{7,8},{8,9},{9,10},{10,1... | collective-permute-start | bytes 1671176 | tf_op jit(solution)/shard_map/while/body/eval_jaxpr/ppermute | solution.py:23
  741.3 19.8 %collective-permute-start.2 = (bf16[128,17,64]{0,2,1:T(8,128)(2,1)S(1)}, bf16[128,17,64]{0,2,1:T(8,128)(2,1)}, u32[]{:S(2)}, u32[]{:S(2)}) collective-permute-start(bf16[128,17,64]{0,2,1:T(8,128)(2,1)S(1)} %copy.116), channel_id=1, source_target_pairs={{0,1},{1,2},{2,3},{3,4},{4,5},{5,6},{6,7},{7,8},{8,9},{9,10},{10,1... | collective-permute-start | bytes 835592 | tf_op jit(solution)/shard_map/while/body/eval_jaxpr/ppermute | solution.py:17
  763.1 17.4 %collective-permute-start.4 = (f32[128,17,64]{0,2,1:T(8,128)S(1)}, f32[128,17,64]{0,2,1:T(8,128)}, u32[]{:S(2)}, u32[]{:S(2)}) collective-permute-start(f32[128,17,64]{0,2,1:T(8,128)S(1)} %get-tuple-element.1076), channel_id=1, source_target_pairs={{0,1},{1,2},{2,3},{3,4},{4,5},{5,6},{6,7},{7,8},{8,9},{9,10},{10,1... | collective-permute-start | bytes 1671176 | tf_op jit(solution)/shard_map/while/body/eval_jaxpr/ppermute | solution.py:23
  763.1 23.3 %collective-permute-start.5 = (f32[128,17,64]{0,2,1:T(8,128)S(1)}, f32[128,17,64]{0,2,1:T(8,128)S(1)}, u32[]{:S(2)}, u32[]{:S(2)}) collective-permute-start(f32[128,17,64]{0,2,1:T(8,128)S(1)} %get-tuple-element.1077), channel_id=1, source_target_pairs={{0,1},{1,2},{2,3},{3,4},{4,5},{5,6},{6,7},{7,8},{8,9},{9,10},{10,1... | collective-permute-start | bytes 1671176 | tf_op jit(solution)/shard_map/while/body/eval_jaxpr/ppermute | solution.py:23
  765.1 21.3 %collective-permute-start.2 = (bf16[128,17,64]{0,2,1:T(8,128)(2,1)S(1)}, bf16[128,17,64]{0,2,1:T(8,128)(2,1)}, u32[]{:S(2)}, u32[]{:S(2)}) collective-permute-start(bf16[128,17,64]{0,2,1:T(8,128)(2,1)S(1)} %copy.116), channel_id=1, source_target_pairs={{0,1},{1,2},{2,3},{3,4},{4,5},{5,6},{6,7},{7,8},{8,9},{9,10},{10,1... | collective-permute-start | bytes 835592 | tf_op jit(solution)/shard_map/while/body/eval_jaxpr/ppermute | solution.py:17
  774.6 11.8 collective-permute-start.3
  787.9 105.6 %all-gather.18.cloned.1.call-start = ((), (), s32[]{:S(2)}) async-start(), calls=%async_computation.9 | async-start | bytes 3342336 | tf_op jit(solution)/shard_map/all_gather | solution.py:277
  797.9 38.5 %all-to-all-start.3 = ((bf16[128,2,2176]{2,0,1:T(8,128)(2,1)}), bf16[128,2,2176]{2,0,1:T(8,128)(2,1)S(1)}, u32[]{:S(2)}, u32[]{:S(2)}) async-start(bf16[128,2,2176]{2,0,1:T(8,128)(2,1)} %bitcast.95), calls=%async_computation.3 | async-start | bytes 2228224 | tf_op jit(solution)/shard_map/all_to_all | solution.py:272
  836.4 12.8 all-to-all-start
  852.6 548.8 %all-reduce.23.cloned.1.call-start = ((), (), s32[]{:S(2)}) async-start(), calls=%async_computation.10 | async-start | bytes 57376768 | tf_op jit(solution)/shard_map/psum | solution.py:295
  (74 other events, 780.5 us)
Sparse Core Ops, SparseCore 0:
  9.6 93.8 all-gather.7
  105.0 37.7 all-gather.9
  144.3 118.3 all-gather.13
  264.1 118.3 all-gather.11
  788.0 61.4 all-gather.15
  851.5 42.0 all-gather.17
  900.5 500.9 all-reduce.22
where the time goes:
time: 1430 us
  waiting for transfers between devices  648 us (45%)
  starting transfers between devices  463 us (32%)
  blocking collectives  122 us (9%)
  local copies, waits for them, and re-layouts  98.9 us (7%)
  matrix products  70.1 us (5%)
  between operations  16.8 us (1%)
    psum x1, waiting for transfers between devices, on_device(): lax.psum((vectors[0], vectors[1], grad_qkv, vectors[2], vectors[3], grad_...  409 us
    ppermute x62, starting transfers between devices, shifted(): return lax.ppermute(block, axis, route)  350 us
    ppermute x32, starting transfers between devices, from_behind(): return lax.ppermute(value, axis, pairs)  99.1 us
    all_gather x1, waiting for transfers between devices, on_device(): lax.all_gather(up_weight, 'fsdp', axis=0, tiled=True)  75.4 us
    all_gather x1, waiting for transfers between devices, on_device(): lax.all_gather(qkv_weight, 'fsdp', axis=0, tiled=True)  73.9 us
    while x94, local copies, waits for them, and re-layouts  69.4 us
    psum x1, blocking collectives, on_device(): lax.psum((vectors[0], vectors[1], grad_qkv, vectors[2], vectors[3], grad_...  67.7 us
    dot_general x8, matrix products, contract(): lax.dot_general(left, right, (((left_dim,), (right_dim,)), ((), ())), pre...  40.3 us
  transfers between devices with their start and end apart: 105, of which 28 were waited for; matrix products, arithmetic and copies ran while one was open for 7% of the time, Pallas kernels for 0%

commit v1 on v0

v1 whole, which is shorter than its diff:
```python
import jax
import jax.numpy as jnp
from jax import lax
from jax.experimental import pallas as pl
from jax.experimental.pallas import tpu as pltpu
from jax.sharding import PartitionSpec as P

HEADS = 17
HEAD_DIM = 64


EPS = 1e-05
NEG = -1e30


def shifted(block, axis, distance):
    devices = range(lax.axis_size(axis))
    route = [(i - distance, i) for i in devices if i - distance in devices]
    return lax.ppermute(block, axis, route)


def from_behind(value, axis, steps):
    count = lax.axis_size(axis)
    pairs = [(source, (source + steps) % count) for source in range(count)]
    return lax.ppermute(value, axis, pairs)


def normalize(rows, gain, shift):
    mean = jnp.mean(rows, axis=-1, keepdims=True)
    centered = rows - mean
    rstd = lax.rsqrt(jnp.mean(centered * centered, axis=-1, keepdims=True) + EPS)
    hat = centered * rstd
    return (hat * gain + shift, hat, rstd)


def normalize_back(grad, hat, rstd, gain):
    scaled = grad * gain
    return rstd * (
        scaled
        - jnp.mean(scaled, axis=-1, keepdims=True)
        - hat * jnp.mean(scaled * hat, axis=-1, keepdims=True)
    )


def gelu_tanh(value):
    return jax.nn.gelu(value, approximate=True)


def gelu_back(pre, grad):
    _, pull = jax.vjp(gelu_tanh, pre)
    return pull(grad)[0]


def contract(left, right, left_dim, right_dim):
    return lax.dot_general(
        left, right, (((left_dim,), (right_dim,)), ((), ())), preferred_element_type=jnp.float32
    )


def block_scores(query, key_block, query_pos, key_pos, scale):
    scores = (
        jnp.einsum("the,khe->htk", query, key_block, preferred_element_type=jnp.float32) * scale
    )
    allowed = key_pos[None, None, :] <= query_pos[None, :, None]
    return jnp.where(allowed, scores, NEG)


def matmul(left, right, left_dim, right_dim):
    return lax.dot_general(
        left, right, (((left_dim,), (right_dim,)), ((), ())), preferred_element_type=jnp.float32
    )


QUERY_ROWS = 256


def softmax_block(query, keys, values, first_query):
    scores = matmul(keys, query, 1, 1)
    key_pos = lax.broadcasted_iota(jnp.int32, scores.shape, 0)
    query_pos = lax.broadcasted_iota(jnp.int32, scores.shape, 1) + first_query
    scores = jnp.where(key_pos <= query_pos, scores, NEG)
    top = jnp.max(scores, axis=0, keepdims=True)
    weights = jnp.exp(scores - top)
    total = jnp.sum(weights, axis=0, keepdims=True)
    mixed = matmul(values, weights.astype(jnp.bfloat16), 0, 0) / total
    return mixed.astype(jnp.bfloat16), top + jnp.log(total)


def attend_kernel(place_ref, packed_ref, extra_ref, out_ref, outt_ref, lse_ref, xout_ref, xoutt_ref, xlse_ref):
    length = packed_ref.shape[0]
    scale = HEAD_DIM ** (-0.5)
    for start in range(0, length, QUERY_ROWS):
        stop = start + QUERY_ROWS
        query = packed_ref[start:stop, 0:64] * scale
        mixed, lse = softmax_block(
            query.astype(jnp.bfloat16), packed_ref[0:stop, 64:128], packed_ref[0:stop, 128:192], start
        )
        outt_ref[:, start:stop] = mixed
        out_ref[start:stop, :] = mixed.astype(jnp.float32).T.astype(jnp.bfloat16)
        lse_ref[:, start:stop] = lse
    query = (extra_ref[...] * scale).astype(jnp.bfloat16)
    mixed, lse = softmax_block(
        query, packed_ref[:, 192:256], packed_ref[:, 256:320], place_ref[0] * extra_ref.shape[0]
    )
    xoutt_ref[...] = mixed
    xout_ref[...] = mixed.astype(jnp.float32).T.astype(jnp.bfloat16)
    xlse_ref[...] = lse


def back_block(query, keys, values, lse, grad, mixed, first_query):
    scale = HEAD_DIM ** (-0.5)
    query = (query * scale).astype(jnp.bfloat16)
    scores = matmul(keys, query, 1, 1)
    key_pos = lax.broadcasted_iota(jnp.int32, scores.shape, 0)
    query_pos = lax.broadcasted_iota(jnp.int32, scores.shape, 1) + first_query
    prob = jnp.where(key_pos <= query_pos, jnp.exp(scores - lse), 0.0)
    grad_values = matmul(prob.astype(jnp.bfloat16), grad, 1, 0)
    grad_prob = matmul(values, grad, 1, 1)
    delta = jnp.sum(
        grad.astype(jnp.float32).T * mixed.astype(jnp.float32), axis=0, keepdims=True
    )
    grad_score = (prob * (grad_prob - delta)).astype(jnp.bfloat16)
    grad_keys = matmul(grad_score, query, 1, 0)
    grad_query = matmul(keys, grad_score, 0, 0) * scale
    return grad_query.T, grad_keys, grad_values


def attend_back_kernel(
    place_ref, packed_ref, extra_ref, outt_ref, lse_ref, xoutt_ref, xlse_ref, grad_ref, xgrad_ref,
    dpacked_ref, dextra_ref, dkeys, dvalues,
):
    length = packed_ref.shape[0]
    starts = list(range(0, length, QUERY_ROWS))
    for start in reversed(starts):
        stop = start + QUERY_ROWS
        dq, dk, dv = back_block(
            packed_ref[start:stop, 0:64], packed_ref[0:stop, 64:128], packed_ref[0:stop, 128:192],
            lse_ref[:, start:stop], grad_ref[start:stop, :], outt_ref[:, start:stop], start,
        )
        dpacked_ref[start:stop, 0:64] = dq.astype(jnp.bfloat16)
        if start == starts[-1]:
            dkeys[...] = dk
            dvalues[...] = dv
        else:
            dkeys[0:stop, :] += dk
            dvalues[0:stop, :] += dv
    dpacked_ref[:, 64:128] = dkeys[...].astype(jnp.bfloat16)
    dpacked_ref[:, 128:192] = dvalues[...].astype(jnp.bfloat16)
    dq, dk, dv = back_block(
        extra_ref[...], packed_ref[:, 192:256], packed_ref[:, 256:320],
        xlse_ref[...], xgrad_ref[...], xoutt_ref[...], place_ref[0] * extra_ref.shape[0],
    )
    dextra_ref[...] = dq.astype(jnp.bfloat16)
    dpacked_ref[:, 192:256] = dk.astype(jnp.bfloat16)
    dpacked_ref[:, 256:320] = dv.astype(jnp.bfloat16)


def vmem(count):
    return [pl.BlockSpec(memory_space=pltpu.VMEM)] * count


def attend(place, packed, extra):
    length, rows = packed.shape[0], extra.shape[0]
    bf16, f32 = jnp.bfloat16, jnp.float32
    return pl.pallas_call(
        attend_kernel,
        out_shape=(
            jax.ShapeDtypeStruct((length, HEAD_DIM), bf16),
            jax.ShapeDtypeStruct((HEAD_DIM, length), bf16),
            jax.ShapeDtypeStruct((1, length), f32),
            jax.ShapeDtypeStruct((rows, HEAD_DIM), bf16),
            jax.ShapeDtypeStruct((HEAD_DIM, rows), bf16),
            jax.ShapeDtypeStruct((1, rows), f32),
        ),
        in_specs=[pl.BlockSpec(memory_space=pltpu.SMEM)] + vmem(2),
        out_specs=tuple(vmem(6)),
        compiler_params=pltpu.CompilerParams(vmem_limit_bytes=40 * 2**20),
        name="attend",
    )(place, packed, extra)


def attend_back(place, packed, extra, outt, lse, xoutt, xlse, grad, xgrad):
    length, rows = packed.shape[0], extra.shape[0]
    return pl.pallas_call(
        attend_back_kernel,
        out_shape=(
            jax.ShapeDtypeStruct((length, 5 * HEAD_DIM), jnp.bfloat16),
            jax.ShapeDtypeStruct((rows, HEAD_DIM), jnp.bfloat16),
        ),
        in_specs=[pl.BlockSpec(memory_space=pltpu.SMEM)] + vmem(8),
        out_specs=tuple(vmem(2)),
        scratch_shapes=[
            pltpu.VMEM((length, HEAD_DIM), jnp.float32),
            pltpu.VMEM((length, HEAD_DIM), jnp.float32),
        ],
        compiler_params=pltpu.CompilerParams(vmem_limit_bytes=48 * 2**20),
        name="attend_back",
    )(place, packed, extra, outt, lse, xoutt, xlse, grad, xgrad)


def swap(blocks_of, axis):
    return lax.all_to_all(blocks_of, axis, split_axis=0, concat_axis=0, tiled=True)


def by_head(rows_of, blocks):
    return rows_of[:, : blocks * HEAD_DIM].reshape(-1, blocks, HEAD_DIM).transpose(1, 0, 2)


def from_head(parts, last):
    blocks, rows, _ = parts.shape
    return jnp.concatenate([parts.transpose(1, 0, 2).reshape(rows, blocks * HEAD_DIM), last], axis=1)


def head_attention(query, keys, values):
    blocks = lax.axis_size("ctx")
    rows = query.shape[0]
    place = lax.axis_index("ctx").astype(jnp.int32).reshape(1)
    cut = blocks * HEAD_DIM
    shared = jnp.concatenate([keys[:, cut:], values[:, cut:]], axis=1)
    packed = jnp.concatenate(
        [by_head(query, blocks), by_head(keys, blocks), by_head(values, blocks),
         jnp.broadcast_to(shared[None], (blocks, rows, 2 * HEAD_DIM))],
        axis=2,
    )
    packed = swap(packed, "ctx").reshape(blocks * rows, 5 * HEAD_DIM)
    extra = query[:, cut:]
    out, outt, lse, xout, xoutt, xlse = attend(place, packed, extra)
    back = swap(out.reshape(blocks, rows, HEAD_DIM), "ctx")
    joined = from_head(back, xout)

    def backward(grad_joined):
        grad = swap(by_head(grad_joined, blocks), "ctx").reshape(blocks * rows, HEAD_DIM)
        dpacked, dextra = attend_back(
            place, packed, extra, outt, lse, xoutt, xlse, grad, grad_joined[:, cut:]
        )
        dback = swap(dpacked.reshape(blocks, rows, 5 * HEAD_DIM), "ctx")
        dshared = jnp.sum(dback[:, :, 3 * HEAD_DIM :].astype(jnp.float32), axis=0).astype(jnp.bfloat16)
        return (
            from_head(dback[:, :, :HEAD_DIM], dextra),
            from_head(dback[:, :, HEAD_DIM : 2 * HEAD_DIM], dshared[:, :HEAD_DIM]),
            from_head(dback[:, :, 2 * HEAD_DIM : 3 * HEAD_DIM], dshared[:, HEAD_DIM:]),
        )

    return joined, backward


def ring_attention(query, keys, values):
    position = lax.axis_index("ctx")
    blocks = lax.axis_size("ctx")
    count_rows, width = query.shape
    scale = HEAD_DIM ** (-0.5)
    offsets = jnp.arange(count_rows, dtype=jnp.int32)
    query_pos = position * count_rows + offsets
    shape_heads = (count_rows, HEADS, HEAD_DIM)
    query, keys, values = (part.reshape(shape_heads) for part in (query, keys, values))

    def forward_block(carry, key_block, value_block, source):
        run_max, run_sum, accum = carry
        scores = block_scores(query, key_block, query_pos, source * count_rows + offsets, scale)
        new_max = jnp.maximum(run_max, jnp.max(scores, axis=-1))
        factor = jnp.exp(run_max - new_max)
        weights = jnp.exp(scores - new_max[:, :, None])
        run_sum = run_sum * factor + jnp.sum(weights, axis=-1)
        accum = accum * factor[:, :, None] + jnp.einsum(
            "htk,khe->hte",
            weights.astype(jnp.bfloat16),
            value_block,
            preferred_element_type=jnp.float32,
        )
        return (new_max, run_sum, accum)

    def forward_visit(step, state):
        carry, key_block, value_block, stored = state
        source = (position - step) % blocks
        carry = lax.cond(
            source <= position,
            lambda inner: forward_block(inner, key_block, value_block, source),
            lambda inner: inner,
            carry,
        )
        return (carry, key_block, value_block, stored)

    def forward_step(step, state):
        carry, key_block, value_block, stored = forward_visit(step, state)
        key_block, value_block = shifted((key_block, value_block), "ctx", 1)
        return (carry, key_block, value_block, stored)

    stored_start = ()
    start = (
        jnp.full((HEADS, count_rows), NEG, jnp.float32),
        jnp.zeros((HEADS, count_rows), jnp.float32),
        jnp.zeros((HEADS, count_rows, HEAD_DIM), jnp.float32),
    )
    state = lax.fori_loop(0, blocks - 1, forward_step, (start, keys, values, stored_start))
    (run_max, run_sum, accum), _, _, stored_blocks = forward_visit(blocks - 1, state)
    attended = (accum / run_sum[:, :, None]).transpose(1, 0, 2).astype(jnp.bfloat16)
    lse = run_max + jnp.log(run_sum)

    def backward(grad_joined):
        grad_attended = grad_joined.reshape(shape_heads)
        delta_rows = jnp.sum(
            grad_attended.astype(jnp.float32) * attended.astype(jnp.float32), axis=-1
        ).T

        def backward_block(source, key_block, value_block, grads):
            grad_query, grad_keys, grad_values = grads
            scores = block_scores(query, key_block, query_pos, source * count_rows + offsets, scale)
            prob = jnp.exp(scores - lse[:, :, None])
            grad_values = grad_values + jnp.einsum(
                "htk,the->khe",
                prob.astype(jnp.bfloat16),
                grad_attended,
                preferred_element_type=jnp.float32,
            )
            grad_prob = jnp.einsum(
                "the,khe->htk", grad_attended, value_block, preferred_element_type=jnp.float32
            )
            grad_score = (prob * (grad_prob - delta_rows[:, :, None]) * scale).astype(jnp.bfloat16)
            grad_query = grad_query + jnp.einsum(
                "htk,khe->the", grad_score, key_block, preferred_element_type=jnp.float32
            )
            grad_keys = grad_keys + jnp.einsum(
                "htk,the->khe", grad_score, query, preferred_element_type=jnp.float32
            )
            return (grad_query, grad_keys, grad_values)

        zero_block = jnp.zeros(shape_heads, jnp.float32)

        def backward_step(step, state):
            grad_query, key_block, value_block, grad_keys, grad_values = state
            source = (position - step) % blocks
            grad_query, grad_keys, grad_values = lax.cond(
                source <= position,
                lambda inner: backward_block(source, key_block, value_block, inner),
                lambda inner: inner,
                (grad_query, grad_keys, grad_values),
            )
            key_block, value_block = shifted((key_block, value_block), "ctx", 1)
            grad_keys, grad_values = from_behind((grad_keys, grad_values), "ctx", 1)
            return (grad_query, key_block, value_block, grad_keys, grad_values)

        grad_query, _, _, grad_keys, grad_values = lax.fori_loop(
            0, blocks, backward_step, (zero_block, keys, values, zero_block, zero_block)
        )
        return tuple(
            part.reshape(count_rows, width) for part in (grad_query, grad_keys, grad_values)
        )

    return attended.reshape(count_rows, width), backward


def on_device(
    block_input,
    cotangent,
    first_gain,
    first_shift,
    qkv_weight,
    query_bias,
    value_bias,
    out_weight,
    out_bias,
    second_gain,
    second_shift,
    up_weight,
    up_bias,
    down_weight,
    down_bias,
):
    fsdp = lax.axis_size("fsdp")
    blocks = lax.axis_size("ctx")
    place = lax.axis_index("fsdp")
    width = HEADS * HEAD_DIM
    f32, bf16 = jnp.float32, jnp.bfloat16
    small = (
        first_gain, first_shift, query_bias, value_bias, out_bias, second_gain, second_shift,
        down_bias, up_bias,
    )
    sizes = [part.shape[0] for part in small]
    gathered = lax.all_gather(jnp.concatenate(small), "fsdp", axis=0, tiled=False)
    whole_small, at = [], 0
    for size in sizes:
        whole_small.append(gathered[:, at : at + size].reshape(fsdp * size).astype(f32))
        at += size
    gain_one, shift_one, bias_q, bias_v, bias_o, gain_two, shift_two, bias_d, bias_u = whole_small
    whole_qkv, whole_out, whole_up, whole_down = (
        lax.all_gather(part, "fsdp", axis=0, tiled=True)
        for part in (qkv_weight, out_weight, up_weight, down_weight)
    )
    rows = block_input.astype(f32)
    first_norm, first_hat, first_rstd = normalize(rows, gain_one, shift_one)
    first_act = first_norm.astype(bf16)
    qkv = jnp.dot(first_act, whole_qkv, preferred_element_type=f32)
    query = (qkv[:, :width] + bias_q).astype(bf16)
    keys = qkv[:, width : 2 * width].astype(bf16)
    values = (qkv[:, 2 * width :] + bias_v).astype(bf16)
    attention = head_attention if HEADS == blocks + 1 else ring_attention
    joined, attention_back = attention(query, keys, values)
    mid = rows + jnp.dot(joined, whole_out, preferred_element_type=f32) + bias_o
    second_norm, second_hat, second_rstd = normalize(mid, gain_two, shift_two)
    second_act = second_norm.astype(bf16)
    pre = jnp.dot(second_act, whole_up, preferred_element_type=f32) + bias_u
    act = gelu_tanh(pre).astype(bf16)
    block_output = mid + jnp.dot(act, whole_down, preferred_element_type=f32) + bias_d

    def left(part):
        return lax.all_to_all(part, "fsdp", split_axis=1, concat_axis=0, tiled=True)

    def right(part):
        return lax.all_gather(part, "fsdp", axis=0, tiled=True)

    def weight_grad(left_part, right_part):
        return lax.psum(contract(left(left_part), right(right_part), 0, 0).astype(bf16), "ctx")

    cot_float = cotangent.astype(f32)
    grad_down = weight_grad(act, cotangent)
    grad_down_bias = jnp.sum(cot_float, axis=0)
    grad_pre = gelu_back(pre, contract(cotangent, whole_down, 1, 1))
    grad_pre_b = grad_pre.astype(bf16)
    grad_up = weight_grad(second_act, grad_pre_b)
    grad_up_bias = jnp.sum(grad_pre, axis=0)
    grad_second = contract(grad_pre_b, whole_up, 1, 1)
    grad_second_gain = jnp.sum(grad_second * second_hat, axis=0)
    grad_second_shift = jnp.sum(grad_second, axis=0)
    grad_mid = cot_float + normalize_back(grad_second, second_hat, second_rstd, gain_two)
    grad_mid_b = grad_mid.astype(bf16)
    grad_out = weight_grad(joined, grad_mid_b)
    grad_out_bias = jnp.sum(grad_mid, axis=0)
    grad_attended = contract(grad_mid_b, whole_out, 1, 1).astype(bf16)
    grad_query, grad_keys, grad_values = attention_back(grad_attended)
    grad_query_bias = jnp.sum(grad_query.astype(f32), axis=0)
    grad_value_bias = jnp.sum(grad_values.astype(f32), axis=0)
    grad_qkv_b = jnp.concatenate([grad_query, grad_keys, grad_values], axis=1).astype(bf16)
    grad_qkv = weight_grad(first_act, grad_qkv_b)
    grad_first = contract(grad_qkv_b, whole_qkv, 1, 1)
    grad_first_gain = jnp.sum(grad_first * first_hat, axis=0)
    grad_first_shift = jnp.sum(grad_first, axis=0)
    input_grad = grad_mid + normalize_back(grad_first, first_hat, first_rstd, gain_one)
    vectors = (
        grad_first_gain, grad_first_shift, grad_query_bias, grad_value_bias, grad_out_bias,
        grad_second_gain, grad_second_shift, grad_down_bias, grad_up_bias,
    )
    summed = lax.psum(
        jnp.concatenate([part.reshape(fsdp, -1) for part in vectors], axis=1), ("fsdp", "ctx")
    )
    mine = lax.dynamic_index_in_dim(summed, place, 0, keepdims=False)
    shards, at = [], 0
    for size in sizes:
        shards.append(mine[at : at + size])
        at += size
    gain_g1, shift_g1, bias_gq, bias_gv, bias_go, gain_g2, shift_g2, bias_gd, bias_gu = shards
    return (
        block_output,
        input_grad,
        gain_g1,
        shift_g1,
        grad_qkv.astype(f32),
        bias_gq,
        bias_gv,
        grad_out.astype(f32),
        bias_go,
        gain_g2,
        shift_g2,
        grad_up.astype(f32),
        bias_gu,
        grad_down.astype(f32),
        bias_gd,
    )


def solution(mesh):
    placed = (
        P(("fsdp", "ctx"), None),
        P(("fsdp", "ctx"), None),
        P("fsdp"),
        P("fsdp"),
        P("fsdp", None),
        P("fsdp"),
        P("fsdp"),
        P("fsdp", None),
        P("fsdp"),
        P("fsdp"),
        P("fsdp"),
        P("fsdp", None),
        P("fsdp"),
        P("fsdp", None),
        P("fsdp"),
    )
    return jax.shard_map(
        on_device,
        mesh=mesh,
        in_specs=placed,
        out_specs=(
            P(("fsdp", "ctx"), None),
            P(("fsdp", "ctx"), None),
            P("fsdp"),
            P("fsdp"),
            P("fsdp", None),
            P("fsdp"),
            P("fsdp"),
            P("fsdp", None),
            P("fsdp"),
            P("fsdp"),
            P("fsdp"),
            P("fsdp", None),
            P("fsdp"),
            P("fsdp", None),
            P("fsdp"),
        ),
        check_vma=False,
    )
```

time: 1430 us -> 854 us (0.60)
  starting transfers between devices: 463 us -> 38.6 us
  local copies, waits for them, and re-layouts: 98.9 us -> 23.8 us
  waiting for transfers between devices: 648 us -> 574 us
  blocking collectives: 122 us -> 93.9 us
  other arithmetic: 7.31 us -> 22.7 us
  Pallas kernels: 0 us -> 14.9 us
    ppermute x94 -> x0, starting transfers between devices: 449 us -> none  [the longest x62 350 us: shifted(): return lax.ppermute(block, axis, route)]
    psum x1, waiting for transfers between devices: 409 us -> 205 us  [weight_grad(): lax.psum(contract(left(left_part), right(right_part), 0, 0).astype(bf16),...]
    all_gather x6, waiting for transfers between devices: 185 us -> 296 us  [the longest x4 296 us: on_device(): lax.all_gather(part, 'fsdp', axis=0, tiled=True)]
    while x94 -> x0, local copies, waits for them, and re-layouts: 69.4 us -> none
    all_to_all x4 -> x8, waiting for transfers between devices: 8.29 us -> 69.2 us  [the longest x4 63.1 us: swap(): lax.all_to_all(blocks_of, axis, split_axis=0, concat_axis=0, tiled=True)]
    ppermute x94 -> x0, waiting for transfers between devices: 42 us -> none  [the longest x32 23.7 us: from_behind(): return lax.ppermute(value, axis, pairs)]
    psum x1, blocking collectives: 67.7 us -> 42.7 us  [on_device(): lax.psum(jnp.concatenate([part.reshape(fsdp, -1) for part in vectors], ax...]
    all_to_all x4 -> x8, starting transfers between devices: 13.9 us -> 38 us  [the longest x4 23.4 us: swap(): lax.all_to_all(blocks_of, axis, split_axis=0, concat_axis=0, tiled=True)]
  transfers between devices with their start and end apart: 105 -> 15, of which waited for: 28 -> 10; matrix products, arithmetic and copies ran while one was open for 7% -> 7% of each run, Pallas kernels for 0% -> 1%
where the time goes in v1:
time: 854 us; the launch traced here: 845 us
  waiting for transfers between devices  574 us (67%)
  blocking collectives  93.9 us (11%)
  matrix products  62.2 us (7%)
  starting transfers between devices  38.6 us (5%)
  local copies, waits for them, and re-layouts  23.8 us (3%)
  other arithmetic  22.7 us (3%)
  between operations  15.1 us (2%)
  Pallas kernels  14.9 us (2%)
    all_gather x4, waiting for transfers between devices, on_device(): lax.all_gather(part, 'fsdp', axis=0, tiled=True)  296 us
    psum x1, waiting for transfers between devices, weight_grad(): lax.psum(contract(left(left_part), right(right_part), 0, 0).astype(bf16),...  205 us
    all_to_all x4, waiting for transfers between devices, swap(): lax.all_to_all(blocks_of, axis, split_axis=0, concat_axis=0, tiled=True)  63.1 us
    all_gather x2, blocking collectives, right(): return lax.all_gather(part, 'fsdp', axis=0, tiled=True)  45.7 us
    psum x1, blocking collectives, on_device(): lax.psum(jnp.concatenate([part.reshape(fsdp, -1) for part in vectors], ax...  42.7 us
    dot_general x8, matrix products, contract(): lax.dot_general(left, right, (((left_dim,), (right_dim,)), ((), ())), pre...  37 us
    all_to_all x4, starting transfers between devices, swap(): lax.all_to_all(blocks_of, axis, split_axis=0, concat_axis=0, tiled=True)  23.4 us
  transfers between devices with their start and end apart: 15, of which 10 were waited for; matrix products, arithmetic and copies ran while one was open for 7% of the time, Pallas kernels for 1%

profile of v1, /device:TPU:0, one launch (start us, length us, event | category | flops | bytes accessed | tf_op | source)
XLA Modules:
  0.0 844.7 jit_solution(13384276011647886056)
XLA Ops:
  7.2 0.7 all-gather.9.cloned.1.call-update
  8.0 0.7 all-gather.15.cloned.1.call-update
  8.7 0.7 all-gather.11.cloned.1.call-update
  10.3 5.4 all-gather.1
  16.9 86.5 %all-gather.9.cloned.1.call-done = bf16[1088,3264]{1,0:T(8,128)(2,1)} async-done(((bf16[544,3264]{1,0:T(8,128)(2,1)}), bf16[1088,3264]{1,0:T(8,128)(2,1)}) %all-gather.9.cloned.1.call-update) | async-done | bytes 7102480 | tf_op jit(solution)/shard_map/all_gather | solution.py:386
  103.4 6.1 fusion.35
  110.4 1.1 pad_maximum_fusion
  111.5 5.7 all-to-all-start
  117.5 27.2 %all-to-all-done = bf16[16,128,320]{1,2,0:T(8,128)(2,1)} async-done(((bf16[16,128,320]{1,2,0:T(8,128)(2,1)}), bf16[16,128,320]{1,2,0:T(8,128)(2,1)}, u32[]{:S(2)}, u32[]{:S(2)}) %all-to-all-start) | async-done | bytes 1310752 | tf_op jit(solution)/shard_map/all_to_all | solution.py:202
  144.7 1.8 copy.57
  146.5 7.0 attend.1
  153.5 0.9 copy.58
  154.4 8.2 all-to-all-start.1
  162.6 60.7 %all-gather.15.cloned.1.call-done = bf16[4352,1088]{0,1:T(8,128)(2,1)} async-done(((bf16[2176,1088]{0,1:T(8,128)(2,1)}), bf16[4352,1088]{0,1:T(8,128)(2,1)}) %all-gather.15.cloned.1.call-update) | async-done | bytes 9469968 | tf_op jit(solution)/shard_map/all_gather | solution.py:386
  223.3 6.7 fusion.37
  230.1 32.5 %all-gather.11.cloned.1.call-done = bf16[1088,1088]{1,0:T(8,128)(2,1)} async-done(((bf16[544,1088]{1,0:T(8,128)(2,1)}), bf16[1088,1088]{1,0:T(8,128)(2,1)}) %all-gather.11.cloned.1.call-update) | async-done | bytes 2367504 | tf_op jit(solution)/shard_map/all_gather | solution.py:386
  262.7 3.0 fusion.36
  266.2 116.3 %all-gather.13.cloned.1.call-done = bf16[1088,4352]{1,0:T(8,128)(2,1)} async-done(((bf16[544,4352]{1,0:T(8,128)(2,1)}), bf16[1088,4352]{1,0:T(8,128)(2,1)}) %all-gather.13.cloned.1.call-update) | async-done | bytes 9469968 | tf_op jit(solution)/shard_map/all_gather | solution.py:386
  382.5 9.0 %fusion.29 = (f32[4352]{0:T(1024)S(1)}, bf16[128,4352]{1,0:T(8,128)(2,1)}, bf16[128,4352]{1,0:T(8,128)(2,1)}) fusion(f32[128,4352]{1,0:T(8,128)} %fusion.37, f32[4352]{0:T(1024)S(1)} %reshape.259, bf16[128,1088]{0,1:T(8,128)(2,1)S(1)} %add_convert_fusion.1, bf16[1088,4352]{1,0:T(8,128)(2,1)} %all-gather.13.cloned.1.call-done), kind=kOutput, calls=%fused_computation.93 | convolution fusion | flops 1225518848 | bytes 14239744 | tf_op jit(solution)/shard_map/dot_general | solution.py:401
  391.5 6.8 multiply_reduce_fusion
  398.9 1.3 copy-done.1
  400.2 0.9 convolution_convert_fusion.4
  401.2 0.7 copy-done.18
  401.9 0.7 slice.193
  402.6 1.8 copy.61
  404.4 5.9 all-to-all-start.2
  410.3 0.8 slice.194.xgrad_ref
  411.1 9.3 %all-to-all-done.2 = bf16[16,128,64]{1,2,0:T(8,128)(2,1)} async-done(((bf16[16,128,64]{1,2,0:T(8,128)(2,1)}), bf16[16,128,64]{1,2,0:T(8,128)(2,1)}, u32[]{:S(2)}, u32[]{:S(2)}) %all-to-all-start.2) | async-done | bytes 262176 | tf_op jit(solution)/shard_map/all_to_all | solution.py:202
  420.4 1.2 copy.62
  421.6 7.9 attend_back.1
  429.5 1.1 copy-done
  430.7 2.5 copy.63
  433.2 3.7 all-to-all-start.3
  437.7 26.6 %all-to-all-done.3 = bf16[16,128,320]{1,2,0:T(8,128)(2,1)S(1)} async-done(((bf16[16,128,320]{1,2,0:T(8,128)(2,1)}), bf16[16,128,320]{1,2,0:T(8,128)(2,1)S(1)}, u32[]{:S(2)}, u32[]{:S(2)}) %all-to-all-start.3) | async-done | bytes 1310752 | tf_op jit(solution)/shard_map/all_to_all | solution.py:202
  464.3 1.1 copy-done.4
  465.4 0.7 constant_dynamic-update-slice_fusion.4
  466.7 0.7 constant_dynamic-update-slice_fusion.2
  467.5 1.1 slice_reduce_fusion
  469.2 0.7 constant_dynamic-update-slice_fusion.1
  470.6 0.7 pad_maximum_fusion.1
  471.3 3.4 all-to-all-start.5
  474.8 1.1 copy.91
  475.8 5.5 all-to-all-done.5
  481.3 0.7 copy-done.20
  482.0 3.6 all-to-all-start.7
  485.6 36.5 %all_gather.39 = bf16[256,1088]{0,1:T(8,128)(2,1)} all-gather(bf16[128,1088]{0,1:T(8,128)(2,1)} %param.16), channel_id=1, replica_groups=mesh['fsdp'=2,'ctx'=16] {'fsdp'}, dimensions={0}, use_global_device_ids=true | all-gather | bytes 835584 | tf_op jit(solution)/shard_map/all_gather | solution.py:409
  522.1 9.2 %all_gather.37 = bf16[256,1088]{0,1:T(8,128)(2,1)S(1)} all-gather(bf16[128,1088]{0,1:T(8,128)(2,1)} %copy-done.10), channel_id=1, replica_groups=mesh['fsdp'=2,'ctx'=16] {'fsdp'}, dimensions={0}, use_global_device_ids=true | all-gather | bytes 835584 | tf_op jit(solution)/shard_map/all_gather | solution.py:409
  531.3 2.6 convolution_convert_fusion.3
  533.9 4.1 all-to-all-start.6
  538.0 4.7 convolution_convert_fusion
  543.3 3.4 all-to-all-start.4
  547.1 5.3 convolution_convert_fusion.1
  552.4 4.4 convolution_convert_fusion.2
  557.3 7.1 fusion.1
  564.4 5.5 fusion.20
  570.8 42.7 %psum.35 = f32[2,6528]{1,0:T(2,128)S(1)} all-reduce(f32[2,6528]{1,0:T(2,128)S(1)} %concatenate.32), channel_id=1, replica_groups=mesh['fsdp'=2,'ctx'=16] {'fsdp','ctx'}, use_global_device_ids=true, to_apply=%region_18.0 | all-reduce | flops 13056 | bytes 104448 | tf_op jit(solution)/shard_map/psum | solution.py:442
  613.5 0.7 dynamic-slice_reduce_fusion
  614.2 0.7 dynamic-slice_reduce_fusion.1
  614.9 1.0 fusion.19
  616.0 205.2 %all-reduce.3.cloned.1.call-done = (bf16[544,3264]{1,0:T(8,128)(2,1)}, bf16[544,1088]{1,0:T(8,128)(2,1)}, bf16[544,4352]{1,0:T(8,128)(2,1)}, bf16[2176,1088]{0,1:T(8,128)(2,1)}) async-done(((bf16[544,3264]{1,0:T(8,128)(2,1)}, bf16[544,1088]{1,0:T(8,128)(2,1)}, bf16[544,4352]{1,0:T(8,128)(2,1)}, bf16[2176,1088]{0,1:T(8,128)(2,1)}), (bf16[544,3264]{1,0:T(8,128)(2,1)}, bf16[544,1088]{1,0:T(8,128)(2,1)}, ...) | async-done | bytes 14204944 | tf_op jit(solution)/shard_map/psum | solution.py:412
  821.2 5.7 convert_element_type.184
  826.9 1.6 convert_element_type.186
  828.6 4.5 convert_element_type.188
  833.0 4.4 convert_element_type.190
  (140 shorter events, 9.2 us)
Async XLA Ops:
  7.2 96.2 %all-gather.9.cloned.1.call-start = ((), (), s32[]{:S(2)}) async-start(), calls=%async_computation.8 | async-start | bytes 10862592 | tf_op jit(solution)/shard_map/all_gather | solution.py:386
  7.9 215.4 %all-gather.15.cloned.1.call-start = ((), (), s32[]{:S(2)}) async-start(), calls=%async_computation.11 | async-start | bytes 14204928 | tf_op jit(solution)/shard_map/all_gather | solution.py:386
  8.7 254.0 %all-gather.11.cloned.1.call-start = ((), (), s32[]{:S(2)}) async-start(), calls=%async_computation.9 | async-start | bytes 3760128 | tf_op jit(solution)/shard_map/all_gather | solution.py:386
  9.4 0.7 copy-start.21
  9.4 0.7 copy-start.22
  9.4 0.7 copy-start.23
  9.4 0.7 copy-start.24
  9.4 0.7 copy-start.25
  9.5 0.7 copy-start.26
  9.5 0.7 copy-start.27
  9.5 0.7 copy-start.28
  9.5 0.7 copy-start.29
  9.5 6.7 copy-start.3
  9.5 373.0 %all-gather.13.cloned.1.call-start = ((), (), s32[]{:S(2)}) async-start(), calls=%async_computation.10 | async-start | bytes 14204928 | tf_op jit(solution)/shard_map/all_gather | solution.py:386
  16.9 92.6 %copy-start.9 = (bf16[128,1088]{0,1:T(8,128)(2,1)}, bf16[128,1088]{0,1:T(8,128)(2,1)S(1)}, u32[]{:S(2)}) copy-start(bf16[128,1088]{0,1:T(8,128)(2,1)S(1)} %fusion.15) | copy-start | bytes 835588
  111.5 33.1 %all-to-all-start = ((bf16[16,128,320]{1,2,0:T(8,128)(2,1)}), bf16[16,128,320]{1,2,0:T(8,128)(2,1)}, u32[]{:S(2)}, u32[]{:S(2)}) async-start(bf16[16,128,320]{1,2,0:T(8,128)(2,1)} %pad_maximum_fusion), calls=%async_computation | async-start | bytes 2621440 | tf_op jit(solution)/shard_map/all_to_all | solution.py:202
  117.5 105.9 %copy-start.7 = (bf16[128,1088]{0,1:T(8,128)(2,1)S(1)}, bf16[128,1088]{0,1:T(8,128)(2,1)}, u32[]{:S(2)}) copy-start(bf16[128,1088]{0,1:T(8,128)(2,1)} %param.16) | copy-start | bytes 835588
  154.4 108.2 %all-to-all-start.1 = ((bf16[16,128,64]{1,2,0:T(8,128)(2,1)}), bf16[16,128,64]{1,2,0:T(8,128)(2,1)S(1)}, u32[]{:S(2)}, u32[]{:S(2)}) async-start(bf16[16,128,64]{1,2,0:T(8,128)(2,1)} %copy.58), calls=%async_computation.1 | async-start | bytes 524288 | tf_op jit(solution)/shard_map/all_to_all | solution.py:202
  262.7 3.5 copy-start.15
  266.2 125.3 %copy-start.19 = (bf16[128,1088]{0,1:T(8,128)(2,1)}, bf16[128,1088]{0,1:T(8,128)(2,1)S(1)}, u32[]{:S(2)}) copy-start(bf16[128,1088]{0,1:T(8,128)(2,1)S(1)} %add_convert_fusion.1) | copy-start | bytes 835588
  391.5 6.9 copy-start.8
  398.3 1.9 copy-start.1
  398.9 5.6 copy-start.5
  400.2 0.9 copy-start.10
  401.2 0.7 copy-start.18
  404.4 16.0 %all-to-all-start.2 = ((bf16[16,128,64]{1,2,0:T(8,128)(2,1)}), bf16[16,128,64]{1,2,0:T(8,128)(2,1)}, u32[]{:S(2)}, u32[]{:S(2)}) async-start(bf16[16,128,64]{1,2,0:T(8,128)(2,1)} %bitcast.108), calls=%async_computation.2 | async-start | bytes 524288 | tf_op jit(solution)/shard_map/all_to_all | solution.py:202
  429.5 1.1 copy-start
  433.2 31.1 %all-to-all-start.3 = ((bf16[16,128,320]{1,2,0:T(8,128)(2,1)}), bf16[16,128,320]{1,2,0:T(8,128)(2,1)S(1)}, u32[]{:S(2)}, u32[]{:S(2)}) async-start(bf16[16,128,320]{1,2,0:T(8,128)(2,1)} %copy.63), calls=%async_computation.3 | async-start | bytes 2621440 | tf_op jit(solution)/shard_map/all_to_all | solution.py:202
  436.9 110.2 %all-gather.19.cloned.1.call-start = ((), (), s32[]{:S(2)}) async-start(), calls=%async_computation.13 | async-start | bytes 3342336 | tf_op jit(solution)/shard_map/all_gather | solution.py:409
  437.5 114.9 %all-gather.17.cloned.1.call-start = ((), (), s32[]{:S(2)}) async-start(), calls=%async_computation.12 | async-start | bytes 2506752 | tf_op jit(solution)/shard_map/all_gather | solution.py:409
  437.6 32.9 %copy-start.16 = (bf16[16,128,64]{1,2,0:T(8,128)(2,1)S(1)}, bf16[16,128,64]{1,2,0:T(8,128)(2,1)}, u32[]{:S(2)}) copy-start(bf16[16,128,64]{1,2,0:T(8,128)(2,1)} %copy-done.15) | copy-start | bytes 786436
  464.3 1.1 copy-start.4
  465.4 10.4 %copy-start.11 = (bf16[16,128,64]{1,2,0:T(8,128)(2,1)}, bf16[16,128,64]{1,2,0:T(8,128)(2,1)S(1)}, u32[]{:S(2)}) copy-start(bf16[16,128,64]{1,2,0:T(8,128)(2,1)S(1)} %get-tuple-element.58) | copy-start | bytes 786436
  465.4 10.4 %copy-start.13 = (bf16[16,128,64]{1,2,0:T(8,128)(2,1)}, bf16[16,128,64]{1,2,0:T(8,128)(2,1)S(1)}, u32[]{:S(2)}) copy-start(bf16[16,128,64]{1,2,0:T(8,128)(2,1)S(1)} %get-tuple-element.60) | copy-start | bytes 786436
  465.4 9.3 %copy-start.2 = (bf16[128,4352]{1,0:T(8,128)(2,1)S(1)}, bf16[128,4352]{1,0:T(8,128)(2,1)}, u32[]{:S(2)}) copy-start(bf16[128,4352]{1,0:T(8,128)(2,1)} %get-tuple-element.55) | copy-start | bytes 3342340
  471.3 10.0 %all-to-all-start.5 = ((bf16[128,2,544]{0,2,1:T(8,128)(2,1)}), bf16[128,2,544]{0,2,1:T(8,128)(2,1)S(1)}, u32[]{:S(2)}, u32[]{:S(2)}) async-start(bf16[128,2,544]{0,2,1:T(8,128)(2,1)} %bitcast.25), calls=%async_computation.5 | async-start | bytes 557056 | tf_op jit(solution)/shard_map/all_to_all | solution.py:406
  481.3 0.7 copy-start.20
  482.0 51.9 %all-to-all-start.7 = ((bf16[128,2,2176]{2,0,1:T(8,128)(2,1)}), bf16[128,2,2176]{2,0,1:T(8,128)(2,1)S(1)}, u32[]{:S(2)}, u32[]{:S(2)}) async-start(bf16[128,2,2176]{2,0,1:T(8,128)(2,1)} %bitcast.84), calls=%async_computation.7 | async-start | bytes 2228224 | tf_op jit(solution)/shard_map/all_to_all | solution.py:406
  533.9 9.5 %all-to-all-start.6 = ((bf16[128,2,544]{0,2,1:T(8,128)(2,1)}), bf16[128,2,544]{0,2,1:T(8,128)(2,1)}, u32[]{:S(2)}, u32[]{:S(2)}) async-start(bf16[128,2,544]{0,2,1:T(8,128)(2,1)} %bitcast.104), calls=%async_computation.6 | async-start | bytes 557056 | tf_op jit(solution)/shard_map/all_to_all | solution.py:406
  543.3 9.1 %all-to-all-start.4 = ((bf16[128,2,544]{0,2,1:T(8,128)(2,1)}), bf16[128,2,544]{0,2,1:T(8,128)(2,1)S(1)}, u32[]{:S(2)}, u32[]{:S(2)}) async-start(bf16[128,2,544]{0,2,1:T(8,128)(2,1)} %bitcast.97), calls=%async_computation.4 | async-start | bytes 557056 | tf_op jit(solution)/shard_map/all_to_all | solution.py:406
  546.8 274.4 %all-reduce.3.cloned.1.call-start = ((), (), s32[]{:S(2)}) async-start(), calls=%async_computation.14 | async-start | bytes 28688384 | tf_op jit(solution)/shard_map/psum | solution.py:412
  564.4 5.7 copy-start.14
  564.4 6.0 copy-start.12
  564.4 50.5 %copy-start.6 = (f32[128,1088]{0,1:T(8,128)S(1)}, f32[128,1088]{0,1:T(8,128)}, u32[]{:S(2)}) copy-start(f32[128,1088]{0,1:T(8,128)} %copy-done.5) | copy-start | bytes 1671172
  821.2 7.4 slice-start.2
  821.2 5.7 copy-start.17
  821.2 7.4 slice-start.3
  826.9 6.1 slice-start
  828.6 4.5 slice-start.1
Sparse Core Ops, SparseCore 0:
  9.6 93.7 all-gather.8
  104.9 118.3 all-gather.14
  224.9 37.7 all-gather.10
  264.1 118.3 all-gather.12
  439.6 34.9 all-gather.18
  475.9 43.9 all-gather.16
  557.0 264.1 all-reduce.2

commit v2 on v1

--- a/solution.py
+++ b/solution.py
@@ -347,6 +347,42 @@
         )
 
     return attended.reshape(count_rows, width), backward
+
+
+def other_half(value):
+    return lax.ppermute(value, "fsdp", [(0, 1), (1, 0)])
+
+
+def partner(value, bit):
+    count = lax.axis_size("ctx")
+    return lax.ppermute(value, "ctx", [(source, source ^ bit) for source in range(count)])
+
+
+def after(value, earlier):
+    return lax.optimization_barrier((value, earlier))[0]
+
+
+def gather_weights(shards):
+    quarter = lax.axis_index("ctx") % 4
+    place = lax.axis_index("fsdp")
+    wholes, earlier = [], None
+    for shard in shards:
+        depth, columns = shard.shape
+        parts = shard.reshape(4, depth // 4, columns)
+        piece = lax.dynamic_slice_in_dim(parts, quarter, 1, 0)
+        if earlier is not None:
+            piece = after(piece, earlier)
+        first = other_half(piece)
+        earlier = first
+        second = partner(first, 2)
+        third = partner(first, 1)
+        fourth = partner(second, 1)
+        whole = jnp.concatenate([parts, parts], axis=0)
+        base = (1 - place) * 4
+        for got, bits in ((first, 0), (second, 2), (third, 1), (fourth, 3)):
+            whole = lax.dynamic_update_slice_in_dim(whole, got, base + (quarter ^ bits), 0)
+        wholes.append(whole.reshape(2 * depth, columns))
+    return wholes
 
 
 def on_device(
@@ -382,10 +418,14 @@
         whole_small.append(gathered[:, at : at + size].reshape(fsdp * size).astype(f32))
         at += size
     gain_one, shift_one, bias_q, bias_v, bias_o, gain_two, shift_two, bias_d, bias_u = whole_small
-    whole_qkv, whole_out, whole_up, whole_down = (
-        lax.all_gather(part, "fsdp", axis=0, tiled=True)
-        for part in (qkv_weight, out_weight, up_weight, down_weight)
-    )
+    shards = (qkv_weight, out_weight, up_weight, down_weight)
+    paired = fsdp == 2 and blocks % 4 == 0
+    if paired:
+        whole_qkv, whole_out, whole_up, whole_down = gather_weights(shards)
+    else:
+        whole_qkv, whole_out, whole_up, whole_down = (
+            lax.all_gather(part, "fsdp", axis=0, tiled=True) for part in shards
+        )
     rows = block_input.astype(f32)
     first_norm, first_hat, first_rstd = normalize(rows, gain_one, shift_one)
     first_act = first_norm.astype(bf16)
@@ -403,27 +443,39 @@
     block_output = mid + jnp.dot(act, whole_down, preferred_element_type=f32) + bias_d
 
     def left(part):
+        if paired:
+            half = part.shape[1] // 2
+            own = lax.dynamic_slice_in_dim(part, place * half, half, 1)
+            sent = lax.dynamic_slice_in_dim(part, (1 - place) * half, half, 1)
+            return jnp.concatenate([own, other_half(sent)], axis=0)
         return lax.all_to_all(part, "fsdp", split_axis=1, concat_axis=0, tiled=True)
 
     def right(part):
+        if paired:
+            return jnp.concatenate([part, other_half(part)], axis=0)
         return lax.all_gather(part, "fsdp", axis=0, tiled=True)
 
     def weight_grad(left_part, right_part):
-        return lax.psum(contract(left(left_part), right(right_part), 0, 0).astype(bf16), "ctx")
+        return contract(left(left_part), right(right_part), 0, 0).astype(bf16)
+
+    def total(value, earlier=None):
+        if earlier is not None:
+            value = after(value, earlier)
+        return lax.psum(value, "ctx")
 
     cot_float = cotangent.astype(f32)
-    grad_down = weight_grad(act, cotangent)
+    grad_down = total(weight_grad(act, cotangent))
     grad_down_bias = jnp.sum(cot_float, axis=0)
     grad_pre = gelu_back(pre, contract(cotangent, whole_down, 1, 1))
     grad_pre_b = grad_pre.astype(bf16)
-    grad_up = weight_grad(second_act, grad_pre_b)
+    grad_up = total(weight_grad(second_act, grad_pre_b), grad_down)
     grad_up_bias = jnp.sum(grad_pre, axis=0)
     grad_second = contract(grad_pre_b, whole_up, 1, 1)
     grad_second_gain = jnp.sum(grad_second * second_hat, axis=0)
     grad_second_shift = jnp.sum(grad_second, axis=0)
     grad_mid = cot_float + normalize_back(grad_second, second_hat, second_rstd, gain_two)
     grad_mid_b = grad_mid.astype(bf16)
-    grad_out = weight_grad(joined, grad_mid_b)
+    grad_out = total(weight_grad(joined, grad_mid_b), grad_up)
     grad_out_bias = jnp.sum(grad_mid, axis=0)
     grad_attended = contract(grad_mid_b, whole_out, 1, 1).astype(bf16)
     grad_query, grad_keys, grad_values = attention_back(grad_attended)
@@ -439,10 +491,15 @@
         grad_first_gain, grad_first_shift, grad_query_bias, grad_value_bias, grad_out_bias,
         grad_second_gain, grad_second_shift, grad_down_bias, grad_up_bias,
     )
-    summed = lax.psum(
-        jnp.concatenate([part.reshape(fsdp, -1) for part in vectors], axis=1), ("fsdp", "ctx")
-    )
-    mine = lax.dynamic_index_in_dim(summed, place, 0, keepdims=False)
+    packed_vectors = jnp.concatenate([part.reshape(fsdp, -1) for part in vectors], axis=1)
+    mine = lax.dynamic_index_in_dim(packed_vectors, place, 0, keepdims=False)
+    if paired:
+        sent = lax.dynamic_index_in_dim(packed_vectors, 1 - place, 0, keepdims=False)
+        mine = mine + other_half(sent)
+    else:
+        mine = lax.psum_scatter(packed_vectors, "fsdp", scatter_dimension=0, tiled=True)[0]
+    grad_qkv, mine = total((grad_qkv, mine.astype(bf16)), grad_out)
+    mine = mine.astype(f32)
     shards, at = [], 0
     for size in sizes:
         shards.append(mine[at : at + size])

time: 854 us -> 749 us (0.88)
  waiting for transfers between devices: 574 us -> 424 us
  local copies, waits for them, and re-layouts: 23.8 us -> 62 us
  other arithmetic: 22.7 us -> 48.7 us
  blocking collectives: 93.9 us -> 78 us
    all_gather x6 -> x0, waiting for transfers between devices: 296 us -> none  [the longest x4 296 us: on_device(): lax.all_gather(part, 'fsdp', axis=0, tiled=True)]
    ppermute x0 -> x25, waiting for transfers between devices: none -> 133 us  [the longest x13 78.4 us: other_half(): return lax.ppermute(value, 'fsdp', [(0, 1), (1, 0)])]
    psum x1 -> x4, waiting for transfers between devices: 205 us -> 270 us  [total(): return lax.psum(value, 'ctx')]
    all_gather x2 -> x0, blocking collectives: 45.7 us -> none  [right(): return lax.all_gather(part, 'fsdp', axis=0, tiled=True)]
    all_to_all x4, waiting for transfers between devices: 63.1 us -> 21.3 us  [swap(): lax.all_to_all(blocks_of, axis, split_axis=0, concat_axis=0, tiled=True)]
    dynamic_update_slice x0 -> x16, local copies, waits for them, and re-layouts: none -> 23.2 us  [gather_weights(): lax.dynamic_update_slice_in_dim(whole, got, base + (quarter ^ bits), 0)]
    concatenate x0 -> x4, other arithmetic: none -> 22.2 us  [gather_weights(): whole = jnp.concatenate([parts, parts], axis=0)]
    ppermute x0 -> x25, starting transfers between devices: none -> 21.4 us  [the longest x13 15 us: other_half(): return lax.ppermute(value, 'fsdp', [(0, 1), (1, 0)])]
  transfers between devices with their start and end apart: 15 -> 33, of which waited for: 10 -> 17; matrix products, arithmetic and copies ran while one was open for 7% -> 21% of each run, Pallas kernels for 1% -> 2%
where the time goes in v2:
time: 749 us; the launch traced here: 741 us
  waiting for transfers between devices  424 us (57%)
  blocking collectives  78 us (10%)
  local copies, waits for them, and re-layouts  62 us (8%)
  matrix products  55.9 us (7%)
  other arithmetic  48.7 us (7%)
  starting transfers between devices  42.2 us (6%)
  Pallas kernels  14.9 us (2%)
  between operations  14.9 us (2%)
    psum x4, waiting for transfers between devices, total(): return lax.psum(value, 'ctx')  270 us
    ppermute x13, waiting for transfers between devices, other_half(): return lax.ppermute(value, 'fsdp', [(0, 1), (1, 0)])  78.4 us
    psum x1, blocking collectives, total(): return lax.psum(value, 'ctx')  58.7 us
    ppermute x12, waiting for transfers between devices, partner(): lax.ppermute(value, 'ctx', [(source, source ^ bit) for source in range(co...  54.7 us
    dot_general x8, matrix products, contract(): lax.dot_general(left, right, (((left_dim,), (right_dim,)), ((), ())), pre...  33.1 us
    dynamic_update_slice x16, local copies, waits for them, and re-layouts, gather_weights(): lax.dynamic_update_slice_in_dim(whole, got, base + (quarter ^ bits), 0)  23.2 us
    concatenate x4, other arithmetic, gather_weights(): whole = jnp.concatenate([parts, parts], axis=0)  22.2 us
    all_to_all x4, waiting for transfers between devices, swap(): lax.all_to_all(blocks_of, axis, split_axis=0, concat_axis=0, tiled=True)  21.3 us
  transfers between devices with their start and end apart: 33, of which 17 were waited for; matrix products, arithmetic and copies ran while one was open for 21% of the time, Pallas kernels for 2%

profile of v2, /device:TPU:0, one launch (start us, length us, event | category | flops | bytes accessed | tf_op | source)
XLA Modules:
  0.0 740.8 jit_solution(14284852595802775445)
XLA Ops:
  7.2 3.0 collective-permute-start.24
  11.6 6.2 concatenate.61
  17.8 19.2 %all-gather.1 = bf16[2,1,6528]{2,1,0:T(2,128)(2,1)S(1)} all-gather(bf16[1,1,6528]{2,1,0:T(2,128)(2,1)S(1)} %reshape.273), channel_id=2, replica_groups=mesh['fsdp'=2,'ctx'=16] {'fsdp'}, dimensions={0}, use_global_device_ids=true | all-gather | bytes 39168 | tf_op jit(solution)/shard_map/all_gather | solution.py:415
  37.2 6.9 pad_maximum_fusion.2
  44.6 2.4 constant_dynamic-slice_fusion.7
  46.9 8.2 %copy.57 = bf16[2176,1088]{1,0:T(8,128)(2,1)} copy(bf16[2176,1088]{0,1:T(8,128)(2,1)} %param.28) | data formatting | bytes 9469952 | tf_op args[13]
  55.2 10.6 %pad_maximum_fusion = bf16[8,544,1088]{2,1,0:T(8,128)(2,1)} fusion(bf16[4,544,1088]{2,1,0:T(8,128)(2,1)} %bitcast.70), kind=kLoop, calls=%fused_computation.1 | loop fusion | flops 4734976 | bytes 14204928 | tf_op jit(solution)/shard_map/concatenate | solution.py:380
  66.9 4.5 pad_maximum_fusion.1
  72.4 1.7 collective-permute-start.4
  74.9 2.6 constant_dynamic-slice_fusion.6
  77.5 1.5 collective-permute-start.1
  79.0 2.3 collective-permute-done.4
  84.7 22.0 %collective-permute-done.5 = bf16[1,136,1088]{2,1,0:T(8,128)(2,1)S(1)} collective-permute-done((bf16[1,136,1088]{2,1,0:T(8,128)(2,1)}, bf16[1,136,1088]{2,1,0:T(8,128)(2,1)S(1)}, u32[]{:S(2)}, u32[]{:S(2)}) %collective-permute-start.5) | collective-permute-done | bytes 295968 | tf_op jit(solution)/shard_map/ppermute | solution.py:358
  110.4 25.0 %collective-permute-done.8 = bf16[1,136,4352]{2,1,0:T(8,128)(2,1)} collective-permute-done((bf16[1,136,4352]{2,1,0:T(8,128)(2,1)S(1)}, bf16[1,136,4352]{2,1,0:T(8,128)(2,1)}, u32[]{:S(2)}, u32[]{:S(2)}) %collective-permute-start.8) | collective-permute-done | bytes 1183776 | tf_op jit(solution)/shard_map/ppermute | solution.py:353
  135.7 1.7 collective-permute-start.9
  138.4 6.1 fusion.61
  146.5 5.5 all-to-all-start
  152.0 2.4 constant_dynamic-update-slice_fusion.12
  154.4 10.5 %collective-permute-done.12 = bf16[1,544,1088]{2,1,0:T(8,128)(2,1)} collective-permute-done((bf16[1,544,1088]{2,1,0:T(8,128)(2,1)}, bf16[1,544,1088]{2,1,0:T(8,128)(2,1)}, u32[]{:S(2)}, u32[]{:S(2)}) %collective-permute-start.12) | collective-permute-done | bytes 1183776 | tf_op jit(solution)/shard_map/ppermute | solution.py:353
  164.9 1.5 collective-permute-start.13
  166.4 6.5 collective-permute-done.9
  172.9 2.4 constant_dynamic-update-slice_fusion.11
  175.2 2.5 constant_dynamic-update-slice_fusion.8
  177.7 2.4 constant_dynamic-update-slice_fusion.10
  180.1 25.3 %collective-permute-done.13 = bf16[1,544,1088]{2,1,0:T(8,128)(2,1)} collective-permute-done((bf16[1,544,1088]{2,1,0:T(8,128)(2,1)}, bf16[1,544,1088]{2,1,0:T(8,128)(2,1)}, u32[]{:S(2)}, u32[]{:S(2)}) %collective-permute-start.13) | collective-permute-done | bytes 1183776 | tf_op jit(solution)/shard_map/ppermute | solution.py:358
  205.4 2.5 constant_dynamic-update-slice_fusion.7
  209.9 7.0 attend.1
  217.8 6.2 all-to-all-start.1
  224.3 2.4 constant_dynamic-update-slice_fusion.9
  226.8 7.4 all-to-all-done.1
  234.1 3.0 fusion.62
  237.6 6.0 multiply_convert_fusion
  245.3 2.6 constant_dynamic-update-slice_fusion.5
  247.9 8.7 %fusion.56 = (f32[4352]{0:T(1024)S(1)}, bf16[128,4352]{1,0:T(8,128)(2,1)S(1)}) fusion(f32[128,4352]{1,0:T(8,128)S(1)} %get-tuple-element.96, bf16[4352,1088]{1,0:T(8,128)(2,1)} %bitcast.18, bf16[128,1088]{0,1:T(8,128)(2,1)S(1)} %copy-done.22), kind=kOutput, calls=%fused_computation.148 | convolution fusion | flops 1223847680 | bytes 13108224 | tf_op jit(solution)/shard_map/dot_general | solution.py:55
  256.7 3.5 multiply_reduce_fusion
  260.2 4.6 convolution_convert_fusion
  264.8 1.8 fusion.55
  269.4 1.8 copy.59
  271.2 4.2 all-to-all-start.2
  276.2 13.9 %all-to-all-done.2 = bf16[16,128,64]{1,2,0:T(8,128)(2,1)} async-done(((bf16[16,128,64]{1,2,0:T(8,128)(2,1)}), bf16[16,128,64]{1,2,0:T(8,128)(2,1)}, u32[]{:S(2)}, u32[]{:S(2)}) %all-to-all-start.2) | async-done | bytes 262176 | tf_op jit(solution)/shard_map/all_to_all | solution.py:202
  291.3 7.9 %attend_back.1 = (bf16[2048,320]{1,0:T(8,128)(2,1)S(1)}, bf16[128,64]{1,0:T(8,128)(2,1)S(1)}) custom-call(s32[1]{0:T(128)} %bitcast.place_ref, bf16[2048,320]{1,0:T(8,128)(2,1)S(1)} %bitcast.60, bf16[128,64]{1,0:T(8,128)(2,1)S(1)} %slice.151.extra_ref, bf16[64,2048]{1,0:T(8,128)(2,1)S(1)} %get-tuple-element.35.outt_ref, ...), custom_call_target="tpu_custom_call" | custom-call | tf_op jit(solution)/shard_map/attend_back/pallas_call | solution.py:184
  300.3 2.7 copy.61
  303.0 4.4 all-to-all-start.3
  309.7 27.6 %collective-permute-done.21 = bf16[128,544]{0,1:T(8,128)(2,1)S(1)} collective-permute-done((bf16[128,544]{0,1:T(8,128)(2,1)S(1)}, bf16[128,544]{0,1:T(8,128)(2,1)S(1)}, u32[]{:S(2)}, u32[]{:S(2)}) %collective-permute-start.21) | collective-permute-done | bytes 139296 | tf_op jit(solution)/shard_map/ppermute | solution.py:353
  337.2 4.8 convolution_convert_fusion.1
  342.1 55.7 %all-reduce.5.cloned.1.call-done = bf16[2176,1088]{0,1:T(8,128)(2,1)} async-done(((bf16[2176,1088]{0,1:T(8,128)(2,1)}), bf16[2176,1088]{0,1:T(8,128)(2,1)}) %all-reduce.5.cloned.1.call-update) | async-done | bytes 4734992 | tf_op jit(solution)/shard_map/psum | solution.py:464
  397.9 1.5 collective-permute-start.20
  401.0 8.3 %collective-permute-done.19 = bf16[128,544]{0,1:T(8,128)(2,1)S(1)} collective-permute-done((bf16[128,544]{0,1:T(8,128)(2,1)S(1)}, bf16[128,544]{0,1:T(8,128)(2,1)S(1)}, u32[]{:S(2)}, u32[]{:S(2)}) %collective-permute-start.19) | collective-permute-done | bytes 139296 | tf_op jit(solution)/shard_map/ppermute | solution.py:353
  409.2 1.6 convolution_convert_fusion.3
  413.4 1.5 collective-permute-start.17
  414.9 105.3 %all-reduce.7.cloned.1.call-done = bf16[544,4352]{1,0:T(8,128)(2,1)} async-done(((bf16[544,4352]{1,0:T(8,128)(2,1)}), bf16[544,4352]{1,0:T(8,128)(2,1)}) %all-reduce.7.cloned.1.call-update) | async-done | bytes 4734992 | tf_op jit(solution)/shard_map/psum | solution.py:464
  520.5 5.9 fusion.29
  527.4 1.5 collective-permute-start.18
  529.7 2.0 collective-permute-done.18
  531.7 2.7 collective-permute-done.16
  534.4 3.0 convolution_convert_fusion.2
  537.3 80.7 %all-reduce.9.cloned.1.call-done = bf16[544,1088]{1,0:T(8,128)(2,1)} async-done(((bf16[544,1088]{1,0:T(8,128)(2,1)}), bf16[544,1088]{1,0:T(8,128)(2,1)}) %all-reduce.9.cloned.1.call-update) | async-done | bytes 1183760 | tf_op jit(solution)/shard_map/psum | solution.py:464
  618.1 7.7 %fusion.1 = f32[128,1088]{0,1:T(8,128)} fusion(f32[128,1088]{0,1:T(8,128)S(1)} %get-tuple-element.94, bf16[128,4352]{1,0:T(8,128)(2,1)S(1)} %copy-done.4, bf16[4352,1088]{1,0:T(8,128)(2,1)} %bitcast.18, f32[1088]{0:T(1024)S(1)} %reshape.271), kind=kOutput, calls=%fused_computation.15 | convolution fusion | flops 1212432384 | bytes 11702528 | tf_op jit(solution)/shard_map/dot_general | solution.py:443
  625.8 7.2 convert_element_type.198
  634.1 4.5 convert_element_type.197
  638.5 58.7 %psum.38 = bf16[6528]{0:T(1024)(128)(2,1)S(1)} all-reduce(bf16[6528]{0:T(1024)(128)(2,1)S(1)} %add_convert_fusion.2), channel_id=1, replica_groups=mesh['fsdp'=2,'ctx'=16] {'ctx'}, use_global_device_ids=true, to_apply=%region_21.22 | all-reduce | flops 6528 | bytes 26112 | tf_op jit(solution)/shard_map/psum | solution.py:464
  697.9 1.6 convert_element_type.196
  700.2 28.1 %all-reduce.11.cloned.1.call-done = bf16[544,3264]{1,0:T(8,128)(2,1)} async-done(((bf16[544,3264]{1,0:T(8,128)(2,1)}), bf16[544,3264]{1,0:T(8,128)(2,1)}) %all-reduce.11.cloned.1.call-update) | async-done | bytes 3551248 | tf_op jit(solution)/shard_map/psum | solution.py:464
  728.3 5.6 convert_element_type.195
  (199 shorter events, 37.0 us)
Async XLA Ops:
  7.2 253.0 %collective-permute-start.24 = (bf16[128,1088]{0,1:T(8,128)(2,1)}, bf16[128,1088]{0,1:T(8,128)(2,1)}, u32[]{:S(2)}, u32[]{:S(2)}) collective-permute-start(bf16[128,1088]{0,1:T(8,128)(2,1)} %param.16), channel_id=1, source_target_pairs={{0,16},{16,0},{1,17},{17,1},{2,18},{18,2},{3,19},{19,3},{4,20},{20... | collective-permute-start | bytes 835592 | tf_op jit(solution)/shard_map/ppermute | solution.py:353
  11.4 60.0 %collective-permute-start = (bf16[1,136,3264]{2,1,0:T(8,128)(2,1)S(1)}, bf16[1,136,3264]{2,1,0:T(8,128)(2,1)S(1)}, u32[]{:S(2)}, u32[]{:S(2)}) collective-permute-start(bf16[1,136,3264]{2,1,0:T(8,128)(2,1)S(1)} %constant_dynamic-slice_fusion.9), channel_id=1, source_target_pairs={{0,16},{16,0},{1,17},{17,1},{2,18},{18,2},{3,19},{19,3},{4,20},{20... | collective-permute-start | bytes 2663432 | tf_op jit(solution)/shard_map/ppermute | solution.py:353
  37.2 6.9 copy-start.7
  55.2 11.8 %slice-start.3 = ((s8[4734976]{0:T(1024)(128)(4,1)}), s8[4194304]{0:T(1024)(128)(4,1)S(1)}, s32[]{:S(2)}) async-start(s8[4734976]{0:T(1024)(128)(4,1)} %bitcast.75), calls=%async_computation.11 | async-start | bytes 8388608
  55.2 11.0 %copy-start.16 = (bf16[544,1088]{1,0:T(8,128)(2,1)S(1)}, bf16[544,1088]{1,0:T(8,128)(2,1)}, u32[]{:S(2)}) copy-start(bf16[544,1088]{1,0:T(8,128)(2,1)} %param.22) | copy-start | bytes 3551236
  55.2 11.8 %slice-start.4 = ((s8[4734976]{0:T(1024)(128)(4,1)}), s8[540672]{0:T(1024)(128)(4,1)S(1)}, s32[]{:S(2)}) async-start(s8[4734976]{0:T(1024)(128)(4,1)} %bitcast.75), calls=%async_computation.12 | async-start | bytes 1081344
  66.1 72.3 %copy-start.12 = (bf16[128,1088]{0,1:T(8,128)(2,1)}, bf16[128,1088]{0,1:T(8,128)(2,1)S(1)}, u32[]{:S(2)}) copy-start(bf16[128,1088]{0,1:T(8,128)(2,1)S(1)} %fusion.24) | copy-start | bytes 835588
  71.4 1.0 copy-start.23
  72.4 8.9 %collective-permute-start.4 = (bf16[1,136,1088]{2,1,0:T(8,128)(2,1)}, bf16[1,136,1088]{2,1,0:T(8,128)(2,1)}, u32[]{:S(2)}, u32[]{:S(2)}) collective-permute-start(bf16[1,136,1088]{2,1,0:T(8,128)(2,1)} %constant_dynamic-slice_fusion.8), channel_id=1, source_target_pairs={{0,16},{16,0},{1,17},{17,1},{2,18},{18,2},{3,19},{19,3},{4,20},{20... | collective-permute-start | bytes 887816 | tf_op jit(solution)/shard_map/ppermute | solution.py:353
  74.9 2.6 copy-start.24
  74.9 31.9 %copy-start.18 = (bf16[1,136,4352]{2,1,0:T(8,128)(2,1)S(1)}, bf16[1,136,4352]{2,1,0:T(8,128)(2,1)}, u32[]{:S(2)}) copy-start(bf16[1,136,4352]{2,1,0:T(8,128)(2,1)} %constant_dynamic-slice_fusion.7) | copy-start | bytes 3551236
  77.5 31.9 %collective-permute-start.2 = (bf16[1,136,3264]{2,1,0:T(8,128)(2,1)S(1)}, bf16[1,136,3264]{2,1,0:T(8,128)(2,1)S(1)}, u32[]{:S(2)}, u32[]{:S(2)}) collective-permute-start(bf16[1,136,3264]{2,1,0:T(8,128)(2,1)S(1)} %copy-done.24), channel_id=1, source_target_pairs={{0,1},{1,0},{2,3},{3,2},{4,5},{5,4},{6,7},{7,6},{8,9},{9,8},{10,11... | collective-permute-start | bytes 2663432 | tf_op jit(solution)/shard_map/ppermute | solution.py:358
  77.5 29.7 %collective-permute-start.1 = (bf16[1,136,3264]{2,1,0:T(8,128)(2,1)S(1)}, bf16[1,136,3264]{2,1,0:T(8,128)(2,1)S(1)}, u32[]{:S(2)}, u32[]{:S(2)}) collective-permute-start(bf16[1,136,3264]{2,1,0:T(8,128)(2,1)S(1)} %copy-done.24), channel_id=1, source_target_pairs={{0,2},{1,3},{2,0},{3,1},{4,6},{5,7},{6,4},{7,5},{8,10},{9,11},{10,... | collective-permute-start | bytes 2663432 | tf_op jit(solution)/shard_map/ppermute | solution.py:358
  81.3 25.4 %collective-permute-start.5 = (bf16[1,136,1088]{2,1,0:T(8,128)(2,1)}, bf16[1,136,1088]{2,1,0:T(8,128)(2,1)S(1)}, u32[]{:S(2)}, u32[]{:S(2)}) collective-permute-start(bf16[1,136,1088]{2,1,0:T(8,128)(2,1)} %collective-permute-done.4), channel_id=1, source_target_pairs={{0,2},{1,3},{2,0},{3,1},{4,6},{5,7},{6,4},{7,5},{8,10},{9,11},{10,... | collective-permute-start | bytes 887816 | tf_op jit(solution)/shard_map/ppermute | solution.py:358
  83.7 23.1 %collective-permute-start.6 = (bf16[1,136,1088]{2,1,0:T(8,128)(2,1)}, bf16[1,136,1088]{2,1,0:T(8,128)(2,1)S(1)}, u32[]{:S(2)}, u32[]{:S(2)}) collective-permute-start(bf16[1,136,1088]{2,1,0:T(8,128)(2,1)} %collective-permute-done.4), channel_id=1, source_target_pairs={{0,1},{1,0},{2,3},{3,2},{4,5},{5,4},{6,7},{7,6},{8,9},{9,8},{10,11... | collective-permute-start | bytes 887816 | tf_op jit(solution)/shard_map/ppermute | solution.py:358
  106.7 1.6 collective-permute-start.7
  106.8 28.6 %collective-permute-start.8 = (bf16[1,136,4352]{2,1,0:T(8,128)(2,1)S(1)}, bf16[1,136,4352]{2,1,0:T(8,128)(2,1)}, u32[]{:S(2)}, u32[]{:S(2)}) collective-permute-start(bf16[1,136,4352]{2,1,0:T(8,128)(2,1)S(1)} %copy-done.18), channel_id=1, source_target_pairs={{0,16},{16,0},{1,17},{17,1},{2,18},{18,2},{3,19},{19,3},{4,20},{20... | collective-permute-start | bytes 3551240 | tf_op jit(solution)/shard_map/ppermute | solution.py:353
  107.2 30.2 %collective-permute-start.3 = (bf16[1,136,3264]{2,1,0:T(8,128)(2,1)S(1)}, bf16[1,136,3264]{2,1,0:T(8,128)(2,1)S(1)}, u32[]{:S(2)}, u32[]{:S(2)}) collective-permute-start(bf16[1,136,3264]{2,1,0:T(8,128)(2,1)S(1)} %collective-permute-done.1), channel_id=1, source_target_pairs={{0,1},{1,0},{2,3},{3,2},{4,5},{5,4},{6,7},{7,6},{8,9},{9,8},{10,11... | collective-permute-start | bytes 2663432 | tf_op jit(solution)/shard_map/ppermute | solution.py:358
  108.4 30.0 %copy-start.1 = (bf16[8,136,1088]{2,1,0:T(8,128)(2,1)}, bf16[8,136,1088]{2,1,0:T(8,128)(2,1)S(1)}, u32[]{:S(2)}) copy-start(bf16[8,136,1088]{2,1,0:T(8,128)(2,1)S(1)} %constant_dynamic-update-slice_fusion.13) | copy-start | bytes 7102468
  135.4 29.5 %collective-permute-start.12 = (bf16[1,544,1088]{2,1,0:T(8,128)(2,1)}, bf16[1,544,1088]{2,1,0:T(8,128)(2,1)}, u32[]{:S(2)}, u32[]{:S(2)}) collective-permute-start(bf16[1,544,1088]{2,1,0:T(8,128)(2,1)} %constant_dynamic-slice_fusion.6), channel_id=1, source_target_pairs={{0,16},{16,0},{1,17},{17,1},{2,18},{18,2},{3,19},{19,3},{4,20},{20... | collective-permute-start | bytes 3551240 | tf_op jit(solution)/shard_map/ppermute | solution.py:353
  135.7 42.0 %collective-permute-start.10 = (bf16[1,136,4352]{2,1,0:T(8,128)(2,1)}, bf16[1,136,4352]{2,1,0:T(8,128)(2,1)}, u32[]{:S(2)}, u32[]{:S(2)}) collective-permute-start(bf16[1,136,4352]{2,1,0:T(8,128)(2,1)} %collective-permute-done.8), channel_id=1, source_target_pairs={{0,1},{1,0},{2,3},{3,2},{4,5},{5,4},{6,7},{7,6},{8,9},{9,8},{10,11... | collective-permute-start | bytes 3551240 | tf_op jit(solution)/shard_map/ppermute | solution.py:358
  135.7 37.2 %collective-permute-start.9 = (bf16[1,136,4352]{2,1,0:T(8,128)(2,1)}, bf16[1,136,4352]{2,1,0:T(8,128)(2,1)}, u32[]{:S(2)}, u32[]{:S(2)}) collective-permute-start(bf16[1,136,4352]{2,1,0:T(8,128)(2,1)} %collective-permute-done.8), channel_id=1, source_target_pairs={{0,2},{1,3},{2,0},{3,1},{4,6},{5,7},{6,4},{7,5},{8,10},{9,11},{10,... | collective-permute-start | bytes 3551240 | tf_op jit(solution)/shard_map/ppermute | solution.py:358
  146.5 62.5 %all-to-all-start = ((bf16[16,128,320]{1,2,0:T(8,128)(2,1)}), bf16[16,128,320]{1,2,0:T(8,128)(2,1)S(1)}, u32[]{:S(2)}, u32[]{:S(2)}) async-start(bf16[16,128,320]{1,2,0:T(8,128)(2,1)} %pad_maximum_fusion.4), calls=%async_computation | async-start | bytes 2621440 | tf_op jit(solution)/shard_map/all_to_all | solution.py:202
  164.9 43.0 %collective-permute-start.14 = (bf16[1,544,1088]{2,1,0:T(8,128)(2,1)}, bf16[1,544,1088]{2,1,0:T(8,128)(2,1)S(1)}, u32[]{:S(2)}, u32[]{:S(2)}) collective-permute-start(bf16[1,544,1088]{2,1,0:T(8,128)(2,1)} %collective-permute-done.12), channel_id=1, source_target_pairs={{0,1},{1,0},{2,3},{3,2},{4,5},{5,4},{6,7},{7,6},{8,9},{9,8},{10,11... | collective-permute-start | bytes 3551240 | tf_op jit(solution)/shard_map/ppermute | solution.py:358
  164.9 40.5 %collective-permute-start.13 = (bf16[1,544,1088]{2,1,0:T(8,128)(2,1)}, bf16[1,544,1088]{2,1,0:T(8,128)(2,1)}, u32[]{:S(2)}, u32[]{:S(2)}) collective-permute-start(bf16[1,544,1088]{2,1,0:T(8,128)(2,1)} %collective-permute-done.12), channel_id=1, source_target_pairs={{0,2},{1,3},{2,0},{3,1},{4,6},{5,7},{6,4},{7,5},{8,10},{9,11},{10,... | collective-permute-start | bytes 3551240 | tf_op jit(solution)/shard_map/ppermute | solution.py:358
  172.9 51.4 %collective-permute-start.11 = (bf16[1,136,4352]{2,1,0:T(8,128)(2,1)}, bf16[1,136,4352]{2,1,0:T(8,128)(2,1)}, u32[]{:S(2)}, u32[]{:S(2)}) collective-permute-start(bf16[1,136,4352]{2,1,0:T(8,128)(2,1)} %collective-permute-done.9), channel_id=1, source_target_pairs={{0,1},{1,0},{2,3},{3,2},{4,5},{5,4},{6,7},{7,6},{8,9},{9,8},{10,11... | collective-permute-start | bytes 3551240 | tf_op jit(solution)/shard_map/ppermute | solution.py:358
  205.4 39.9 %collective-permute-start.15 = (bf16[1,544,1088]{2,1,0:T(8,128)(2,1)}, bf16[1,544,1088]{2,1,0:T(8,128)(2,1)}, u32[]{:S(2)}, u32[]{:S(2)}) collective-permute-start(bf16[1,544,1088]{2,1,0:T(8,128)(2,1)} %collective-permute-done.13), channel_id=1, source_target_pairs={{0,1},{1,0},{2,3},{3,2},{4,5},{5,4},{6,7},{7,6},{8,9},{9,8},{10,11... | collective-permute-start | bytes 3551240 | tf_op jit(solution)/shard_map/ppermute | solution.py:358
  217.8 16.3 %all-to-all-start.1 = ((bf16[16,128,64]{1,2,0:T(8,128)(2,1)}), bf16[16,128,64]{1,2,0:T(8,128)(2,1)S(1)}, u32[]{:S(2)}, u32[]{:S(2)}) async-start(bf16[16,128,64]{1,2,0:T(8,128)(2,1)} %copy.55), calls=%async_computation.1 | async-start | bytes 524288 | tf_op jit(solution)/shard_map/all_to_all | solution.py:202
  224.1 173.8 %all-reduce.5.cloned.1.call-start = ((), (), s32[]{:S(2)}) async-start(), calls=%async_computation.4 | async-start | bytes 9469952 | tf_op jit(solution)/shard_map/psum | solution.py:464
  234.1 3.1 copy-start.14
  237.6 6.0 copy-start.10
  243.7 1.6 copy-start.3
  243.7 4.2 copy-start.22
  243.9 16.3 %collective-permute-start.23 = (bf16[128,2176]{1,0:T(8,128)(2,1)S(1)}, bf16[128,2176]{1,0:T(8,128)(2,1)S(1)}, u32[]{:S(2)}, u32[]{:S(2)}) collective-permute-start(bf16[128,2176]{1,0:T(8,128)(2,1)S(1)} %get-tuple-element.65), channel_id=1, source_target_pairs={{0,16},{16,0},{1,17},{17,1},{2,18},{18,2},{3,19},{19,3},{4,20},{20... | collective-permute-start | bytes 1671176 | tf_op jit(solution)/shard_map/ppermute | solution.py:353
  245.3 11.3 %slice-start = ((s8[9469952]{0:T(1024)(128)(4,1)}), s8[4194304]{0:T(1024)(128)(4,1)S(1)}, s32[]{:S(2)}) async-start(s8[9469952]{0:T(1024)(128)(4,1)} %bitcast.65), calls=%async_computation.8 | async-start | bytes 8388608
  247.9 8.8 %slice-start.1 = ((s8[9469952]{0:T(1024)(128)(4,1)}), s8[4194304]{0:T(1024)(128)(4,1)S(1)}, s32[]{:S(2)}) async-start(s8[9469952]{0:T(1024)(128)(4,1)} %bitcast.65), calls=%async_computation.9 | async-start | bytes 8388608
  247.9 8.8 %slice-start.2 = ((s8[9469952]{0:T(1024)(128)(4,1)}), s8[1081344]{0:T(1024)(128)(4,1)S(1)}, s32[]{:S(2)}) async-start(s8[9469952]{0:T(1024)(128)(4,1)} %bitcast.65), calls=%async_computation.10 | async-start | bytes 2162688
  256.6 3.5 copy-start.5
  264.8 2.0 copy-start.2
  266.6 4.6 copy-start.8
  271.2 18.9 %all-to-all-start.2 = ((bf16[16,128,64]{1,2,0:T(8,128)(2,1)}), bf16[16,128,64]{1,2,0:T(8,128)(2,1)}, u32[]{:S(2)}, u32[]{:S(2)}) async-start(bf16[16,128,64]{1,2,0:T(8,128)(2,1)} %bitcast.93), calls=%async_computation.2 | async-start | bytes 524288 | tf_op jit(solution)/shard_map/all_to_all | solution.py:202
  299.2 1.1 copy-start
  300.3 7.1 copy-start.6
  300.3 8.1 %copy-start.11 = (bf16[128,1088]{0,1:T(8,128)(2,1)S(1)}, bf16[128,1088]{0,1:T(8,128)(2,1)}, u32[]{:S(2)}) copy-start(bf16[128,1088]{0,1:T(8,128)(2,1)} %copy-done.10) | copy-start | bytes 835588
  303.0 107.9 %all-to-all-start.3 = ((bf16[16,128,320]{1,2,0:T(8,128)(2,1)}), bf16[16,128,320]{1,2,0:T(8,128)(2,1)}, u32[]{:S(2)}, u32[]{:S(2)}) async-start(bf16[16,128,320]{1,2,0:T(8,128)(2,1)} %copy.61), calls=%async_computation.3 | async-start | bytes 2621440 | tf_op jit(solution)/shard_map/all_to_all | solution.py:202
  307.4 212.8 %all-reduce.7.cloned.1.call-start = ((), (), s32[]{:S(2)}) async-start(), calls=%async_computation.5 | async-start | bytes 9469952 | tf_op jit(solution)/shard_map/psum | solution.py:464
  307.5 29.8 %collective-permute-start.22 = (bf16[128,4352]{1,0:T(8,128)(2,1)S(1)}, bf16[128,4352]{1,0:T(8,128)(2,1)}, u32[]{:S(2)}, u32[]{:S(2)}) collective-permute-start(bf16[128,4352]{1,0:T(8,128)(2,1)S(1)} %copy-done.6), channel_id=1, source_target_pairs={{0,16},{16,0},{1,17},{17,1},{2,18},{18,2},{3,19},{19,3},{4,20},{20... | collective-permute-start | bytes 3342344 | tf_op jit(solution)/shard_map/ppermute | solution.py:353
  308.5 28.8 %collective-permute-start.21 = (bf16[128,544]{0,1:T(8,128)(2,1)S(1)}, bf16[128,544]{0,1:T(8,128)(2,1)S(1)}, u32[]{:S(2)}, u32[]{:S(2)}) collective-permute-start(bf16[128,544]{0,1:T(8,128)(2,1)S(1)} %get-tuple-element.67), channel_id=1, source_target_pairs={{0,16},{16,0},{1,17},{17,1},{2,18},{18,2},{3,19},{19,3},{4,20},{20... | collective-permute-start | bytes 417800 | tf_op jit(solution)/shard_map/ppermute | solution.py:353
  342.1 55.8 %copy-start.21 = (bf16[128,1088]{0,1:T(8,128)(2,1)S(1)}, bf16[128,1088]{0,1:T(8,128)(2,1)}, u32[]{:S(2)}) copy-start(bf16[128,1088]{0,1:T(8,128)(2,1)} %copy-done.20) | copy-start | bytes 835588
  342.1 57.4 %copy-start.15 = (bf16[16,128,64]{1,2,0:T(8,128)(2,1)S(1)}, bf16[16,128,64]{1,2,0:T(8,128)(2,1)}, u32[]{:S(2)}) copy-start(bf16[16,128,64]{1,2,0:T(8,128)(2,1)} %copy-done.14) | copy-start | bytes 786436
  397.9 220.2 %all-reduce.9.cloned.1.call-start = ((), (), s32[]{:S(2)}) async-start(), calls=%async_computation.6 | async-start | bytes 2506752 | tf_op jit(solution)/shard_map/psum | solution.py:464
  397.9 11.3 %collective-permute-start.20 = (bf16[128,1088]{0,1:T(8,128)(2,1)S(1)}, bf16[128,1088]{0,1:T(8,128)(2,1)S(1)}, u32[]{:S(2)}, u32[]{:S(2)}) collective-permute-start(bf16[128,1088]{0,1:T(8,128)(2,1)S(1)} %copy-done.21), channel_id=1, source_target_pairs={{0,16},{16,0},{1,17},{17,1},{2,18},{18,2},{3,19},{19,3},{4,20},{20... | collective-permute-start | bytes 835592 | tf_op jit(solution)/shard_map/ppermute | solution.py:353
  400.0 9.2 %collective-permute-start.19 = (bf16[128,544]{0,1:T(8,128)(2,1)S(1)}, bf16[128,544]{0,1:T(8,128)(2,1)S(1)}, u32[]{:S(2)}, u32[]{:S(2)}) collective-permute-start(bf16[128,544]{0,1:T(8,128)(2,1)S(1)} %get-tuple-element.69), channel_id=1, source_target_pairs={{0,16},{16,0},{1,17},{17,1},{2,18},{18,2},{3,19},{19,3},{4,20},{20... | collective-permute-start | bytes 417800 | tf_op jit(solution)/shard_map/ppermute | solution.py:353
  413.4 121.0 %collective-permute-start.17 = (bf16[128,3264]{0,1:T(8,128)(2,1)S(1)}, bf16[128,3264]{0,1:T(8,128)(2,1)S(1)}, u32[]{:S(2)}, u32[]{:S(2)}) collective-permute-start(bf16[128,3264]{0,1:T(8,128)(2,1)S(1)} %get-tuple-element.74), channel_id=1, source_target_pairs={{0,16},{16,0},{1,17},{17,1},{2,18},{18,2},{3,19},{19,3},{4,20},{20... | collective-permute-start | bytes 2506760 | tf_op jit(solution)/shard_map/ppermute | solution.py:353
  520.2 8.7 %copy-start.13 = (bf16[128,1088]{0,1:T(8,128)(2,1)S(1)}, bf16[128,1088]{0,1:T(8,128)(2,1)}, u32[]{:S(2)}) copy-start(bf16[128,1088]{0,1:T(8,128)(2,1)} %copy-done.12) | copy-start | bytes 835588
  520.2 208.0 %all-reduce.11.cloned.1.call-start = ((), (), s32[]{:S(2)}) async-start(), calls=%async_computation.7 | async-start | bytes 7241728 | tf_op jit(solution)/shard_map/psum | solution.py:464
  527.4 4.2 collective-permute-start.18
  529.0 5.4 collective-permute-start.16
  537.3 80.7 %copy-start.4 = (bf16[128,4352]{1,0:T(8,128)(2,1)S(1)}, bf16[128,4352]{1,0:T(8,128)(2,1)}, u32[]{:S(2)}) copy-start(bf16[128,4352]{1,0:T(8,128)(2,1)} %copy-done.3) | copy-start | bytes 3342340
  618.1 16.0 %slice-start.5 = ((s8[4734976]{0:T(1024)(128)(4,1)}), s8[540672]{0:T(1024)(128)(4,1)S(1)}, s32[]{:S(2)}) async-start(s8[4734976]{0:T(1024)(128)(4,1)} %bitcast.80), calls=%async_computation.13 | async-start | bytes 1081344
  625.8 7.2 copy-start.9
  625.8 7.2 copy-start.25
  625.8 8.3 %slice-start.6 = ((s8[4734976]{0:T(1024)(128)(4,1)}), s8[4194304]{0:T(1024)(128)(4,1)S(1)}, s32[]{:S(2)}) async-start(s8[4734976]{0:T(1024)(128)(4,1)} %bitcast.80), calls=%async_computation.14 | async-start | bytes 8388608
  634.1 63.8 %copy-start.17 = (bf16[544,1088]{1,0:T(8,128)(2,1)S(1)}, bf16[544,1088]{1,0:T(8,128)(2,1)}, u32[]{:S(2)}) copy-start(bf16[544,1088]{1,0:T(8,128)(2,1)} %all-reduce.9.cloned.1.call-done) | copy-start | bytes 3551236
  (2 other events, 1.7 us)
Sparse Core Ops, SparseCore 0:
  264.9 132.8 all-reduce.4
  402.5 117.6 all-reduce.6
  524.3 93.7 all-reduce.8
  622.2 106.0 all-reduce.10

commit v3 on v1

--- a/solution.py
+++ b/solution.py
@@ -1,3 +1,5 @@
+import functools
+
 import jax
 import jax.numpy as jnp
 from jax import lax
@@ -347,6 +349,108 @@
         )
 
     return attended.reshape(count_rows, width), backward
+
+
+def other_half(value):
+    return lax.ppermute(value, "fsdp", [(0, 1), (1, 0)])
+
+
+def spans(columns, pieces):
+    tiles = -(-columns // 128)
+    step = -(-tiles // pieces) * 128
+    return [(at, min(step, columns - at)) for at in range(0, columns, step)]
+
+
+def gather_kernel(plan, *refs):
+    count = len(plan)
+    shards, wholes = refs[:count], refs[count : 2 * count]
+    own_sem, send_sem, recv_sem = refs[2 * count :]
+    place, spot = lax.axis_index("fsdp"), lax.axis_index("ctx")
+    quarter = lax.rem(spot, 4)
+    across = (1 - place, spot)
+    beside_core = spot + 1 - 2 * lax.rem(spot, 2)
+    beside_chip = spot + 2 - 4 * (quarter // 2)
+    core, chip = (place, beside_core), (place, beside_chip)
+    twin = lax.rem(beside_chip, 4)
+    barrier = pltpu.get_barrier_semaphore()
+    for device in (across, core, chip):
+        pl.semaphore_signal(barrier, inc=1, device_id=device, device_id_type=pl.DeviceIdType.MESH)
+    pl.semaphore_wait(barrier, 3)
+    mine, theirs = place * 4, (1 - place) * 4
+    parts = [(which, span) for which in range(count) for span in plan[which]]
+
+    def send(part, kind, source, slot, device):
+        which, (at, size) = parts[part]
+        return pltpu.make_async_remote_copy(
+            src_ref=source,
+            dst_ref=wholes[which].at[slot, :, at : at + size],
+            send_sem=send_sem.at[part, kind],
+            recv_sem=recv_sem.at[part, kind],
+            device_id=device,
+            device_id_type=pl.DeviceIdType.MESH,
+        )
+
+    def held(part, slot):
+        which, (at, size) = parts[part]
+        return wholes[which].at[slot, :, at : at + size]
+
+    fetch, over_chip, over_core, again = [], [], [], []
+    for part, (which, (at, size)) in enumerate(parts):
+        source = shards[which].at[quarter, :, at : at + size]
+        fetch.append(send(part, 0, source, mine + quarter, across))
+        over_chip.append(send(part, 1, held(part, theirs + quarter), theirs + quarter, chip))
+        over_core.append(send(part, 2, held(part, theirs + quarter), theirs + quarter, core))
+        again.append(send(part, 3, held(part, theirs + twin), theirs + twin, core))
+        fetch[part].start()
+    locals_ = []
+    for which in range(count):
+        copy = pltpu.make_async_copy(
+            shards[which], wholes[which].at[pl.ds(mine, 4)], own_sem.at[which]
+        )
+        copy.start()
+        locals_.append(copy)
+    total = len(parts)
+    for part in range(total + 1):
+        if part < total:
+            fetch[part].wait_recv()
+            over_chip[part].start()
+            over_core[part].start()
+        if part > 0:
+            over_chip[part - 1].wait_recv()
+            again[part - 1].start()
+    for part in range(total):
+        over_core[part].wait_recv()
+        again[part].wait_recv()
+        for copy in (fetch, over_chip, over_core, again):
+            copy[part].wait_send()
+    for copy in locals_:
+        copy.wait()
+
+
+def gather_weights(shards, pieces, identity):
+    quarters = [shard.reshape(4, shard.shape[0] // 4, shard.shape[1]) for shard in shards]
+    plan = [spans(shard.shape[1], piece) for shard, piece in zip(shards, pieces)]
+    total = sum(len(part) for part in plan)
+    size = sum(shard.size for shard in shards)
+    wholes = pl.pallas_call(
+        functools.partial(gather_kernel, plan),
+        out_shape=tuple(
+            jax.ShapeDtypeStruct((8,) + part.shape[1:], part.dtype) for part in quarters
+        ),
+        in_specs=[pl.BlockSpec(memory_space=pl.ANY)] * len(shards),
+        out_specs=tuple([pl.BlockSpec(memory_space=pl.ANY)] * len(shards)),
+        scratch_shapes=[
+            pltpu.SemaphoreType.DMA((len(shards),)),
+            pltpu.SemaphoreType.DMA((total, 4)),
+            pltpu.SemaphoreType.DMA((total, 4)),
+        ],
+        compiler_params=pltpu.CompilerParams(collective_id=identity, has_side_effects=True),
+        cost_estimate=pl.CostEstimate(flops=0, bytes_accessed=16 * size, transcendentals=0),
+        name="gather_weights",
+    )(*quarters)
+    return [
+        whole.reshape(2 * shard.shape[0], shard.shape[1]) for whole, shard in zip(wholes, shards)
+    ]
 
 
 def on_device(
@@ -376,16 +480,24 @@
         down_bias, up_bias,
     )
     sizes = [part.shape[0] for part in small]
-    gathered = lax.all_gather(jnp.concatenate(small), "fsdp", axis=0, tiled=False)
+    paired = fsdp == 2 and blocks % 4 == 0
+    packed_small = jnp.concatenate(small)
+    if paired:
+        apart = other_half(packed_small)
+        gathered = jnp.where(
+            place == 0, jnp.stack([packed_small, apart]), jnp.stack([apart, packed_small])
+        )
+    else:
+        gathered = lax.all_gather(packed_small, "fsdp", axis=0, tiled=False)
     whole_small, at = [], 0
     for size in sizes:
         whole_small.append(gathered[:, at : at + size].reshape(fsdp * size).astype(f32))
         at += size
     gain_one, shift_one, bias_q, bias_v, bias_o, gain_two, shift_two, bias_d, bias_u = whole_small
-    whole_qkv, whole_out, whole_up, whole_down = (
-        lax.all_gather(part, "fsdp", axis=0, tiled=True)
-        for part in (qkv_weight, out_weight, up_weight, down_weight)
-    )
+    if paired:
+        (whole_qkv,) = gather_weights((qkv_weight,), (4,), 1)
+    else:
+        whole_qkv = lax.all_gather(qkv_weight, "fsdp", axis=0, tiled=True)
     rows = block_input.astype(f32)
     first_norm, first_hat, first_rstd = normalize(rows, gain_one, shift_one)
     first_act = first_norm.astype(bf16)
@@ -393,6 +505,14 @@
     query = (qkv[:, :width] + bias_q).astype(bf16)
     keys = qkv[:, width : 2 * width].astype(bf16)
     values = (qkv[:, 2 * width :] + bias_v).astype(bf16)
+    later = (out_weight, up_weight, down_weight)
+    if paired:
+        later = lax.optimization_barrier((later, qkv))[0]
+        whole_out, whole_up, whole_down = gather_weights(later, (1, 3, 3), 2)
+    else:
+        whole_out, whole_up, whole_down = (
+            lax.all_gather(part, "fsdp", axis=0, tiled=True) for part in later
+        )
     attention = head_attention if HEADS == blocks + 1 else ring_attention
     joined, attention_back = attention(query, keys, values)
     mid = rows + jnp.dot(joined, whole_out, preferred_element_type=f32) + bias_o
@@ -403,13 +523,20 @@
     block_output = mid + jnp.dot(act, whole_down, preferred_element_type=f32) + bias_d
 
     def left(part):
+        if paired:
+            half = part.shape[1] // 2
+            own = lax.dynamic_slice_in_dim(part, place * half, half, 1)
+            sent = lax.dynamic_slice_in_dim(part, (1 - place) * half, half, 1)
+            return jnp.concatenate([own, other_half(sent)], axis=0)
         return lax.all_to_all(part, "fsdp", split_axis=1, concat_axis=0, tiled=True)
 
     def right(part):
+        if paired:
+            return jnp.concatenate([part, other_half(part)], axis=0)
         return lax.all_gather(part, "fsdp", axis=0, tiled=True)
 
     def weight_grad(left_part, right_part):
-        return lax.psum(contract(left(left_part), right(right_part), 0, 0).astype(bf16), "ctx")
+        return contract(left(left_part), right(right_part), 0, 0).astype(bf16)
 
     cot_float = cotangent.astype(f32)
     grad_down = weight_grad(act, cotangent)
@@ -439,10 +566,22 @@
         grad_first_gain, grad_first_shift, grad_query_bias, grad_value_bias, grad_out_bias,
         grad_second_gain, grad_second_shift, grad_down_bias, grad_up_bias,
     )
-    summed = lax.psum(
-        jnp.concatenate([part.reshape(fsdp, -1) for part in vectors], axis=1), ("fsdp", "ctx")
-    )
-    mine = lax.dynamic_index_in_dim(summed, place, 0, keepdims=False)
+    packed_vectors = jnp.concatenate([part.reshape(fsdp, -1) for part in vectors], axis=1)
+    mine = lax.dynamic_index_in_dim(packed_vectors, place, 0, keepdims=False)
+    if paired:
+        sent = lax.dynamic_index_in_dim(packed_vectors, 1 - place, 0, keepdims=False)
+        mine = mine + other_half(sent)
+    else:
+        mine = lax.psum_scatter(packed_vectors, "fsdp", scatter_dimension=0, tiled=True)[0]
+    depth, columns = grad_qkv.shape
+    spare = -(-mine.shape[0] // (8 * columns)) * 8
+    below = jnp.pad(mine.astype(bf16), (0, spare * columns - mine.shape[0]))
+    grad_qkv = jnp.concatenate([grad_qkv, below.reshape(spare, columns)], axis=0)
+    grad_qkv, grad_out, grad_up, grad_down = lax.psum(
+        (grad_qkv, grad_out, grad_up, grad_down), "ctx"
+    )
+    mine = grad_qkv[depth:].reshape(-1).astype(f32)
+    grad_qkv = grad_qkv[:depth]
     shards, at = [], 0
     for size in sizes:
         shards.append(mine[at : at + size])

time: 854 us -> 981 us (1.15)
  Pallas kernels: 14.9 us -> 464 us
  waiting for transfers between devices: 574 us -> 332 us
  blocking collectives: 93.9 us -> 0 us
  local copies, waits for them, and re-layouts: 23.8 us -> 37.8 us
    pallas_call x0 -> x2, Pallas kernels: none -> 450 us  [gather_weights(): pl.pallas_call(functools.partial(gather_kernel, plan), out_shape=tuple((j...]
    all_gather x6 -> x0, waiting for transfers between devices: 296 us -> none  [the longest x4 296 us: on_device(): lax.all_gather(part, 'fsdp', axis=0, tiled=True)]
    all_gather x3 -> x0, blocking collectives: 51.1 us -> none  [the longest x2 45.7 us: right(): return lax.all_gather(part, 'fsdp', axis=0, tiled=True)]
    psum x1, waiting for transfers between devices: 205 us -> 256 us  [on_device(): lax.psum((grad_qkv, grad_out, grad_up, grad_down), 'ctx')]
    psum x1 -> x0, blocking collectives: 42.7 us -> none  [on_device(): lax.psum(jnp.concatenate([part.reshape(fsdp, -1) for part in vectors], ax...]
    ppermute x0 -> x10, waiting for transfers between devices: none -> 39.7 us  [other_half(): return lax.ppermute(value, 'fsdp', [(0, 1), (1, 0)])]
    all_to_all x4, waiting for transfers between devices: 63.1 us -> 36.8 us  [swap(): lax.all_to_all(blocks_of, axis, split_axis=0, concat_axis=0, tiled=True)]
    all_to_all x4 -> x0, starting transfers between devices: 14.6 us -> none  [left(): return lax.all_to_all(part, 'fsdp', split_axis=1, concat_axis=0, tiled=True)]
  transfers between devices with their start and end apart: 15 -> 15, of which waited for: 10 -> 6; matrix products, arithmetic and copies ran while one was open for 7% -> 5% of each run, Pallas kernels for 1% -> 46%
where the time goes in v3:
time: 981 us; the launch traced here: 975 us
  Pallas kernels  464 us (47%)
  waiting for transfers between devices  332 us (34%)
  matrix products  58.4 us (6%)
  local copies, waits for them, and re-layouts  37.8 us (4%)
  starting transfers between devices  36 us (4%)
  other arithmetic  31.3 us (3%)
  between operations  14.8 us (2%)
    pallas_call x2, Pallas kernels, gather_weights(): pl.pallas_call(functools.partial(gather_kernel, plan), out_shape=tuple((j...  450 us
    psum x1, waiting for transfers between devices, on_device(): lax.psum((grad_qkv, grad_out, grad_up, grad_down), 'ctx')  256 us
    ppermute x10, waiting for transfers between devices, other_half(): return lax.ppermute(value, 'fsdp', [(0, 1), (1, 0)])  39.7 us
    all_to_all x4, waiting for transfers between devices, swap(): lax.all_to_all(blocks_of, axis, split_axis=0, concat_axis=0, tiled=True)  36.8 us
    dot_general x8, matrix products, contract(): lax.dot_general(left, right, (((left_dim,), (right_dim,)), ((), ())), pre...  34.6 us
    all_to_all x4, starting transfers between devices, swap(): lax.all_to_all(blocks_of, axis, split_axis=0, concat_axis=0, tiled=True)  24.1 us
  transfers between devices with their start and end apart: 15, of which 6 were waited for; matrix products, arithmetic and copies ran while one was open for 5% of the time, Pallas kernels for 46%

profile of v3, /device:TPU:0, one launch (start us, length us, event | category | flops | bytes accessed | tf_op | source)
XLA Modules:
  0.0 974.9 jit_solution(13511225102605083861)
XLA Ops:
  7.2 6.2 concatenate.52
  13.4 3.0 collective-permute-start
  16.5 1.1 convert_reduce_fusion
  17.6 1.1 fusion.30
  18.7 112.6 %gather_weights.2 = bf16[8,136,3264]{2,1,0:T(8,128)(2,1)} custom-call(bf16[4,136,3264]{2,1,0:T(8,128)(2,1)} %bitcast.77), custom_call_target="tpu_custom_call" | custom-call | bytes 28409856 | tf_op jit(solution)/shard_map/gather_weights/pallas_call | solution.py:435
  132.2 6.1 fusion.61
  139.3 1.2 pad_maximum_fusion.1
  140.5 5.3 all-to-all-start
  145.7 27.4 %all-to-all-done = bf16[16,128,320]{1,2,0:T(8,128)(2,1)} async-done(((bf16[16,128,320]{1,2,0:T(8,128)(2,1)}), bf16[16,128,320]{1,2,0:T(8,128)(2,1)}, u32[]{:S(2)}, u32[]{:S(2)}) %all-to-all-start) | async-done | bytes 1310752 | tf_op jit(solution)/shard_map/all_to_all | solution.py:204
  173.2 1.8 copy.55
  175.0 7.0 attend.1
  182.0 0.9 copy.56
  182.9 8.3 all-to-all-start.1
  191.5 8.2 copy.58
  199.7 336.9 %gather_weights.3 = (bf16[8,136,1088]{2,1,0:T(8,128)(2,1)}, bf16[8,136,4352]{2,1,0:T(8,128)(2,1)}, bf16[8,544,1088]{2,1,0:T(8,128)(2,1)}) custom-call(bf16[4,136,1088]{2,1,0:T(8,128)(2,1)} %bitcast.84, bf16[4,136,4352]{2,1,0:T(8,128)(2,1)} %bitcast.72, bf16[4,544,1088]{2,1,0:T(8,128)(2,1)} %bitcast.67), custom_call_target="tpu_custom_call" | custom-call | bytes 85229568 | tf_op jit(solution)/shard_map/gather_weights/pallas_call | solution.py:435
  536.8 3.0 fusion.62
  540.3 7.1 multiply_convert_fusion
  547.4 8.7 fusion.56
  556.1 2.8 multiply_reduce_fusion
  558.9 1.6 fusion.55
  560.6 0.8 convert_element_type.190
  561.4 1.9 convolution_convert_fusion.4
  563.3 0.7 copy-done.17
  564.0 0.7 slice.165
  564.7 1.8 copy.60
  566.5 6.1 all-to-all-start.2
  572.6 0.8 slice.166.xgrad_ref
  573.4 9.3 all-to-all-done.2
  582.7 1.2 copy.61
  583.9 7.9 attend_back.1
  591.8 1.1 copy-done
  592.9 2.6 copy.62
  595.6 4.5 all-to-all-start.3
  600.3 1.1 constant_dynamic-slice_fusion.1
  602.0 1.5 collective-permute-start.9
  604.0 1.2 fusion.48
  605.2 1.5 collective-permute-start.4
  606.8 0.7 constant_dynamic-slice_fusion.5
  609.0 23.2 %collective-permute-done.4 = bf16[128,544]{0,1:T(8,128)(2,1)} collective-permute-done((bf16[128,544]{0,1:T(8,128)(2,1)}, bf16[128,544]{0,1:T(8,128)(2,1)}, u32[]{:S(2)}, u32[]{:S(2)}) %collective-permute-start.4) | collective-permute-done | bytes 139296 | tf_op jit(solution)/shard_map/ppermute | solution.py:355
  632.7 1.5 collective-permute-start.6
  634.2 2.7 convolution_convert_fusion.3
  637.0 4.9 convolution_convert_fusion
  641.9 1.2 fusion.58
  643.1 0.8 constant_dynamic-update-slice_fusion.4
  644.5 0.7 constant_dynamic-update-slice_fusion.2
  645.2 1.1 slice_reduce_fusion
  647.0 0.7 constant_dynamic-update-slice_fusion.1
  648.8 6.1 fusion.29
  655.1 1.1 convert_reduce_fusion.2
  656.8 1.6 collective-permute-start.3
  658.4 4.6 collective-permute-done.6
  663.0 4.9 convolution_convert_fusion.1
  667.9 11.8 %collective-permute-done.3 = f32[6528]{0:T(1024)S(1)} collective-permute-done((f32[6528]{0:T(1024)S(1)}, f32[6528]{0:T(1024)S(1)}, u32[]{:S(2)}, u32[]{:S(2)}) %collective-permute-start.3) | collective-permute-done | bytes 26144 | tf_op jit(solution)/shard_map/ppermute | solution.py:355
  679.9 2.6 convolution_convert_fusion.2
  682.5 2.1 pad_maximum_fusion
  684.7 7.7 fusion.1
  692.5 1.0 fusion.28
  693.5 255.6 %all-reduce.4.cloned.1.call-done = (bf16[552,3264]{1,0:T(8,128)(2,1)}, bf16[544,1088]{1,0:T(8,128)(2,1)}, bf16[544,4352]{1,0:T(8,128)(2,1)}, bf16[2176,1088]{0,1:T(8,128)(2,1)}) async-done(((bf16[552,3264]{1,0:T(8,128)(2,1)}, bf16[544,1088]{1,0:T(8,128)(2,1)}, bf16[544,4352]{1,0:T(8,128)(2,1)}, bf16[2176,1088]{0,1:T(8,128)(2,1)}), (bf16[552,3264]{1,0:T(8,128)(2,1)}, bf16[544,1088]{1,0:T(8,128)(2,1)}, ...) | async-done | bytes 14257168 | tf_op jit(solution)/shard_map/psum | solution.py:580
  949.1 0.8 slice_convert_fusion.1
  950.6 0.7 fusion.59
  951.3 6.1 slice_convert_fusion
  957.4 1.6 convert_element_type.200
  959.1 4.5 convert_element_type.202
  963.6 4.4 convert_element_type.204
  (128 shorter events, 10.1 us)
Async XLA Ops:
  13.4 118.0 %collective-permute-start = (bf16[6528]{0:T(1024)(128)(2,1)S(1)}, bf16[6528]{0:T(1024)(128)(2,1)S(1)}, u32[]{:S(2)}, u32[]{:S(2)}) collective-permute-start(bf16[6528]{0:T(1024)(128)(2,1)S(1)} %concatenate.52), channel_id=1, source_target_pairs={{0,16},{16,0},{1,17},{17,1},{2,18},{18,2},{3,19},{19,3},{4,20},{20... | collective-permute-start | bytes 39176 | tf_op jit(solution)/shard_map/ppermute | solution.py:355
  18.7 113.1 %copy-start.5 = (bf16[128,1088]{0,1:T(8,128)(2,1)S(1)}, bf16[128,1088]{0,1:T(8,128)(2,1)}, u32[]{:S(2)}) copy-start(bf16[128,1088]{0,1:T(8,128)(2,1)} %param.15) | copy-start | bytes 835588
  132.2 6.1 copy-start.10
  140.5 32.7 %all-to-all-start = ((bf16[16,128,320]{1,2,0:T(8,128)(2,1)}), bf16[16,128,320]{1,2,0:T(8,128)(2,1)}, u32[]{:S(2)}, u32[]{:S(2)}) async-start(bf16[16,128,320]{1,2,0:T(8,128)(2,1)} %pad_maximum_fusion.1), calls=%async_computation | async-start | bytes 2621440 | tf_op jit(solution)/shard_map/all_to_all | solution.py:204
  182.9 353.8 %all-to-all-start.1 = ((bf16[16,128,64]{1,2,0:T(8,128)(2,1)}), bf16[16,128,64]{1,2,0:T(8,128)(2,1)S(1)}, u32[]{:S(2)}, u32[]{:S(2)}) async-start(bf16[16,128,64]{1,2,0:T(8,128)(2,1)} %copy.56), calls=%async_computation.1 | async-start | bytes 524288 | tf_op jit(solution)/shard_map/all_to_all | solution.py:204
  536.8 3.1 copy-start.13
  540.3 7.1 copy-start.8
  540.3 15.8 %slice-start = ((s8[9469952]{0:T(1024)(128)(4,1)}), s8[4194304]{0:T(1024)(128)(4,1)S(1)}, s32[]{:S(2)}) async-start(s8[9469952]{0:T(1024)(128)(4,1)} %bitcast.62), calls=%async_computation.5 | async-start | bytes 8388608
  540.3 15.8 %slice-start.1 = ((s8[9469952]{0:T(1024)(128)(4,1)}), s8[4194304]{0:T(1024)(128)(4,1)S(1)}, s32[]{:S(2)}) async-start(s8[9469952]{0:T(1024)(128)(4,1)} %bitcast.62), calls=%async_computation.6 | async-start | bytes 8388608
  547.4 8.7 slice-start.2
  556.1 2.8 copy-start.3
  558.9 2.5 copy-start.1
  560.6 6.0 copy-start.6
  563.3 0.7 copy-start.17
  566.5 16.1 %all-to-all-start.2 = ((bf16[16,128,64]{1,2,0:T(8,128)(2,1)}), bf16[16,128,64]{1,2,0:T(8,128)(2,1)}, u32[]{:S(2)}, u32[]{:S(2)}) async-start(bf16[16,128,64]{1,2,0:T(8,128)(2,1)} %bitcast.88), calls=%async_computation.2 | async-start | bytes 524288 | tf_op jit(solution)/shard_map/all_to_all | solution.py:204
  591.8 1.1 copy-start
  592.9 7.4 copy-start.2
  595.6 8.5 copy-start.14
  595.6 11.2 %copy-start.11 = (bf16[128,1088]{0,1:T(8,128)(2,1)S(1)}, bf16[128,1088]{0,1:T(8,128)(2,1)}, u32[]{:S(2)}) copy-start(bf16[128,1088]{0,1:T(8,128)(2,1)} %copy-done.10) | copy-start | bytes 835588
  595.6 46.4 %all-to-all-start.3 = ((bf16[16,128,320]{1,2,0:T(8,128)(2,1)}), bf16[16,128,320]{1,2,0:T(8,128)(2,1)}, u32[]{:S(2)}, u32[]{:S(2)}) async-start(bf16[16,128,320]{1,2,0:T(8,128)(2,1)} %copy.62), calls=%async_computation.3 | async-start | bytes 2621440 | tf_op jit(solution)/shard_map/all_to_all | solution.py:204
  600.1 8.2 copy-start.9
  600.1 349.0 %all-reduce.4.cloned.1.call-start = ((), (), s32[]{:S(2)}) async-start(), calls=%async_computation.4 | async-start | bytes 28794880 | tf_op jit(solution)/shard_map/psum | solution.py:580
  601.5 35.5 %collective-permute-start.8 = (bf16[128,2176]{1,0:T(8,128)(2,1)}, bf16[128,2176]{1,0:T(8,128)(2,1)}, u32[]{:S(2)}, u32[]{:S(2)}) collective-permute-start(bf16[128,2176]{1,0:T(8,128)(2,1)} %get-tuple-element.67), channel_id=1, source_target_pairs={{0,16},{16,0},{1,17},{17,1},{2,18},{18,2},{3,19},{19,3},{4,20},{20... | collective-permute-start | bytes 1671176 | tf_op jit(solution)/shard_map/ppermute | solution.py:355
  602.0 35.0 %collective-permute-start.9 = (bf16[128,1088]{0,1:T(8,128)(2,1)}, bf16[128,1088]{0,1:T(8,128)(2,1)}, u32[]{:S(2)}, u32[]{:S(2)}) collective-permute-start(bf16[128,1088]{0,1:T(8,128)(2,1)} %param.16), channel_id=1, source_target_pairs={{0,16},{16,0},{1,17},{17,1},{2,18},{18,2},{3,19},{19,3},{4,20},{20... | collective-permute-start | bytes 835592 | tf_op jit(solution)/shard_map/ppermute | solution.py:355
  603.5 29.2 %collective-permute-start.5 = (bf16[128,1088]{0,1:T(8,128)(2,1)}, bf16[128,1088]{0,1:T(8,128)(2,1)}, u32[]{:S(2)}, u32[]{:S(2)}) collective-permute-start(bf16[128,1088]{0,1:T(8,128)(2,1)} %convert_element_type.190), channel_id=1, source_target_pairs={{0,16},{16,0},{1,17},{17,1},{2,18},{18,2},{3,19},{19,3},{4,20},{20... | collective-permute-start | bytes 835592 | tf_op jit(solution)/shard_map/ppermute | solution.py:355
  605.2 31.8 %copy-start.15 = (bf16[128,2176]{1,0:T(8,128)(2,1)S(1)}, bf16[128,2176]{1,0:T(8,128)(2,1)}, u32[]{:S(2)}) copy-start(bf16[128,2176]{1,0:T(8,128)(2,1)} %get-tuple-element.66) | copy-start | bytes 1671172
  605.2 26.9 %collective-permute-start.4 = (bf16[128,544]{0,1:T(8,128)(2,1)}, bf16[128,544]{0,1:T(8,128)(2,1)}, u32[]{:S(2)}, u32[]{:S(2)}) collective-permute-start(bf16[128,544]{0,1:T(8,128)(2,1)} %get-tuple-element.71), channel_id=1, source_target_pairs={{0,16},{16,0},{1,17},{17,1},{2,18},{18,2},{3,19},{19,3},{4,20},{20... | collective-permute-start | bytes 417800 | tf_op jit(solution)/shard_map/ppermute | solution.py:355
  607.4 72.4 %collective-permute-start.1 = (bf16[128,544]{0,1:T(8,128)(2,1)}, bf16[128,544]{0,1:T(8,128)(2,1)}, u32[]{:S(2)}, u32[]{:S(2)}) collective-permute-start(bf16[128,544]{0,1:T(8,128)(2,1)} %get-tuple-element.73), channel_id=1, source_target_pairs={{0,16},{16,0},{1,17},{17,1},{2,18},{18,2},{3,19},{19,3},{4,20},{20... | collective-permute-start | bytes 417800 | tf_op jit(solution)/shard_map/ppermute | solution.py:355
  632.2 30.8 %collective-permute-start.7 = (bf16[128,4352]{1,0:T(8,128)(2,1)}, bf16[128,4352]{1,0:T(8,128)(2,1)}, u32[]{:S(2)}, u32[]{:S(2)}) collective-permute-start(bf16[128,4352]{1,0:T(8,128)(2,1)} %copy-done.3), channel_id=1, source_target_pairs={{0,16},{16,0},{1,17},{17,1},{2,18},{18,2},{3,19},{19,3},{4,20},{20... | collective-permute-start | bytes 3342344 | tf_op jit(solution)/shard_map/ppermute | solution.py:355
  632.7 30.3 %collective-permute-start.6 = (bf16[128,544]{0,1:T(8,128)(2,1)}, bf16[128,544]{0,1:T(8,128)(2,1)}, u32[]{:S(2)}, u32[]{:S(2)}) collective-permute-start(bf16[128,544]{0,1:T(8,128)(2,1)} %get-tuple-element.69), channel_id=1, source_target_pairs={{0,16},{16,0},{1,17},{17,1},{2,18},{18,2},{3,19},{19,3},{4,20},{20... | collective-permute-start | bytes 417800 | tf_op jit(solution)/shard_map/ppermute | solution.py:355
  643.1 5.2 copy-start.12
  648.3 14.7 %copy-start.4 = (bf16[128,4352]{1,0:T(8,128)(2,1)S(1)}, bf16[128,4352]{1,0:T(8,128)(2,1)}, u32[]{:S(2)}) copy-start(bf16[128,4352]{1,0:T(8,128)(2,1)} %copy-done.3) | copy-start | bytes 3342340
  648.3 31.6 %collective-permute-start.2 = (bf16[128,3264]{0,1:T(8,128)(2,1)}, bf16[128,3264]{0,1:T(8,128)(2,1)}, u32[]{:S(2)}, u32[]{:S(2)}) collective-permute-start(bf16[128,3264]{0,1:T(8,128)(2,1)} %get-tuple-element.84), channel_id=1, source_target_pairs={{0,16},{16,0},{1,17},{17,1},{2,18},{18,2},{3,19},{19,3},{4,20},{20... | collective-permute-start | bytes 2506760 | tf_op jit(solution)/shard_map/ppermute | solution.py:355
  656.8 22.9 %collective-permute-start.3 = (f32[6528]{0:T(1024)S(1)}, f32[6528]{0:T(1024)S(1)}, u32[]{:S(2)}, u32[]{:S(2)}) collective-permute-start(f32[6528]{0:T(1024)S(1)} %get-tuple-element.51), channel_id=1, source_target_pairs={{0,16},{16,0},{1,17},{17,1},{2,18},{18,2},{3,19},{19,3},{4,20},{20... | collective-permute-start | bytes 78344 | tf_op jit(solution)/shard_map/ppermute | solution.py:355
  684.7 7.7 copy-start.7
  684.7 7.7 copy-start.18
  950.6 8.4 slice-start.5
  951.3 6.1 copy-start.16
  951.3 7.8 slice-start.6
  957.4 6.1 slice-start.3
  959.1 4.5 slice-start.4
Sparse Core Ops, SparseCore 0:
  684.7 264.3 all-reduce.3

commit v4 on v2

--- a/solution.py
+++ b/solution.py
@@ -458,24 +458,19 @@
     def weight_grad(left_part, right_part):
         return contract(left(left_part), right(right_part), 0, 0).astype(bf16)
 
-    def total(value, earlier=None):
-        if earlier is not None:
-            value = after(value, earlier)
-        return lax.psum(value, "ctx")
-
     cot_float = cotangent.astype(f32)
-    grad_down = total(weight_grad(act, cotangent))
+    grad_down = weight_grad(act, cotangent)
     grad_down_bias = jnp.sum(cot_float, axis=0)
     grad_pre = gelu_back(pre, contract(cotangent, whole_down, 1, 1))
     grad_pre_b = grad_pre.astype(bf16)
-    grad_up = total(weight_grad(second_act, grad_pre_b), grad_down)
+    grad_up = weight_grad(second_act, grad_pre_b)
     grad_up_bias = jnp.sum(grad_pre, axis=0)
     grad_second = contract(grad_pre_b, whole_up, 1, 1)
     grad_second_gain = jnp.sum(grad_second * second_hat, axis=0)
     grad_second_shift = jnp.sum(grad_second, axis=0)
     grad_mid = cot_float + normalize_back(grad_second, second_hat, second_rstd, gain_two)
     grad_mid_b = grad_mid.astype(bf16)
-    grad_out = total(weight_grad(joined, grad_mid_b), grad_up)
+    grad_out = weight_grad(joined, grad_mid_b)
     grad_out_bias = jnp.sum(grad_mid, axis=0)
     grad_attended = contract(grad_mid_b, whole_out, 1, 1).astype(bf16)
     grad_query, grad_keys, grad_values = attention_back(grad_attended)
@@ -498,8 +493,15 @@
         mine = mine + other_half(sent)
     else:
         mine = lax.psum_scatter(packed_vectors, "fsdp", scatter_dimension=0, tiled=True)[0]
-    grad_qkv, mine = total((grad_qkv, mine.astype(bf16)), grad_out)
-    mine = mine.astype(f32)
+    depth, columns = grad_qkv.shape
+    spare = -(-mine.shape[0] // (8 * columns)) * 8
+    below = jnp.pad(mine.astype(bf16), (0, spare * columns - mine.shape[0]))
+    grad_qkv = jnp.concatenate([grad_qkv, below.reshape(spare, columns)], axis=0)
+    grad_qkv, grad_out, grad_up, grad_down = lax.psum(
+        (grad_qkv, grad_out, grad_up, grad_down), "ctx"
+    )
+    mine = grad_qkv[depth:].reshape(-1).astype(f32)
+    grad_qkv = grad_qkv[:depth]
     shards, at = [], 0
     for size in sizes:
         shards.append(mine[at : at + size])

time: 749 us -> 651 us (0.87)
  blocking collectives: 78 us -> 14.4 us
  waiting for transfers between devices: 424 us -> 375 us
  local copies, waits for them, and re-layouts: 62 us -> 71.4 us
    psum x1 -> x0, blocking collectives: 58.7 us -> none  [total(): return lax.psum(value, 'ctx')]
    ppermute x13, waiting for transfers between devices: 78.4 us -> 48.6 us  [other_half(): return lax.ppermute(value, 'fsdp', [(0, 1), (1, 0)])]
    psum x4 -> x1, waiting for transfers between devices: 270 us -> 256 us  [on_device(): lax.psum((grad_qkv, grad_out, grad_up, grad_down), 'ctx')]
    unnamed x75 -> x83, local copies, waits for them, and re-layouts: 11.7 us -> 16.2 us
  transfers between devices with their start and end apart: 33 -> 30, of which waited for: 17 -> 13; matrix products, arithmetic and copies ran while one was open for 21% -> 20% of each run, Pallas kernels for 2% -> 1%
where the time goes in v4:
time: 651 us; the launch traced here: 643 us
  waiting for transfers between devices  375 us (58%)
  local copies, waits for them, and re-layouts  71.4 us (11%)
  matrix products  58.1 us (9%)
  other arithmetic  50.7 us (8%)
  starting transfers between devices  43.6 us (7%)
  Pallas kernels  14.9 us (2%)
  between operations  14.9 us (2%)
  blocking collectives  14.4 us (2%)
    psum x1, waiting for transfers between devices, on_device(): lax.psum((grad_qkv, grad_out, grad_up, grad_down), 'ctx')  256 us
    ppermute x12, waiting for transfers between devices, partner(): lax.ppermute(value, 'ctx', [(source, source ^ bit) for source in range(co...  53.2 us
    ppermute x13, waiting for transfers between devices, other_half(): return lax.ppermute(value, 'fsdp', [(0, 1), (1, 0)])  48.6 us
    dot_general x8, matrix products, contract(): lax.dot_general(left, right, (((left_dim,), (right_dim,)), ((), ())), pre...  34.3 us
    dynamic_update_slice x16, local copies, waits for them, and re-layouts, gather_weights(): lax.dynamic_update_slice_in_dim(whole, got, base + (quarter ^ bits), 0)  23.3 us
    concatenate x4, other arithmetic, gather_weights(): whole = jnp.concatenate([parts, parts], axis=0)  22.3 us
    all_to_all x4, starting transfers between devices, swap(): lax.all_to_all(blocks_of, axis, split_axis=0, concat_axis=0, tiled=True)  20.5 us
    all_to_all x4, waiting for transfers between devices, swap(): lax.all_to_all(blocks_of, axis, split_axis=0, concat_axis=0, tiled=True)  16.8 us
  transfers between devices with their start and end apart: 30, of which 13 were waited for; matrix products, arithmetic and copies ran while one was open for 20% of the time, Pallas kernels for 1%

profile of v4, /device:TPU:0, one launch (start us, length us, event | category | flops | bytes accessed | tf_op | source)
XLA Modules:
  0.0 643.0 jit_solution(3442799372436377551)
XLA Ops:
  8.4 3.0 collective-permute-start
  11.5 6.2 concatenate.64
  17.7 14.4 %all-gather.1 = bf16[2,1,6528]{2,1,0:T(2,128)(2,1)S(1)} all-gather(bf16[1,1,6528]{2,1,0:T(2,128)(2,1)S(1)} %reshape.281), channel_id=2, replica_groups=mesh['fsdp'=2,'ctx'=16] {'fsdp'}, dimensions={0}, use_global_device_ids=true | all-gather | bytes 39168 | tf_op jit(solution)/shard_map/all_gather | solution.py:415
  32.3 6.9 %pad_maximum_fusion.2 = bf16[8,136,3264]{2,1,0:T(8,128)(2,1)} fusion(bf16[4,136,3264]{2,1,0:T(8,128)(2,1)} %bitcast.79), kind=kLoop, calls=%fused_computation.4 | loop fusion | flops 3551232 | bytes 10653696 | tf_op jit(solution)/shard_map/concatenate | solution.py:380
  39.6 2.4 constant_dynamic-slice_fusion.7
  42.0 8.2 %copy.57 = bf16[2176,1088]{1,0:T(8,128)(2,1)} copy(bf16[2176,1088]{0,1:T(8,128)(2,1)} %param.28) | data formatting | bytes 9469952 | tf_op args[13]
  50.3 10.6 %pad_maximum_fusion = bf16[8,544,1088]{2,1,0:T(8,128)(2,1)} fusion(bf16[4,544,1088]{2,1,0:T(8,128)(2,1)} %bitcast.70), kind=kLoop, calls=%fused_computation.1 | loop fusion | flops 4734976 | bytes 14204928 | tf_op jit(solution)/shard_map/concatenate | solution.py:380
  62.1 4.5 pad_maximum_fusion.1
  67.5 1.7 collective-permute-start.4
  70.0 2.6 constant_dynamic-slice_fusion.6
  72.6 1.5 collective-permute-start.1
  74.1 2.3 collective-permute-done.4
  78.8 1.5 collective-permute-start.8
  81.3 20.5 %collective-permute-done.5 = bf16[1,136,1088]{2,1,0:T(8,128)(2,1)S(1)} collective-permute-done((bf16[1,136,1088]{2,1,0:T(8,128)(2,1)}, bf16[1,136,1088]{2,1,0:T(8,128)(2,1)S(1)}, u32[]{:S(2)}, u32[]{:S(2)}) %collective-permute-start.5) | collective-permute-done | bytes 295968 | tf_op jit(solution)/shard_map/ppermute | solution.py:358
  108.5 6.1 fusion.61
  116.6 5.3 all-to-all-start
  121.9 2.4 constant_dynamic-update-slice_fusion.12
  124.3 11.1 %collective-permute-done.12 = bf16[1,544,1088]{2,1,0:T(8,128)(2,1)} collective-permute-done((bf16[1,544,1088]{2,1,0:T(8,128)(2,1)}, bf16[1,544,1088]{2,1,0:T(8,128)(2,1)}, u32[]{:S(2)}, u32[]{:S(2)}) %collective-permute-start.12) | collective-permute-done | bytes 1183776 | tf_op jit(solution)/shard_map/ppermute | solution.py:353
  135.4 1.5 collective-permute-start.13
  136.9 6.1 collective-permute-done.9
  143.0 2.4 constant_dynamic-update-slice_fusion.11
  145.4 2.5 constant_dynamic-update-slice_fusion.8
  147.8 2.4 constant_dynamic-update-slice_fusion.10
  150.2 25.6 %collective-permute-done.13 = bf16[1,544,1088]{2,1,0:T(8,128)(2,1)} collective-permute-done((bf16[1,544,1088]{2,1,0:T(8,128)(2,1)}, bf16[1,544,1088]{2,1,0:T(8,128)(2,1)}, u32[]{:S(2)}, u32[]{:S(2)}) %collective-permute-start.13) | collective-permute-done | bytes 1183776 | tf_op jit(solution)/shard_map/ppermute | solution.py:358
  175.8 2.5 constant_dynamic-update-slice_fusion.7
  180.3 7.0 %attend.1 = (bf16[2048,64]{1,0:T(8,128)(2,1)S(1)}, bf16[64,2048]{1,0:T(8,128)(2,1)S(1)}, f32[1,2048]{1,0:T(1,128)S(1)}, bf16[128,64]{1,0:T(8,128)(2,1)S(1)}, bf1...) custom-call(s32[1]{0:T(128)} %bitcast.place_ref, bf16[2048,320]{1,0:T(8,128)(2,1)S(1)} %bitcast.59, ...), custom_call_target="tpu_custom_call" | custom-call | tf_op jit(solution)/shard_map/attend/pallas_call | solution.py:165
  188.3 6.2 all-to-all-start.1
  194.5 2.4 constant_dynamic-update-slice_fusion.9
  196.9 7.6 %all-to-all-done.1 = bf16[16,128,64]{1,2,0:T(8,128)(2,1)S(1)} async-done(((bf16[16,128,64]{1,2,0:T(8,128)(2,1)}), bf16[16,128,64]{1,2,0:T(8,128)(2,1)S(1)}, u32[]{:S(2)}, u32[]{:S(2)}) %all-to-all-start.1) | async-done | bytes 262176 | tf_op jit(solution)/shard_map/all_to_all | solution.py:202
  204.5 3.0 fusion.62
  208.0 7.0 %multiply_convert_fusion = (bf16[128,4352]{1,0:T(8,128)(2,1)}, f32[128,4352]{1,0:T(8,128)S(1)}) fusion(f32[4352]{0:T(1024)S(1)} %reshape.277, bf16[128,1088]{0,1:T(8,128)(2,1)S(1)} %add_convert_fusion.1, bf16[1088,4352]{1,0:T(8,128)(2,1)} %bitcast.64), kind=kOutput, calls=%fused_computation.28 | convolution fusion | flops 1217724416 | bytes 13108224 | tf_op jit(solution)/shard_map/dot_general | solution.py:441
  215.1 2.6 constant_dynamic-update-slice_fusion.5
  217.6 8.7 %fusion.56 = (f32[4352]{0:T(1024)S(1)}, bf16[128,4352]{1,0:T(8,128)(2,1)S(1)}) fusion(f32[128,4352]{1,0:T(8,128)S(1)} %get-tuple-element.92, bf16[4352,1088]{1,0:T(8,128)(2,1)} %bitcast.18, bf16[128,1088]{0,1:T(8,128)(2,1)S(1)} %copy-done.19), kind=kOutput, calls=%fused_computation.151 | convolution fusion | flops 1223847680 | bytes 13108224 | tf_op jit(solution)/shard_map/dot_general | solution.py:55
  226.4 2.8 multiply_reduce_fusion
  233.5 1.8 copy.59
  235.3 4.7 all-to-all-start.2
  240.8 9.3 %all-to-all-done.2 = bf16[16,128,64]{1,2,0:T(8,128)(2,1)} async-done(((bf16[16,128,64]{1,2,0:T(8,128)(2,1)}), bf16[16,128,64]{1,2,0:T(8,128)(2,1)}, u32[]{:S(2)}, u32[]{:S(2)}) %all-to-all-start.2) | async-done | bytes 262176 | tf_op jit(solution)/shard_map/all_to_all | solution.py:202
  251.3 7.9 %attend_back.1 = (bf16[2048,320]{1,0:T(8,128)(2,1)S(1)}, bf16[128,64]{1,0:T(8,128)(2,1)S(1)}) custom-call(s32[1]{0:T(128)} %bitcast.place_ref, bf16[2048,320]{1,0:T(8,128)(2,1)S(1)} %bitcast.60, bf16[128,64]{1,0:T(8,128)(2,1)S(1)} %slice.159.extra_ref, bf16[64,2048]{1,0:T(8,128)(2,1)S(1)} %get-tuple-element.31.outt_ref, ...), custom_call_target="tpu_custom_call" | custom-call | tf_op jit(solution)/shard_map/attend_back/pallas_call | solution.py:184
  260.3 2.6 copy.61
  262.9 4.4 all-to-all-start.3
  268.7 1.4 collective-permute-start.23
  270.8 1.6 constant_dynamic-slice_fusion.5
  272.4 1.4 collective-permute-start.16
  273.8 2.2 fusion.48
  276.6 1.7 constant_dynamic-slice_fusion.3
  278.3 1.4 collective-permute-start.19
  280.0 10.5 %collective-permute-done.24 = bf16[128,1088]{0,1:T(8,128)(2,1)} collective-permute-done((bf16[128,1088]{0,1:T(8,128)(2,1)}, bf16[128,1088]{0,1:T(8,128)(2,1)}, u32[]{:S(2)}, u32[]{:S(2)}) %collective-permute-start.24) | collective-permute-done | bytes 278560 | tf_op jit(solution)/shard_map/ppermute | solution.py:353
  290.5 1.4 collective-permute-start.21
  292.5 5.1 convolution_convert_fusion
  297.6 4.8 collective-permute-done.19
  302.4 2.6 convolution_convert_fusion.3
  311.5 1.4 collective-permute-start.17
  312.9 6.6 %fusion.29 = (f32[1088]{0:T(1024)S(1)}, f32[128]{0:T(128)}, f32[128]{0:T(128)}, f32[1088]{0:T(1024)S(1)}, f32[128,1088]{0,1:T(8,128)}) fusion(bf16[128,1088]{0,1:T(8,128)(2,1)S(1)} %copy-done.6, f32[128]{0:T(128)S(1)} %copy-done.25, f32[128]{0:T(128)S(1)} %broadcast_multiply_fusion.5, f32[1088]{0:T(1024)S(1)} %reshape.270, bf16[1088,3264]{1,0:T(8,128)(2,1)} %bitcast.69, ...), kind=kOutput, calls=%fused_computation.53 | convolution fusion | flops 910505600 | bytes 8788736 | tf_op jit(solution)/shard_map/dot_general | solution.py:55
  322.2 7.1 %collective-permute-done.22 = bf16[128,4352]{1,0:T(8,128)(2,1)} collective-permute-done((bf16[128,4352]{1,0:T(8,128)(2,1)S(1)}, bf16[128,4352]{1,0:T(8,128)(2,1)}, u32[]{:S(2)}, u32[]{:S(2)}) %collective-permute-start.22) | collective-permute-done | bytes 1114144 | tf_op jit(solution)/shard_map/ppermute | solution.py:353
  329.3 4.9 convolution_convert_fusion.1
  334.2 12.8 %collective-permute-done.18 = f32[6528]{0:T(1024)S(1)} collective-permute-done((f32[6528]{0:T(1024)S(1)}, f32[6528]{0:T(1024)S(1)}, u32[]{:S(2)}, u32[]{:S(2)}) %collective-permute-start.18) | collective-permute-done | bytes 26144 | tf_op jit(solution)/shard_map/ppermute | solution.py:353
  347.1 2.6 convolution_convert_fusion.2
  349.7 2.1 pad_maximum_fusion.3
  351.9 7.7 %fusion.1 = f32[128,1088]{0,1:T(8,128)} fusion(f32[128,1088]{0,1:T(8,128)S(1)} %get-tuple-element.90, bf16[128,4352]{1,0:T(8,128)(2,1)S(1)} %copy-done.3, bf16[4352,1088]{1,0:T(8,128)(2,1)} %bitcast.18, f32[1088]{0:T(1024)S(1)} %reshape.278), kind=kOutput, calls=%fused_computation.17 | convolution fusion | flops 1212432384 | bytes 11702528 | tf_op jit(solution)/shard_map/dot_general | solution.py:443
  360.8 256.5 %all-reduce.4.cloned.1.call-done = (bf16[552,3264]{1,0:T(8,128)(2,1)}, bf16[544,1088]{1,0:T(8,128)(2,1)}, bf16[544,4352]{1,0:T(8,128)(2,1)}, bf16[2176,1088]{0,1:T(8,128)(2,1)}) async-done(((bf16[552,3264]{1,0:T(8,128)(2,1)}, bf16[544,1088]{1,0:T(8,128)(2,1)}, bf16[544,4352]{1,0:T(8,128)(2,1)}, bf16[2176,1088]{0,1:T(8,128)(2,1)}), (bf16[552,3264]{1,0:T(8,128)(2,1)}, bf16[544,1088]{1,0:T(8,128)(2,1)}, ...) | async-done | bytes 14257168 | tf_op jit(solution)/shard_map/psum | solution.py:500
  619.4 6.1 slice_convert_fusion
  625.5 1.6 convert_element_type.200
  627.2 4.5 convert_element_type.202
  631.6 4.4 convert_element_type.204
  (203 shorter events, 43.7 us)
Async XLA Ops:
  8.4 58.1 %collective-permute-start = (bf16[1,136,3264]{2,1,0:T(8,128)(2,1)S(1)}, bf16[1,136,3264]{2,1,0:T(8,128)(2,1)S(1)}, u32[]{:S(2)}, u32[]{:S(2)}) collective-permute-start(bf16[1,136,3264]{2,1,0:T(8,128)(2,1)S(1)} %constant_dynamic-slice_fusion.9), channel_id=1, source_target_pairs={{0,16},{16,0},{1,17},{17,1},{2,18},{18,2},{3,19},{19,3},{4,20},{20... | collective-permute-start | bytes 2663432 | tf_op jit(solution)/shard_map/ppermute | solution.py:353
  32.3 6.9 %copy-start.6 = (bf16[128,1088]{0,1:T(8,128)(2,1)S(1)}, bf16[128,1088]{0,1:T(8,128)(2,1)}, u32[]{:S(2)}) copy-start(bf16[128,1088]{0,1:T(8,128)(2,1)} %param.15) | copy-start | bytes 835588
  39.5 21.4 %copy-start.24 = (f32[128]{0:T(128)}, f32[128]{0:T(128)S(1)}, u32[]{:S(2)}) copy-start(f32[128]{0:T(128)S(1)} %add_rsqrt_fusion.1) | copy-start | bytes 1540
  50.2 11.8 %slice-start.3 = ((s8[4734976]{0:T(1024)(128)(4,1)}), s8[4194304]{0:T(1024)(128)(4,1)S(1)}, s32[]{:S(2)}) async-start(s8[4734976]{0:T(1024)(128)(4,1)} %bitcast.75), calls=%async_computation.8 | async-start | bytes 8388608
  50.3 11.0 %copy-start.13 = (bf16[544,1088]{1,0:T(8,128)(2,1)S(1)}, bf16[544,1088]{1,0:T(8,128)(2,1)}, u32[]{:S(2)}) copy-start(bf16[544,1088]{1,0:T(8,128)(2,1)} %param.22) | copy-start | bytes 3551236
  50.3 11.8 %slice-start.4 = ((s8[4734976]{0:T(1024)(128)(4,1)}), s8[540672]{0:T(1024)(128)(4,1)S(1)}, s32[]{:S(2)}) async-start(s8[4734976]{0:T(1024)(128)(4,1)} %bitcast.75), calls=%async_computation.9 | async-start | bytes 1081344
  61.2 47.3 %copy-start.10 = (bf16[128,1088]{0,1:T(8,128)(2,1)}, bf16[128,1088]{0,1:T(8,128)(2,1)S(1)}, u32[]{:S(2)}) copy-start(bf16[128,1088]{0,1:T(8,128)(2,1)S(1)} %fusion.24) | copy-start | bytes 835588
  67.5 8.9 %collective-permute-start.4 = (bf16[1,136,1088]{2,1,0:T(8,128)(2,1)}, bf16[1,136,1088]{2,1,0:T(8,128)(2,1)}, u32[]{:S(2)}, u32[]{:S(2)}) collective-permute-start(bf16[1,136,1088]{2,1,0:T(8,128)(2,1)} %constant_dynamic-slice_fusion.8), channel_id=1, source_target_pairs={{0,16},{16,0},{1,17},{17,1},{2,18},{18,2},{3,19},{19,3},{4,20},{20... | collective-permute-start | bytes 887816 | tf_op jit(solution)/shard_map/ppermute | solution.py:353
  70.0 2.6 copy-start.21
  70.0 8.8 %copy-start.15 = (bf16[1,136,4352]{2,1,0:T(8,128)(2,1)S(1)}, bf16[1,136,4352]{2,1,0:T(8,128)(2,1)}, u32[]{:S(2)}) copy-start(bf16[1,136,4352]{2,1,0:T(8,128)(2,1)} %constant_dynamic-slice_fusion.7) | copy-start | bytes 3551236
  72.6 31.9 %collective-permute-start.2 = (bf16[1,136,3264]{2,1,0:T(8,128)(2,1)S(1)}, bf16[1,136,3264]{2,1,0:T(8,128)(2,1)S(1)}, u32[]{:S(2)}, u32[]{:S(2)}) collective-permute-start(bf16[1,136,3264]{2,1,0:T(8,128)(2,1)S(1)} %copy-done.21), channel_id=1, source_target_pairs={{0,1},{1,0},{2,3},{3,2},{4,5},{5,4},{6,7},{7,6},{8,9},{9,8},{10,11... | collective-permute-start | bytes 2663432 | tf_op jit(solution)/shard_map/ppermute | solution.py:358
  72.6 29.3 %collective-permute-start.1 = (bf16[1,136,3264]{2,1,0:T(8,128)(2,1)S(1)}, bf16[1,136,3264]{2,1,0:T(8,128)(2,1)S(1)}, u32[]{:S(2)}, u32[]{:S(2)}) collective-permute-start(bf16[1,136,3264]{2,1,0:T(8,128)(2,1)S(1)} %copy-done.21), channel_id=1, source_target_pairs={{0,2},{1,3},{2,0},{3,1},{4,6},{5,7},{6,4},{7,5},{8,10},{9,11},{10,... | collective-permute-start | bytes 2663432 | tf_op jit(solution)/shard_map/ppermute | solution.py:358
  76.4 25.4 %collective-permute-start.5 = (bf16[1,136,1088]{2,1,0:T(8,128)(2,1)}, bf16[1,136,1088]{2,1,0:T(8,128)(2,1)S(1)}, u32[]{:S(2)}, u32[]{:S(2)}) collective-permute-start(bf16[1,136,1088]{2,1,0:T(8,128)(2,1)} %collective-permute-done.4), channel_id=1, source_target_pairs={{0,2},{1,3},{2,0},{3,1},{4,6},{5,7},{6,4},{7,5},{8,10},{9,11},{10,... | collective-permute-start | bytes 887816 | tf_op jit(solution)/shard_map/ppermute | solution.py:358
  78.8 26.7 %collective-permute-start.8 = (bf16[1,136,4352]{2,1,0:T(8,128)(2,1)S(1)}, bf16[1,136,4352]{2,1,0:T(8,128)(2,1)}, u32[]{:S(2)}, u32[]{:S(2)}) collective-permute-start(bf16[1,136,4352]{2,1,0:T(8,128)(2,1)S(1)} %copy-done.15), channel_id=1, source_target_pairs={{0,16},{16,0},{1,17},{17,1},{2,18},{18,2},{3,19},{19,3},{4,20},{20... | collective-permute-start | bytes 3551240 | tf_op jit(solution)/shard_map/ppermute | solution.py:353
  80.3 21.5 %collective-permute-start.6 = (bf16[1,136,1088]{2,1,0:T(8,128)(2,1)}, bf16[1,136,1088]{2,1,0:T(8,128)(2,1)S(1)}, u32[]{:S(2)}, u32[]{:S(2)}) collective-permute-start(bf16[1,136,1088]{2,1,0:T(8,128)(2,1)} %collective-permute-done.4), channel_id=1, source_target_pairs={{0,1},{1,0},{2,3},{3,2},{4,5},{5,4},{6,7},{7,6},{8,9},{9,8},{10,11... | collective-permute-start | bytes 887816 | tf_op jit(solution)/shard_map/ppermute | solution.py:358
  101.8 1.6 collective-permute-start.7
  101.9 5.6 collective-permute-start.3
  103.4 5.1 copy-start.1
  105.5 29.9 %collective-permute-start.12 = (bf16[1,544,1088]{2,1,0:T(8,128)(2,1)}, bf16[1,544,1088]{2,1,0:T(8,128)(2,1)}, u32[]{:S(2)}, u32[]{:S(2)}) collective-permute-start(bf16[1,544,1088]{2,1,0:T(8,128)(2,1)} %constant_dynamic-slice_fusion.6), channel_id=1, source_target_pairs={{0,16},{16,0},{1,17},{17,1},{2,18},{18,2},{3,19},{19,3},{4,20},{20... | collective-permute-start | bytes 3551240 | tf_op jit(solution)/shard_map/ppermute | solution.py:353
  106.1 41.7 %collective-permute-start.10 = (bf16[1,136,4352]{2,1,0:T(8,128)(2,1)}, bf16[1,136,4352]{2,1,0:T(8,128)(2,1)}, u32[]{:S(2)}, u32[]{:S(2)}) collective-permute-start(bf16[1,136,4352]{2,1,0:T(8,128)(2,1)} %collective-permute-done.8), channel_id=1, source_target_pairs={{0,1},{1,0},{2,3},{3,2},{4,5},{5,4},{6,7},{7,6},{8,9},{9,8},{10,11... | collective-permute-start | bytes 3551240 | tf_op jit(solution)/shard_map/ppermute | solution.py:358
  106.1 36.9 %collective-permute-start.9 = (bf16[1,136,4352]{2,1,0:T(8,128)(2,1)}, bf16[1,136,4352]{2,1,0:T(8,128)(2,1)}, u32[]{:S(2)}, u32[]{:S(2)}) collective-permute-start(bf16[1,136,4352]{2,1,0:T(8,128)(2,1)} %collective-permute-done.8), channel_id=1, source_target_pairs={{0,2},{1,3},{2,0},{3,1},{4,6},{5,7},{6,4},{7,5},{8,10},{9,11},{10,... | collective-permute-start | bytes 3551240 | tf_op jit(solution)/shard_map/ppermute | solution.py:358
  116.6 62.8 %all-to-all-start = ((bf16[16,128,320]{1,2,0:T(8,128)(2,1)}), bf16[16,128,320]{1,2,0:T(8,128)(2,1)S(1)}, u32[]{:S(2)}, u32[]{:S(2)}) async-start(bf16[16,128,320]{1,2,0:T(8,128)(2,1)} %pad_maximum_fusion.5), calls=%async_computation | async-start | bytes 2621440 | tf_op jit(solution)/shard_map/all_to_all | solution.py:202
  135.4 42.9 %collective-permute-start.14 = (bf16[1,544,1088]{2,1,0:T(8,128)(2,1)}, bf16[1,544,1088]{2,1,0:T(8,128)(2,1)S(1)}, u32[]{:S(2)}, u32[]{:S(2)}) collective-permute-start(bf16[1,544,1088]{2,1,0:T(8,128)(2,1)} %collective-permute-done.12), channel_id=1, source_target_pairs={{0,1},{1,0},{2,3},{3,2},{4,5},{5,4},{6,7},{7,6},{8,9},{9,8},{10,11... | collective-permute-start | bytes 3551240 | tf_op jit(solution)/shard_map/ppermute | solution.py:358
  135.4 40.4 %collective-permute-start.13 = (bf16[1,544,1088]{2,1,0:T(8,128)(2,1)}, bf16[1,544,1088]{2,1,0:T(8,128)(2,1)}, u32[]{:S(2)}, u32[]{:S(2)}) collective-permute-start(bf16[1,544,1088]{2,1,0:T(8,128)(2,1)} %collective-permute-done.12), channel_id=1, source_target_pairs={{0,2},{1,3},{2,0},{3,1},{4,6},{5,7},{6,4},{7,5},{8,10},{9,11},{10,... | collective-permute-start | bytes 3551240 | tf_op jit(solution)/shard_map/ppermute | solution.py:358
  143.0 51.5 %collective-permute-start.11 = (bf16[1,136,4352]{2,1,0:T(8,128)(2,1)}, bf16[1,136,4352]{2,1,0:T(8,128)(2,1)}, u32[]{:S(2)}, u32[]{:S(2)}) collective-permute-start(bf16[1,136,4352]{2,1,0:T(8,128)(2,1)} %collective-permute-done.9), channel_id=1, source_target_pairs={{0,1},{1,0},{2,3},{3,2},{4,5},{5,4},{6,7},{7,6},{8,9},{9,8},{10,11... | collective-permute-start | bytes 3551240 | tf_op jit(solution)/shard_map/ppermute | solution.py:358
  175.8 39.2 %collective-permute-start.15 = (bf16[1,544,1088]{2,1,0:T(8,128)(2,1)}, bf16[1,544,1088]{2,1,0:T(8,128)(2,1)}, u32[]{:S(2)}, u32[]{:S(2)}) collective-permute-start(bf16[1,544,1088]{2,1,0:T(8,128)(2,1)} %collective-permute-done.13), channel_id=1, source_target_pairs={{0,1},{1,0},{2,3},{3,2},{4,5},{5,4},{6,7},{7,6},{8,9},{9,8},{10,11... | collective-permute-start | bytes 3551240 | tf_op jit(solution)/shard_map/ppermute | solution.py:358
  188.3 16.2 %all-to-all-start.1 = ((bf16[16,128,64]{1,2,0:T(8,128)(2,1)}), bf16[16,128,64]{1,2,0:T(8,128)(2,1)S(1)}, u32[]{:S(2)}, u32[]{:S(2)}) async-start(bf16[16,128,64]{1,2,0:T(8,128)(2,1)} %copy.55), calls=%async_computation.1 | async-start | bytes 524288 | tf_op jit(solution)/shard_map/all_to_all | solution.py:202
  204.5 3.1 copy-start.12
  208.0 7.0 %copy-start.9 = (bf16[128,1088]{0,1:T(8,128)(2,1)}, bf16[128,1088]{0,1:T(8,128)(2,1)S(1)}, u32[]{:S(2)}) copy-start(bf16[128,1088]{0,1:T(8,128)(2,1)S(1)} %add_convert_fusion.1) | copy-start | bytes 835588
  215.0 2.6 copy-start.19
  215.1 11.4 %slice-start = ((s8[9469952]{0:T(1024)(128)(4,1)}), s8[4194304]{0:T(1024)(128)(4,1)S(1)}, s32[]{:S(2)}) async-start(s8[9469952]{0:T(1024)(128)(4,1)} %bitcast.65), calls=%async_computation.5 | async-start | bytes 8388608
  217.6 8.8 %slice-start.1 = ((s8[9469952]{0:T(1024)(128)(4,1)}), s8[4194304]{0:T(1024)(128)(4,1)S(1)}, s32[]{:S(2)}) async-start(s8[9469952]{0:T(1024)(128)(4,1)} %bitcast.65), calls=%async_computation.6 | async-start | bytes 8388608
  217.6 8.8 %slice-start.2 = ((s8[9469952]{0:T(1024)(128)(4,1)}), s8[1081344]{0:T(1024)(128)(4,1)S(1)}, s32[]{:S(2)}) async-start(s8[9469952]{0:T(1024)(128)(4,1)} %bitcast.65), calls=%async_computation.7 | async-start | bytes 2162688
  226.4 2.8 copy-start.4
  229.2 1.9 copy-start.2
  229.8 5.6 copy-start.7
  235.3 14.7 %all-to-all-start.2 = ((bf16[16,128,64]{1,2,0:T(8,128)(2,1)}), bf16[16,128,64]{1,2,0:T(8,128)(2,1)}, u32[]{:S(2)}, u32[]{:S(2)}) async-start(bf16[16,128,64]{1,2,0:T(8,128)(2,1)} %bitcast.95), calls=%async_computation.2 | async-start | bytes 524288 | tf_op jit(solution)/shard_map/all_to_all | solution.py:202
  259.2 1.1 copy-start
  260.3 7.3 %copy-start.3 = (bf16[128,4352]{1,0:T(8,128)(2,1)S(1)}, bf16[128,4352]{1,0:T(8,128)(2,1)}, u32[]{:S(2)}) copy-start(bf16[128,4352]{1,0:T(8,128)(2,1)} %get-tuple-element.91) | copy-start | bytes 3342340
  262.9 42.2 %all-to-all-start.3 = ((bf16[16,128,320]{1,2,0:T(8,128)(2,1)}), bf16[16,128,320]{1,2,0:T(8,128)(2,1)}, u32[]{:S(2)}, u32[]{:S(2)}) async-start(bf16[16,128,320]{1,2,0:T(8,128)(2,1)} %copy.61), calls=%async_computation.3 | async-start | bytes 2621440 | tf_op jit(solution)/shard_map/all_to_all | solution.py:202
  267.3 24.6 %copy-start.5 = (bf16[128,4352]{1,0:T(8,128)(2,1)S(1)}, bf16[128,4352]{1,0:T(8,128)(2,1)}, u32[]{:S(2)}) copy-start(bf16[128,4352]{1,0:T(8,128)(2,1)} %copy-done.4) | copy-start | bytes 3342340
  267.4 349.8 %all-reduce.4.cloned.1.call-start = ((), (), s32[]{:S(2)}) async-start(), calls=%async_computation.4 | async-start | bytes 28794880 | tf_op jit(solution)/shard_map/psum | solution.py:500
  268.7 23.2 %collective-permute-start.23 = (bf16[128,2176]{1,0:T(8,128)(2,1)}, bf16[128,2176]{1,0:T(8,128)(2,1)}, u32[]{:S(2)}, u32[]{:S(2)}) collective-permute-start(bf16[128,2176]{1,0:T(8,128)(2,1)} %get-tuple-element.61), channel_id=1, source_target_pairs={{0,16},{16,0},{1,17},{17,1},{2,18},{18,2},{3,19},{19,3},{4,20},{20... | collective-permute-start | bytes 1671176 | tf_op jit(solution)/shard_map/ppermute | solution.py:353
  270.2 20.3 %collective-permute-start.24 = (bf16[128,1088]{0,1:T(8,128)(2,1)}, bf16[128,1088]{0,1:T(8,128)(2,1)}, u32[]{:S(2)}, u32[]{:S(2)}) collective-permute-start(bf16[128,1088]{0,1:T(8,128)(2,1)} %param.16), channel_id=1, source_target_pairs={{0,16},{16,0},{1,17},{17,1},{2,18},{18,2},{3,19},{19,3},{4,20},{20... | collective-permute-start | bytes 835592 | tf_op jit(solution)/shard_map/ppermute | solution.py:353
  272.4 74.7 %collective-permute-start.16 = (bf16[128,544]{0,1:T(8,128)(2,1)}, bf16[128,544]{0,1:T(8,128)(2,1)}, u32[]{:S(2)}, u32[]{:S(2)}) collective-permute-start(bf16[128,544]{0,1:T(8,128)(2,1)} %get-tuple-element.67), channel_id=1, source_target_pairs={{0,16},{16,0},{1,17},{17,1},{2,18},{18,2},{3,19},{19,3},{4,20},{20... | collective-permute-start | bytes 417800 | tf_op jit(solution)/shard_map/ppermute | solution.py:353
  276.0 26.4 %collective-permute-start.20 = (bf16[128,1088]{0,1:T(8,128)(2,1)}, bf16[128,1088]{0,1:T(8,128)(2,1)}, u32[]{:S(2)}, u32[]{:S(2)}) collective-permute-start(bf16[128,1088]{0,1:T(8,128)(2,1)} %copy-done.17), channel_id=1, source_target_pairs={{0,16},{16,0},{1,17},{17,1},{2,18},{18,2},{3,19},{19,3},{4,20},{20... | collective-permute-start | bytes 835592 | tf_op jit(solution)/shard_map/ppermute | solution.py:353
  278.3 24.1 %collective-permute-start.19 = (bf16[128,544]{0,1:T(8,128)(2,1)}, bf16[128,544]{0,1:T(8,128)(2,1)}, u32[]{:S(2)}, u32[]{:S(2)}) collective-permute-start(bf16[128,544]{0,1:T(8,128)(2,1)} %get-tuple-element.65), channel_id=1, source_target_pairs={{0,16},{16,0},{1,17},{17,1},{2,18},{18,2},{3,19},{19,3},{4,20},{20... | collective-permute-start | bytes 417800 | tf_op jit(solution)/shard_map/ppermute | solution.py:353
  290.5 31.7 %collective-permute-start.21 = (bf16[128,544]{0,1:T(8,128)(2,1)}, bf16[128,544]{0,1:T(8,128)(2,1)}, u32[]{:S(2)}, u32[]{:S(2)}) collective-permute-start(bf16[128,544]{0,1:T(8,128)(2,1)} %get-tuple-element.63), channel_id=1, source_target_pairs={{0,16},{16,0},{1,17},{17,1},{2,18},{18,2},{3,19},{19,3},{4,20},{20... | collective-permute-start | bytes 417800 | tf_op jit(solution)/shard_map/ppermute | solution.py:353
  291.9 37.4 %collective-permute-start.22 = (bf16[128,4352]{1,0:T(8,128)(2,1)S(1)}, bf16[128,4352]{1,0:T(8,128)(2,1)}, u32[]{:S(2)}, u32[]{:S(2)}) collective-permute-start(bf16[128,4352]{1,0:T(8,128)(2,1)S(1)} %copy-done.5), channel_id=1, source_target_pairs={{0,16},{16,0},{1,17},{17,1},{2,18},{18,2},{3,19},{19,3},{4,20},{20... | collective-permute-start | bytes 3342344 | tf_op jit(solution)/shard_map/ppermute | solution.py:353
  292.5 9.9 %copy-start.18 = (bf16[128,1088]{0,1:T(8,128)(2,1)S(1)}, bf16[128,1088]{0,1:T(8,128)(2,1)}, u32[]{:S(2)}) copy-start(bf16[128,1088]{0,1:T(8,128)(2,1)} %copy-done.17) | copy-start | bytes 835588
  292.5 9.9 %copy-start.23 = (bf16[128,544]{0,1:T(8,128)(2,1)S(1)}, bf16[128,544]{0,1:T(8,128)(2,1)}, u32[]{:S(2)}) copy-start(bf16[128,544]{0,1:T(8,128)(2,1)} %get-tuple-element.64) | copy-start | bytes 417796
  302.4 10.5 %copy-start.25 = (f32[128]{0:T(128)S(1)}, f32[128]{0:T(128)}, u32[]{:S(2)}) copy-start(f32[128]{0:T(128)} %copy-done.24) | copy-start | bytes 1540
  306.3 3.9 copy-start.11
  311.5 35.6 %collective-permute-start.17 = (bf16[128,3264]{0,1:T(8,128)(2,1)}, bf16[128,3264]{0,1:T(8,128)(2,1)}, u32[]{:S(2)}, u32[]{:S(2)}) collective-permute-start(bf16[128,3264]{0,1:T(8,128)(2,1)} %get-tuple-element.78), channel_id=1, source_target_pairs={{0,16},{16,0},{1,17},{17,1},{2,18},{18,2},{3,19},{19,3},{4,20},{20... | collective-permute-start | bytes 2506760 | tf_op jit(solution)/shard_map/ppermute | solution.py:353
  321.5 25.5 %collective-permute-start.18 = (f32[6528]{0:T(1024)S(1)}, f32[6528]{0:T(1024)S(1)}, u32[]{:S(2)}, u32[]{:S(2)}) collective-permute-start(f32[6528]{0:T(1024)S(1)} %get-tuple-element.45), channel_id=1, source_target_pairs={{0,16},{16,0},{1,17},{17,1},{2,18},{18,2},{3,19},{19,3},{4,20},{20... | collective-permute-start | bytes 78344 | tf_op jit(solution)/shard_map/ppermute | solution.py:353
  351.9 7.8 %copy-start.27 = (f32[128]{0:T(128)S(1)}, f32[128]{0:T(128)}, u32[]{:S(2)}) copy-start(f32[128]{0:T(128)} %get-tuple-element.40) | copy-start | bytes 1540
  351.9 7.8 %copy-start.26 = (f32[128]{0:T(128)S(1)}, f32[128]{0:T(128)}, u32[]{:S(2)}) copy-start(f32[128]{0:T(128)} %get-tuple-element.41) | copy-start | bytes 1540
  351.9 7.8 %copy-start.8 = (f32[128,1088]{0,1:T(8,128)S(1)}, f32[128,1088]{0,1:T(8,128)}, u32[]{:S(2)}) copy-start(f32[128,1088]{0,1:T(8,128)} %copy-done.7) | copy-start | bytes 1671172
  351.9 7.8 %copy-start.22 = (f32[128,1088]{0,1:T(8,128)S(1)}, f32[128,1088]{0,1:T(8,128)}, u32[]{:S(2)}) copy-start(f32[128,1088]{0,1:T(8,128)} %get-tuple-element.95) | copy-start | bytes 1671172
  618.7 8.4 %slice-start.7 = ((s8[4734976]{0:T(1024)(128)(4,1)}), s8[4194304]{0:T(1024)(128)(4,1)S(1)}, s32[]{:S(2)}) async-start(s8[4734976]{0:T(1024)(128)(4,1)} %bitcast.82), calls=%async_computation.12 | async-start | bytes 8388608
  619.4 6.1 copy-start.14
  619.4 7.8 %slice-start.8 = ((s8[4734976]{0:T(1024)(128)(4,1)}), s8[540672]{0:T(1024)(128)(4,1)S(1)}, s32[]{:S(2)}) async-start(s8[4734976]{0:T(1024)(128)(4,1)} %bitcast.82), calls=%async_computation.13 | async-start | bytes 1081344
  625.5 6.1 slice-start.5
  627.2 4.5 slice-start.6
  (3 other events, 2.6 us)
Sparse Core Ops, SparseCore 0:
  352.0 265.1 all-reduce.3
